TPU v7x, 512 devices: a whole 4x8x8 slice. The times are simulated.
512 devices in a mesh: shard: 32 (over y, x), replica: 16 (over z, core).
Axes of the slice: x: 4, y: 8, z: 8, core: 2. Of those that a mesh axis runs over, the one named last changes fastest.
Arguments:
- tokens: bfloat16 [65536, 6144], P(('shard', 'replica')), may hold values from -6 to 6
- weight: bfloat16 [512, 6144], P('shard'), may hold values from -0.078125 to 0.078125
- momentum: float32 [16, 512, 6144], P('replica', 'shard'), may hold values from -6 to 6
- gradient: bfloat16 [16, 512, 6144], P('replica', 'shard'), may hold values from -6 to 6
- indices: int32 [16, 512, 96, 4], P('replica', 'shard'), may hold values from 0 to 63, all different within a row
Outputs:
- projected: bfloat16 [65536, 512], P(('shard', 'replica'))
- new_momentum: float32 [16, 512, 6144], P('replica', 'shard')
Inputs may be any that keep to these rules, and one draw needn't show every extreme that they name: The 4 indices of one replica, row and transform differ.
All inputs are finite; a program needn't handle non-finite values.
Results may differ from a plain program's by a relative error of at most 0.0054.
Values may be sent and summed in bfloat16 or wider, within the bound.
No kernel may reach another device: no remote copies, remote signals or barrier semaphores. Data moves between devices by JAX's collectives and lax.ppermute only.
A program may use at most 64 MiB of HBM per device.

v0:
```python
import math

import jax
import jax.numpy as jnp
from jax import lax
from jax.sharding import PartitionSpec as P

GROUP = 64
TOPK = 4
GROUPS = 96


decay_rate = 0.999
step_size = 0.01


def cosine_table():
    freq = jnp.arange(GROUP, dtype=jnp.float32)[:, None]
    place = jnp.arange(GROUP, dtype=jnp.float32)[None, :]
    values = jnp.cos(math.pi * (2.0 * place + 1.0) * freq / (2.0 * GROUP)) * math.sqrt(2.0 / GROUP)
    return values * jnp.where(freq == 0, math.sqrt(0.5), 1.0)


def forward_spectra(field, cosine):
    height = field.shape[0]
    flat = jnp.dot(field.reshape(-1, GROUP), cosine.T, precision=lax.Precision.HIGHEST)
    return flat.reshape(height, -1, GROUP)


def inverse_field(spectra, cosine):
    height = spectra.shape[0]
    flat = jnp.dot(spectra.reshape(-1, GROUP), cosine, precision=lax.Precision.HIGHEST)
    return flat.reshape(height, -1)


def select_hot(chosen):
    return (chosen[..., None] == jnp.arange(GROUP, dtype=jnp.int32)).astype(jnp.float32)


def decode(shipped, chosen):
    return jnp.sum(shipped.astype(jnp.float32)[..., None] * select_hot(chosen), axis=2)


def pack_codes(chosen):
    packed = jnp.zeros(chosen.shape[:-1], jnp.int32)
    for place in range(TOPK):
        packed = packed + chosen[..., place] * GROUP**place
    return packed


def unpack_codes(packed):
    return jnp.stack([packed // GROUP**place % GROUP for place in range(TOPK)], axis=-1)


def local_step(momentum, gradient, chosen, cosine):
    blended = decay_rate * momentum + gradient.astype(jnp.float32)
    spectra = forward_spectra(blended, cosine)
    onehot = select_hot(chosen)
    picked = jnp.sum(spectra[:, :, None, :] * onehot, axis=3)
    kept_part = jnp.sum(picked[..., None] * onehot, axis=2)
    remain = blended - inverse_field(kept_part, cosine)
    return (remain, picked.astype(jnp.bfloat16))


def local(tokens, weight, momentum, gradient, indices):
    cosine = cosine_table()
    own_chosen = indices[0]
    remain, shipped = local_step(momentum[0], gradient[0], own_chosen, cosine)
    new_momentum = remain[None]
    packed = pack_codes(own_chosen)
    zeros_start = jnp.zeros((weight.shape[0], GROUPS, GROUP), jnp.float32)
    values = lax.all_gather(shipped[None], "replica", axis=0, tiled=True)
    codes = lax.all_gather(packed[None], "replica", axis=0, tiled=True)

    def one_member(member, total_now):
        chosen = unpack_codes(lax.dynamic_index_in_dim(codes, member, 0, keepdims=False))
        shipment = lax.dynamic_index_in_dim(values, member, 0, keepdims=False)
        return total_now + decode(shipment, chosen)

    spectra_sum = lax.fori_loop(0, values.shape[0], one_member, zeros_start)
    renewed = (weight.astype(jnp.float32) - step_size * inverse_field(spectra_sum, cosine)).astype(
        jnp.bfloat16
    )
    projected = jnp.einsum(
        "td,rd->tr",
        tokens,
        lax.all_gather(renewed, "shard", axis=0, tiled=True),
        preferred_element_type=jnp.float32,
    )
    return (projected.astype(jnp.bfloat16), new_momentum)


def solution(mesh):
    in_specs = (
        P(("shard", "replica"), None),
        P("shard", None),
        P("replica", "shard", None),
        P("replica", "shard", None),
        P("replica", "shard", None, None),
    )
    out_specs = (P(("shard", "replica"), None), P("replica", "shard", None))
    return jax.shard_map(local, mesh=mesh, in_specs=in_specs, out_specs=out_specs, check_vma=False)
```

profile of v0, /device:TPU:1, one launch (start us, length us, event | category | flops | bytes accessed | tf_op | source)
XLA Modules:
  0.0 169.0 jit_solution(10228448522901844656)
XLA Ops:
  7.3 1.2 convert_add_fusion
  8.9 1.9 %fusion.10 = f32[16,96,64]{1,2,0:T(8,128)S(1)} fusion(f32[16,96,64]{2,1,0:T(8,128)S(1)} %add.237, f32[64]{0:T(128)S(1)} %get-tuple-element.185, f32[64]{0:T(128)S(1)} %get-tuple-element.186), kind=kOutput, calls=%fused_computation.44 | convolution fusion | flops 75509760 | bytes 786944 | tf_op jit(solution)/shard_map/dot_general | solution.py:26
  10.8 0.6 select_reduce_fusion.2
  11.4 25.2 %all-gather.1 = bf16[256,96,4]{1,2,0:T(4,128)(2,1)S(1)} all-gather(bf16[16,96,4]{1,2,0:T(4,128)(2,1)S(1)} %convert_element_type.56), channel_id=3, replica_groups=mesh['shard'=32,'replica'=16] {'replica'}, dimensions={0}, use_global_device_ids=true | all-gather | bytes 208896 | tf_op jit(solution)/shard_map/all_gather | solution.py:72
  36.6 14.8 %all-gather = s32[256,96,1]{1,2,0:T(1,128)S(1)} all-gather(s32[16,96,1]{1,2,0:T(1,128)S(1)} %fusion.27), channel_id=2, replica_groups=mesh['shard'=32,'replica'=16] {'replica'}, dimensions={0}, use_global_device_ids=true | all-gather | bytes 104448 | tf_op jit(solution)/shard_map/all_gather | solution.py:73
  51.4 12.7 %while.17 = (s32[]{:T(128)}, f32[16,96,64]{1,2,0:T(8,128)S(1)}, s32[16,16,96]{2,1,0:T(8,128)S(1)}, bf16[16,16,96,4]{2,3,1,0:T(4,128)(2,1)S(1)}, s32[]{:T(128)}, /*index=5*/s32[]{:T(128)}) while((s32[]{:T(128)}, f32[16,96,64]{1,2,0:T(8,128)S(1)}, s32[16,16,96]{2,1,0:T(8,128)S(1)}, bf16[16,16,96,4]{2,3,1,0:T(4,128)(2,1)S(1)}, ...), condition=%wide.region_3.4_spmd.clone, body=%wide.region_1.0_spmd.clone.sunk | while | flops 1425411 | bytes 1807967 | solution.py:80
  51.6 0.4 select_reduce_fusion.4
  53.1 0.4 select_reduce_fusion.4
  53.9 0.4 select_reduce_fusion.4
  54.7 0.4 select_reduce_fusion.4
  56.3 0.4 select_reduce_fusion.4
  57.1 0.4 select_reduce_fusion.4
  57.9 0.4 select_reduce_fusion.4
  59.5 0.4 select_reduce_fusion.4
  60.3 0.4 select_reduce_fusion.4
  62.6 0.4 select_reduce_fusion.4
  63.4 0.4 select_reduce_fusion.4
  64.6 0.6 convolution_multiply_fusion
  65.9 0.7 subtract_convert_fusion
  67.6 1.4 fusion.12
  69.3 0.8 sub.32
  70.1 86.7 %all-gather.4.cloned.1.call-done = bf16[512,6144]{1,0:T(8,128)(2,1)} async-done(((bf16[16,6144]{1,0:T(8,128)(2,1)}), bf16[512,6144]{1,0:T(8,128)(2,1)}) %all-gather.4.cloned.1.call-update) | async-done | bytes 6291472 | tf_op jit(solution)/shard_map/all_gather | solution.py:87
  156.8 4.6 %fusion.9 = bf16[128,512]{0,1:T(8,128)(2,1)S(1)} fusion(bf16[512,6144]{1,0:T(8,128)(2,1)} %all-gather.4.cloned.1.call-done, bf16[128,6144]{1,0:T(8,128)(2,1)S(1)} %copy-done), kind=kOutput, calls=%fused_computation.41 | convolution fusion | flops 805371904 | bytes 7995392 | tf_op jit(solution)/shard_map/td,rd->tr/dot_general | solution.py:84
  161.4 0.8 copy.62
  (138 shorter events, 9.5 us)
Async XLA Ops:
  7.2 149.6 %copy-start = (bf16[128,6144]{1,0:T(8,128)(2,1)S(1)}, bf16[128,6144]{1,0:T(8,128)(2,1)}, u32[]{:S(2)}) copy-start(bf16[128,6144]{1,0:T(8,128)(2,1)} %param.7) | copy-start | bytes 4718596
  7.2 1.6 copy-start.1
  7.2 149.6 %all-gather.4.cloned.1.call-start = ((), (), s32[]{:S(2)}) async-start(), calls=%async_computation | async-start | bytes 6488064 | tf_op jit(solution)/shard_map/all_gather | solution.py:87
  64.4 1.5 copy-start.2
Sparse Core Ops, SparseCore 0:
  66.7 90.0 all-gather.3
where the time goes:
time: 169 us
  waiting for transfers between devices  86.7 us (51%)
  blocking collectives  40 us (24%)
  other arithmetic  15.1 us (9%)
  between operations  14.2 us (8%)
  matrix products  8.54 us (5%)
  local copies, waits for them, and re-layouts  3.28 us (2%)
    all_gather x1, waiting for transfers between devices, local(): lax.all_gather(renewed, 'shard', axis=0, tiled=True)  86.7 us
    all_gather x1, blocking collectives, local(): values = lax.all_gather(shipped[None], 'replica', axis=0, tiled=True)  25.2 us
    all_gather x1, blocking collectives, local(): codes = lax.all_gather(packed[None], 'replica', axis=0, tiled=True)  14.8 us
    reduce_sum x16, other arithmetic, decode(): jnp.sum(shipped.astype(jnp.float32)[..., None] * select_hot(chosen), axis=2)  7.03 us
    dot_general x1, matrix products, local(): jnp.einsum('td,rd->tr', tokens, lax.all_gather(renewed, 'shard', axis=0,...  4.57 us
  transfers between devices with their start and end apart: 1, of which 1 were waited for; matrix products, arithmetic and copies ran while one was open for 2% of the time, Pallas kernels for 0%

commit v1 on v0

v1 whole, which is shorter than its diff:
```python
import numpy as np

import jax
import jax.numpy as jnp
from jax import lax
from jax.experimental import pallas as pl
from jax.experimental.pallas import tpu as pltpu
from jax.sharding import PartitionSpec as P

GROUP = 64
TOPK = 4
DECAY = 0.999
STEP = 0.01
PAIR = 2 * GROUP
XS = 4
YS = 8
F32 = jnp.float32
BF16 = jnp.bfloat16
HIGH = lax.Precision.HIGHEST


def pair_table():
    k = np.arange(GROUP, dtype=np.float64)[:, None]
    n = np.arange(GROUP, dtype=np.float64)[None, :]
    c = np.cos(np.pi * (2.0 * n + 1.0) * k / (2.0 * GROUP)) * np.sqrt(2.0 / GROUP)
    c = c * np.where(k == 0, np.sqrt(0.5), 1.0)
    both = np.zeros((PAIR, PAIR), np.float64)
    both[:GROUP, :GROUP] = c
    both[GROUP:, GROUP:] = c
    return both.astype(np.float32)


def contract(a, b, da, db):
    return lax.dot_general(a, b, (((da,), (db,)), ((), ())), precision=HIGH, preferred_element_type=F32)


def step_kernel(momentum, gradient, index, table, new_momentum, send):
    rows, width = momentum.shape[1:]
    pairs = width // PAIR
    lanes = pairs * rows
    blended = DECAY * momentum[0] + gradient[0].astype(F32)
    stacked = jnp.concatenate([blended[:, p * PAIR : (p + 1) * PAIR] for p in range(pairs)], axis=0)
    spectra = contract(table[...], stacked, 1, 1)
    freq = lax.broadcasted_iota(jnp.int32, (GROUP, lanes), 0)
    values, kept = [], []
    for side in range(2):
        part = spectra[side * GROUP : (side + 1) * GROUP]
        keep = jnp.zeros_like(part)
        for j in range(TOPK):
            hot = freq == index[side * TOPK + j][None, :]
            one = jnp.where(hot, part, 0.0)
            values.append(jnp.sum(one, axis=0, keepdims=True))
            keep = keep + one
        kept.append(keep)
    field = contract(jnp.concatenate(kept, axis=0), table[...], 0, 0)
    for p in range(pairs):
        at = slice(p * PAIR, (p + 1) * PAIR)
        new_momentum[0, :, at] = blended[:, at] - field[p * rows : (p + 1) * rows]
    message = jnp.concatenate(values + [index[...].astype(F32)], axis=0).astype(BF16)
    for r in range(send.shape[0]):
        half = r % 2
        send[r] = message[:, half * lanes // 2 : (half + 1) * lanes // 2]


def renew_kernel(received, weight, table, renewed):
    replicas, _, lanes = received.shape
    rows = weight.shape[0]
    half = weight.shape[1] // 2
    core = lax.axis_index("replica") % 2
    freq = lax.broadcasted_iota(jnp.int32, (GROUP, 128), 0).astype(F32)
    columns = []
    for c in range(lanes // 128):
        at = slice(c * 128, (c + 1) * 128)
        sums = [jnp.zeros((GROUP, 128), F32) for _ in range(2)]
        for r in range(replicas):
            message = received[r, :, at].astype(F32)
            for side in range(2):
                for j in range(TOPK):
                    row = side * TOPK + j
                    sums[side] = sums[side] + jnp.where(
                        freq == message[8 + row][None, :], message[row][None, :], 0.0
                    )
        columns.append(jnp.concatenate(sums, axis=0))
    field = contract(jnp.concatenate(columns, axis=1), table[...], 0, 0)
    old = weight[:, pl.ds(pl.multiple_of(core * half, 128), half)].astype(F32)
    per = half // XS // PAIR
    for x in range(XS):
        for p in range(per):
            q = x * per + p
            new = old[:, q * PAIR : (q + 1) * PAIR] - STEP * field[q * rows : (q + 1) * rows]
            new = new.astype(BF16)
            for y in range(YS):
                renewed[y * XS + x, :, p * PAIR : (p + 1) * PAIR] = new


def product_kernel(t0, t1, t2, t3, window, mine, other):
    count = mine.shape[1]
    for d, tokens in enumerate((t0, t1, t2, t3)):
        out = lax.dot_general(
            tokens[...], window[...], (((1,), (1,)), ((), ())), preferred_element_type=F32
        )
        mine[d] = out[:count]
        other[d] = out[count:].astype(BF16)


def order_kernel(mine, arrived, out):
    x = lax.axis_index("shard") % XS
    for d in range(XS):
        out[(x + XS - d) % XS] = (mine[d] + arrived[d].astype(F32)).astype(BF16)


def finish_kernel(parts, out):
    total = parts[0].astype(F32)
    for x in range(1, XS):
        total = total + parts[x].astype(F32)
    out[...] = total.astype(BF16)


def call(kernel, out, *args, flops=0):
    out_list = jax.tree.leaves(out)
    moved = sum(a.size * a.dtype.itemsize for a in args) + sum(o.size * o.dtype.itemsize for o in out_list)
    return pl.pallas_call(
        kernel,
        out_shape=out,
        in_specs=[pl.BlockSpec(memory_space=pltpu.VMEM)] * len(args),
        out_specs=jax.tree.map(lambda _: pl.BlockSpec(memory_space=pltpu.VMEM), out),
        compiler_params=pltpu.CompilerParams(vmem_limit_bytes=40 * 1024 * 1024),
        cost_estimate=pl.CostEstimate(flops=flops, bytes_accessed=moved, transcendentals=0),
    )(*args)


def local(tokens, weight, momentum, gradient, indices):
    count, width = tokens.shape
    rows = weight.shape[0]
    half, piece = width // 2, width // 2 // XS
    table = jnp.asarray(pair_table())
    core = lax.axis_index("replica") % 2
    x = lax.axis_index("shard") % XS
    replicas = lax.axis_size("replica")
    shards = lax.axis_size("shard")

    with jax.named_scope("tokens_core"):
        away = lax.dynamic_slice(tokens, (0, (1 - core) * half), (count, half))
        here = lax.dynamic_slice(tokens, (0, core * half), (count, half))
        came = lax.ppermute(away, "replica", [(i, i ^ 1) for i in range(replicas)])

    with jax.named_scope("local_step"):
        lanes = width // PAIR * rows
        index = indices[0].reshape(rows, width // PAIR, 2, TOPK).transpose(2, 3, 1, 0).reshape(2 * TOPK, lanes)
        new_momentum, send = call(
            step_kernel,
            (
                jax.ShapeDtypeStruct(momentum.shape, F32),
                jax.ShapeDtypeStruct((replicas, 4 * TOPK, lanes // 2), BF16),
            ),
            momentum,
            gradient,
            index,
            table,
            flops=10**8,
        )

    with jax.named_scope("tokens_x"):
        blocks = []
        for d in range(XS):
            start = (x + d) % XS * piece
            block = jnp.concatenate(
                [lax.dynamic_slice(a, (0, start), (count, piece)) for a in (here, came)], axis=0
            )
            if d > 0:
                block = lax.ppermute(
                    block, "shard", [(s, s // XS * XS + (s + d) % XS) for s in range(shards)]
                )
            blocks.append(block)

    with jax.named_scope("exchange"):
        received = lax.all_to_all(send, "replica", 0, 0)
    with jax.named_scope("renew"):
        renewed = call(
            renew_kernel, jax.ShapeDtypeStruct((shards, rows, piece), BF16), received, weight, table, flops=10**8
        )
    with jax.named_scope("window"):
        window = lax.all_to_all(renewed, "shard", 0, 0).reshape(shards * rows, piece)
    with jax.named_scope("product"):
        shape = (XS, count, shards * rows)
        mine, other = call(
            product_kernel,
            (jax.ShapeDtypeStruct(shape, F32), jax.ShapeDtypeStruct(shape, BF16)),
            *blocks,
            window,
            flops=2 * 1024 * 768 * 512,
        )
    with jax.named_scope("sum_core"):
        arrived = lax.ppermute(other, "replica", [(i, i ^ 1) for i in range(replicas)])
        ordered = call(order_kernel, jax.ShapeDtypeStruct(shape, BF16), mine, arrived)
    with jax.named_scope("sum_x"):
        groups = [[y * XS + i for i in range(XS)] for y in range(YS)]
        parts = lax.all_to_all(ordered, "shard", 0, 0, axis_index_groups=groups)
        projected = call(finish_kernel, jax.ShapeDtypeStruct(shape[1:], BF16), parts)
    return projected, new_momentum


def solution(mesh):
    in_specs = (
        P(("shard", "replica"), None),
        P("shard", None),
        P("replica", "shard", None),
        P("replica", "shard", None),
        P("replica", "shard", None, None),
    )
    out_specs = (P(("shard", "replica"), None), P("replica", "shard", None))
    return jax.shard_map(local, mesh=mesh, in_specs=in_specs, out_specs=out_specs, check_vma=False)
```

time: 169 us -> 90.7 us (0.54)
  waiting for transfers between devices: 86.7 us -> 26.9 us
  starting transfers between devices: 0.04 us -> 36.9 us
  blocking collectives: 40 us -> 12.2 us
  other arithmetic: 15.1 us -> 0.11 us
  between operations: 14.2 us -> 0.91 us
  matrix products: 8.54 us -> 0 us
  Pallas kernels: 0 us -> 6.53 us
  local copies, waits for them, and re-layouts: 3.28 us -> 6.44 us
    all_gather x1 -> x0, waiting for transfers between devices: 86.7 us -> none  [local(): lax.all_gather(renewed, 'shard', axis=0, tiled=True)]
    all_gather x2 -> x0, blocking collectives: 40 us -> none  [the longest x1 25.2 us: local(): values = lax.all_gather(shipped[None], 'replica', axis=0, tiled=True)]
    all_to_all x0 -> x2, starting transfers between devices: none -> 21.5 us  [the longest x1 11.8 us: local(): received = lax.all_to_all(send, 'replica', 0, 0)]
    ppermute x0 -> x5, waiting for transfers between devices: none -> 20.8 us  [the longest x3 19.3 us: local(): lax.ppermute(block, 'shard', [(s, s // XS * XS + (s + d) % XS) for s in r...]
    ppermute x0 -> x5, starting transfers between devices: none -> 15.4 us  [the longest x3 10.5 us: local(): lax.ppermute(block, 'shard', [(s, s // XS * XS + (s + d) % XS) for s in r...]
    all_to_all x0 -> x1, blocking collectives: none -> 12.2 us  [local(): parts = lax.all_to_all(ordered, 'shard', 0, 0, axis_index_groups=groups)]
    dot_general x4 -> x0, matrix products: 8.54 us -> none  [the longest x1 4.57 us: local(): jnp.einsum('td,rd->tr', tokens, lax.all_gather(renewed, 'shard', axis=0,...]
    reduce_sum x18 -> x0, other arithmetic: 8.11 us -> none  [the longest x16 7.03 us: decode(): jnp.sum(shipped.astype(jnp.float32)[..., None] * select_hot(chosen), axis=2)]
  transfers between devices with their start and end apart: 1 -> 7, of which waited for: 1 -> 4; matrix products, arithmetic and copies ran while one was open for 2% -> 3% of each run, Pallas kernels for 0% -> 3%
where the time goes in v1:
time: 90.7 us; the launch traced here: 90 us
  starting transfers between devices  36.9 us (41%)
  waiting for transfers between devices  26.9 us (30%)
  blocking collectives  12.2 us (13%)
  Pallas kernels  6.53 us (7%)
  local copies, waits for them, and re-layouts  6.44 us (7%)
  between operations  0.91 us (1%)
    ppermute x3, waiting for transfers between devices, local(): lax.ppermute(block, 'shard', [(s, s // XS * XS + (s + d) % XS) for s in r...  19.3 us
    all_to_all x1, blocking collectives, local(): parts = lax.all_to_all(ordered, 'shard', 0, 0, axis_index_groups=groups)  12.2 us
    all_to_all x1, starting transfers between devices, local(): received = lax.all_to_all(send, 'replica', 0, 0)  11.8 us
    ppermute x3, starting transfers between devices, local(): lax.ppermute(block, 'shard', [(s, s // XS * XS + (s + d) % XS) for s in r...  10.5 us
    all_to_all x1, starting transfers between devices, local(): lax.all_to_all(renewed, 'shard', 0, 0).reshape(shards * rows, piece)  9.67 us
    pallas_call x5, Pallas kernels, call(): pl.pallas_call(kernel, out_shape=out, in_specs=[pl.BlockSpec(memory_space...  6.53 us
    all_to_all x1, waiting for transfers between devices, local(): received = lax.all_to_all(send, 'replica', 0, 0)  6.09 us
    unnamed x13, local copies, waits for them, and re-layouts  3.63 us
  transfers between devices with their start and end apart: 7, of which 4 were waited for; matrix products, arithmetic and copies ran while one was open for 3% of the time, Pallas kernels for 3%

profile of v1, /device:TPU:1, one launch (start us, length us, event | category | flops | bytes accessed | tf_op | source)
XLA Modules:
  0.0 90.0 jit_solution(149442969349309133)
XLA Ops:
  0.6 0.9 copy.9
  1.5 0.1 reshape.10.index
  1.7 1.0 %copy-done = f32[1,16,6144]{2,1,0:T(8,128)S(1)} copy-done((f32[1,16,6144]{2,1,0:T(8,128)S(1)}, f32[1,16,6144]{2,1,0:T(8,128)}, u32[]{:S(2)}) %copy-start) | copy-done | bytes 393240
  2.7 0.8 copy-done.1
  3.5 0.9 %copy-done.4 = bf16[1,16,6144]{2,1,0:T(8,128)(2,1)S(1)} copy-done((bf16[1,16,6144]{2,1,0:T(8,128)(2,1)S(1)}, bf16[1,16,6144]{2,1,0:T(8,128)(2,1)}, u32[]{:S(2)}) %copy-start.4) | copy-done | bytes 196632
  4.4 2.0 %local_step.1 = (f32[1,16,6144]{2,1,0:T(8,128)}, bf16[16,16,384]{2,1,0:T(8,128)(2,1)}) custom-call(f32[1,16,6144]{2,1,0:T(8,128)S(1)} %copy-done, bf16[1,16,6144]{2,1,0:T(8,128)(2,1)S(1)} %copy-done.4, s32[8,768]{1,0:T(8,128)S(1)} %reshape.10.index, f32[128,128]{1,0:T(8,128)S(1)} %copy-done.1), custom_call_target="tpu_custom_call" | custom-call | flops 100000000 | bytes 1269760 | tf_op jit(solution)/shard_map/local_step/pallas_call | solution.py:122
  6.5 11.8 %all-to-all-start = ((bf16[16,16,384]{2,1,0:T(8,128)(2,1)}), bf16[16,16,384]{2,1,0:T(8,128)(2,1)S(1)}, u32[]{:S(2)}, u32[]{:S(2)}) async-start(bf16[16,16,384]{2,1,0:T(8,128)(2,1)} %get-tuple-element.6), calls=%async_computation | async-start | bytes 393216 | tf_op jit(solution)/shard_map/exchange/all_to_all | solution.py:177
  18.3 2.1 %constant_dynamic-slice_fusion.7 = bf16[128,3072]{1,0:T(8,128)(2,1)} fusion(bf16[128,6144]{1,0:T(8,128)(2,1)} %param.6, s32[]{:T(128)S(6)} %select_n.66), kind=kLoop, calls=%fused_computation.11 | loop fusion | bytes 1572868 | tf_op jit(solution)/shard_map/tokens_core/dynamic_slice | solution.py:143
  20.4 2.2 %collective-permute-start = (bf16[128,3072]{1,0:T(8,128)(2,1)}, bf16[128,3072]{1,0:T(8,128)(2,1)S(1)}, u32[]{:S(2)}, u32[]{:S(2)}) collective-permute-start(bf16[128,3072]{1,0:T(8,128)(2,1)} %constant_dynamic-slice_fusion.7), channel_id=1, source_target_pairs={{0,1},{1,0},{2,3},{3,2},{4,5},{5,4},{6,7},{7,6},{8,9},{9,8},{10,11... | collective-permute-start | bytes 2359304 | tf_op jit(solution)/shard_map/tokens_core/ppermute | solution.py:145
  22.6 6.1 %all-to-all-done.received = bf16[16,16,384]{2,1,0:T(8,128)(2,1)S(1)} async-done(((bf16[16,16,384]{2,1,0:T(8,128)(2,1)}), bf16[16,16,384]{2,1,0:T(8,128)(2,1)S(1)}, u32[]{:S(2)}, u32[]{:S(2)}) %all-to-all-start) | async-done | bytes 196640 | tf_op jit(solution)/shard_map/exchange/all_to_all | solution.py:177
  28.6 2.7 %renew.1 = bf16[32,16,768]{2,1,0:T(8,128)(2,1)} custom-call(bf16[16,16,384]{2,1,0:T(8,128)(2,1)S(1)} %all-to-all-done.received, bf16[16,6144]{1,0:T(8,128)(2,1)S(1)} %copy-done.3, f32[128,128]{1,0:T(8,128)S(1)} %copy-done.2), custom_call_target="tpu_custom_call" | custom-call | flops 100000000 | bytes 1245184 | tf_op jit(solution)/shard_map/renew/pallas_call | solution.py:122
  31.3 9.7 %all-to-all-start.1 = ((bf16[32,16,768]{2,1,0:T(8,128)(2,1)}), bf16[32,16,768]{2,1,0:T(8,128)(2,1)S(1)}, u32[]{:S(2)}, u32[]{:S(2)}) async-start(bf16[32,16,768]{2,1,0:T(8,128)(2,1)} %renew.1), calls=%async_computation.1 | async-start | bytes 1572864 | tf_op jit(solution)/shard_map/window/all_to_all | solution.py:183
  41.1 0.5 constant_dynamic-slice_fusion.1
  41.8 3.1 %collective-permute-start.1 = (bf16[256,768]{1,0:T(8,128)(2,1)S(1)}, bf16[256,768]{1,0:T(8,128)(2,1)S(1)}, u32[]{:S(2)}, u32[]{:S(2)}) collective-permute-start(bf16[256,768]{1,0:T(8,128)(2,1)S(1)} %pad_maximum_fusion.1), channel_id=1, source_target_pairs={{0,16},{16,32},{32,48},{48,0},{64,80},{80,96},{96,112},{112,64},{1... | collective-permute-start | bytes 1179656 | tf_op jit(solution)/shard_map/tokens_x/ppermute | solution.py:171
  44.9 4.3 %collective-permute-start.2 = (bf16[256,768]{1,0:T(8,128)(2,1)S(1)}, bf16[256,768]{1,0:T(8,128)(2,1)S(1)}, u32[]{:S(2)}, u32[]{:S(2)}) collective-permute-start(bf16[256,768]{1,0:T(8,128)(2,1)S(1)} %pad_maximum_fusion.2), channel_id=1, source_target_pairs={{0,32},{16,48},{32,0},{48,16},{64,96},{80,112},{96,64},{112,80},{1... | collective-permute-start | bytes 1179656 | tf_op jit(solution)/shard_map/tokens_x/ppermute | solution.py:171
  49.3 3.1 %collective-permute-start.3 = (bf16[256,768]{1,0:T(8,128)(2,1)S(1)}, bf16[256,768]{1,0:T(8,128)(2,1)S(1)}, u32[]{:S(2)}, u32[]{:S(2)}) collective-permute-start(bf16[256,768]{1,0:T(8,128)(2,1)S(1)} %pad_maximum_fusion.3), channel_id=1, source_target_pairs={{0,48},{16,0},{32,16},{48,32},{64,112},{80,64},{96,80},{112,96},{1... | collective-permute-start | bytes 1179656 | tf_op jit(solution)/shard_map/tokens_x/ppermute | solution.py:171
  52.4 10.6 %collective-permute-done.1.t1 = bf16[256,768]{1,0:T(8,128)(2,1)S(1)} collective-permute-done((bf16[256,768]{1,0:T(8,128)(2,1)S(1)}, bf16[256,768]{1,0:T(8,128)(2,1)S(1)}, u32[]{:S(2)}, u32[]{:S(2)}) %collective-permute-start.1) | collective-permute-done | bytes 393248 | tf_op jit(solution)/shard_map/tokens_x/ppermute | solution.py:171
  63.0 8.8 %collective-permute-done.2.t2 = bf16[256,768]{1,0:T(8,128)(2,1)S(1)} collective-permute-done((bf16[256,768]{1,0:T(8,128)(2,1)S(1)}, bf16[256,768]{1,0:T(8,128)(2,1)S(1)}, u32[]{:S(2)}, u32[]{:S(2)}) %collective-permute-start.2) | collective-permute-done | bytes 393248 | tf_op jit(solution)/shard_map/tokens_x/ppermute | solution.py:171
  71.7 1.0 %product.1 = (f32[4,128,512]{2,1,0:T(8,128)S(1)}, bf16[4,128,512]{2,1,0:T(8,128)(2,1)S(1)}) custom-call(bf16[256,768]{1,0:T(8,128)(2,1)S(1)} %pad_maximum_fusion.t0, bf16[256,768]{1,0:T(8,128)(2,1)S(1)} %collective-permute-done.1.t1, bf16[256,768]{1,0:T(8,128)(2,1)S(1)} %collective-permute-done.2.t2, bf16[256,768]{1,0:T(8,128)(2,1)S(1)} %collective-permute-done.3.t3, ...), custom_call_target="tpu_custom_call" | custom-call | flops 805306368 | bytes 3932160 | tf_op jit(solution)/shard_map/product/pallas_call | solution.py:122
  72.8 2.8 %collective-permute-start.4 = (bf16[4,128,512]{2,1,0:T(8,128)(2,1)S(1)}, bf16[4,128,512]{2,1,0:T(8,128)(2,1)S(1)}, u32[]{:S(2)}, u32[]{:S(2)}) collective-permute-start(bf16[4,128,512]{2,1,0:T(8,128)(2,1)S(1)} %get-tuple-element.8), channel_id=1, source_target_pairs={{0,1},{1,0},{2,3},{3,2},{4,5},{5,4},{6,7},{7,6},{8,9},{9,8},{10,11... | collective-permute-start | bytes 1572872 | tf_op jit(solution)/shard_map/sum_core/ppermute | solution.py:194
  75.5 1.5 %collective-permute-done.4.arrived = bf16[4,128,512]{2,1,0:T(8,128)(2,1)S(1)} collective-permute-done((bf16[4,128,512]{2,1,0:T(8,128)(2,1)S(1)}, bf16[4,128,512]{2,1,0:T(8,128)(2,1)S(1)}, u32[]{:S(2)}, u32[]{:S(2)}) %collective-permute-start.4) | collective-permute-done | bytes 524320 | tf_op jit(solution)/shard_map/sum_core/ppermute | solution.py:194
  77.0 0.1 sum_core.1
  77.1 12.2 %all_to_all.15.parts = bf16[4,128,512]{2,1,0:T(8,128)(2,1)S(1)} all-to-all(bf16[4,128,512]{2,1,0:T(8,128)(2,1)S(1)} %sum_core.1), channel_id=1, replica_groups={{0,16,32,48},{64,80,96,112},{128,144,160,176},{192,208,224,240},{256,27..., dimensions={0} | all-to-all | bytes 1048576 | tf_op jit(solution)/shard_map/sum_x/all_to_all | solution.py:198
  89.3 0.7 sum_x.1
  (18 shorter events, 0.2 us)
Async XLA Ops:
  1.5 27.1 %copy-start.2 = (f32[128,128]{1,0:T(8,128)S(1)}, f32[128,128]{1,0:T(8,128)}, u32[]{:S(2)}) copy-start(f32[128,128]{1,0:T(8,128)} %constant.96.clone.table) | copy-start | bytes 196612
  1.5 27.1 %copy-start.3 = (bf16[16,6144]{1,0:T(8,128)(2,1)S(1)}, bf16[16,6144]{1,0:T(8,128)(2,1)}, u32[]{:S(2)}) copy-start(bf16[16,6144]{1,0:T(8,128)(2,1)} %weight.1) | copy-start | bytes 589828
  1.7 1.0 %copy-start = (f32[1,16,6144]{2,1,0:T(8,128)S(1)}, f32[1,16,6144]{2,1,0:T(8,128)}, u32[]{:S(2)}) copy-start(f32[1,16,6144]{2,1,0:T(8,128)} %momentum.1) | copy-start | bytes 1179652
  2.7 0.8 copy-start.1
  3.5 0.9 %copy-start.4 = (bf16[1,16,6144]{2,1,0:T(8,128)(2,1)S(1)}, bf16[1,16,6144]{2,1,0:T(8,128)(2,1)}, u32[]{:S(2)}) copy-start(bf16[1,16,6144]{2,1,0:T(8,128)(2,1)} %gradient.1) | copy-start | bytes 589828
  6.5 22.2 %all-to-all-start = ((bf16[16,16,384]{2,1,0:T(8,128)(2,1)}), bf16[16,16,384]{2,1,0:T(8,128)(2,1)S(1)}, u32[]{:S(2)}, u32[]{:S(2)}) async-start(bf16[16,16,384]{2,1,0:T(8,128)(2,1)} %get-tuple-element.6), calls=%async_computation | async-start | bytes 393216 | tf_op jit(solution)/shard_map/exchange/all_to_all | solution.py:177
  20.4 20.7 %copy-start.5 = (bf16[128,6144]{1,0:T(8,128)(2,1)S(1)}, bf16[128,6144]{1,0:T(8,128)(2,1)}, u32[]{:S(2)}) copy-start(bf16[128,6144]{1,0:T(8,128)(2,1)} %param.6) | copy-start | bytes 4718596
  20.4 21.2 %collective-permute-start = (bf16[128,3072]{1,0:T(8,128)(2,1)}, bf16[128,3072]{1,0:T(8,128)(2,1)S(1)}, u32[]{:S(2)}, u32[]{:S(2)}) collective-permute-start(bf16[128,3072]{1,0:T(8,128)(2,1)} %constant_dynamic-slice_fusion.7), channel_id=1, source_target_pairs={{0,1},{1,0},{2,3},{3,2},{4,5},{5,4},{6,7},{7,6},{8,9},{9,8},{10,11... | collective-permute-start | bytes 2359304 | tf_op jit(solution)/shard_map/tokens_core/ppermute | solution.py:145
  31.3 40.4 %all-to-all-start.1 = ((bf16[32,16,768]{2,1,0:T(8,128)(2,1)}), bf16[32,16,768]{2,1,0:T(8,128)(2,1)S(1)}, u32[]{:S(2)}, u32[]{:S(2)}) async-start(bf16[32,16,768]{2,1,0:T(8,128)(2,1)} %renew.1), calls=%async_computation.1 | async-start | bytes 1572864 | tf_op jit(solution)/shard_map/window/all_to_all | solution.py:183
  41.8 21.2 %collective-permute-start.1 = (bf16[256,768]{1,0:T(8,128)(2,1)S(1)}, bf16[256,768]{1,0:T(8,128)(2,1)S(1)}, u32[]{:S(2)}, u32[]{:S(2)}) collective-permute-start(bf16[256,768]{1,0:T(8,128)(2,1)S(1)} %pad_maximum_fusion.1), channel_id=1, source_target_pairs={{0,16},{16,32},{32,48},{48,0},{64,80},{80,96},{96,112},{112,64},{1... | collective-permute-start | bytes 1179656 | tf_op jit(solution)/shard_map/tokens_x/ppermute | solution.py:171
  44.9 26.8 %collective-permute-start.2 = (bf16[256,768]{1,0:T(8,128)(2,1)S(1)}, bf16[256,768]{1,0:T(8,128)(2,1)S(1)}, u32[]{:S(2)}, u32[]{:S(2)}) collective-permute-start(bf16[256,768]{1,0:T(8,128)(2,1)S(1)} %pad_maximum_fusion.2), channel_id=1, source_target_pairs={{0,32},{16,48},{32,0},{48,16},{64,96},{80,112},{96,64},{112,80},{1... | collective-permute-start | bytes 1179656 | tf_op jit(solution)/shard_map/tokens_x/ppermute | solution.py:171
  49.3 22.4 %collective-permute-start.3 = (bf16[256,768]{1,0:T(8,128)(2,1)S(1)}, bf16[256,768]{1,0:T(8,128)(2,1)S(1)}, u32[]{:S(2)}, u32[]{:S(2)}) collective-permute-start(bf16[256,768]{1,0:T(8,128)(2,1)S(1)} %pad_maximum_fusion.3), channel_id=1, source_target_pairs={{0,48},{16,0},{32,16},{48,32},{64,112},{80,64},{96,80},{112,96},{1... | collective-permute-start | bytes 1179656 | tf_op jit(solution)/shard_map/tokens_x/ppermute | solution.py:171
  72.8 4.3 %collective-permute-start.4 = (bf16[4,128,512]{2,1,0:T(8,128)(2,1)S(1)}, bf16[4,128,512]{2,1,0:T(8,128)(2,1)S(1)}, u32[]{:S(2)}, u32[]{:S(2)}) collective-permute-start(bf16[4,128,512]{2,1,0:T(8,128)(2,1)S(1)} %get-tuple-element.8), channel_id=1, source_target_pairs={{0,1},{1,0},{2,3},{3,2},{4,5},{5,4},{6,7},{7,6},{8,9},{9,8},{10,11... | collective-permute-start | bytes 1572872 | tf_op jit(solution)/shard_map/sum_core/ppermute | solution.py:194

commit v2 on v1

--- a/solution.py
+++ b/solution.py
@@ -14,6 +14,8 @@
 PAIR = 2 * GROUP
 XS = 4
 YS = 8
+MEMBERS = 2 * XS
+VMEM_BYTES = 60 * 1024 * 1024
 F32 = jnp.float32
 BF16 = jnp.bfloat16
 HIGH = lax.Precision.HIGHEST
@@ -34,32 +36,93 @@
     return lax.dot_general(a, b, (((da,), (db,)), ((), ())), precision=HIGH, preferred_element_type=F32)
 
 
-def step_kernel(momentum, gradient, index, table, new_momentum, send):
-    rows, width = momentum.shape[1:]
+def swap_kernel(t0, t1, t2, t3, away):
+    core = lax.axis_index("replica") % 2
+    for d, tokens in enumerate((t0, t1, t2, t3)):
+        away[d] = tokens[1 - core]
+
+
+def lay_out(indices, lanes):
+    rows, _, groups = indices.shape
+    spread = lax.broadcasted_iota(jnp.int32, (rows, lanes), 1) % rows
+    spread = jnp.where(spread == lax.broadcasted_iota(jnp.int32, (rows, lanes), 0), 1.0, 0.0).astype(BF16)
+    pair = lax.broadcasted_iota(jnp.int32, (groups, lanes), 1) // rows
+    transform = lax.broadcasted_iota(jnp.int32, (groups, lanes), 0)
+    spreads = [
+        lax.dot_general(
+            indices[:, j, :].astype(F32).astype(BF16), spread, (((0,), (0,)), ((), ())), preferred_element_type=F32
+        )
+        for j in range(TOPK)
+    ]
+    return [
+        jnp.sum(jnp.where(transform == 2 * pair + side, spreads[j], 0.0), axis=0, keepdims=True)
+        for side in range(2)
+        for j in range(TOPK)
+    ]
+
+
+def choose(momentum, gradient, indices, table):
+    rows, width = momentum.shape
     pairs = width // PAIR
     lanes = pairs * rows
-    blended = DECAY * momentum[0] + gradient[0].astype(F32)
+    blended = DECAY * momentum + gradient.astype(F32)
     stacked = jnp.concatenate([blended[:, p * PAIR : (p + 1) * PAIR] for p in range(pairs)], axis=0)
-    spectra = contract(table[...], stacked, 1, 1)
-    freq = lax.broadcasted_iota(jnp.int32, (GROUP, lanes), 0)
-    values, kept = [], []
+    spectra = contract(table, stacked, 1, 1)
+    freq = lax.broadcasted_iota(jnp.int32, (GROUP, lanes), 0).astype(F32)
+    index = lay_out(indices, lanes)
+    picked = []
     for side in range(2):
         part = spectra[side * GROUP : (side + 1) * GROUP]
-        keep = jnp.zeros_like(part)
-        for j in range(TOPK):
-            hot = freq == index[side * TOPK + j][None, :]
-            one = jnp.where(hot, part, 0.0)
-            values.append(jnp.sum(one, axis=0, keepdims=True))
-            keep = keep + one
-        kept.append(keep)
-    field = contract(jnp.concatenate(kept, axis=0), table[...], 0, 0)
-    for p in range(pairs):
+        picked += [jnp.where(freq == index[side * TOPK + j], part, 0.0) for j in range(TOPK)]
+    return blended, index, picked
+
+
+def fetch(pairs, sems):
+    copies = [pltpu.make_async_copy(a, b, sems.at[i]) for i, (a, b) in enumerate(pairs)]
+    for copy in copies:
+        copy.start()
+    return copies
+
+
+def send_kernel(
+    tokens, momentum, gradient, indices, table, send, c0, c1, c2, c3, cut, mom, grad, ind, tab, sems
+):
+    x = lax.axis_index("shard") % XS
+    piece = cut.shape[2]
+    loads = fetch([(momentum, mom), (gradient, grad), (indices, ind), (table, tab)], sems)
+    pieces, first = [], len(loads)
+    for d in range(XS):
+        for h in range(2):
+            at = pl.multiple_of((h * XS + (x + d) % XS) * piece, 128)
+            pieces.append((tokens.at[:, pl.ds(at, piece)], cut.at[2 * d + h]))
+    cuts = fetch(pieces, sems.at[pl.ds(first, MEMBERS)])
+    for load in loads:
+        load.wait()
+    _, index, picked = choose(mom[0], grad[0], ind, tab[...])
+    values = [jnp.sum(p, axis=0, keepdims=True) for p in picked]
+    message = jnp.concatenate(values + index, axis=0).astype(BF16)
+    half = message.shape[1] // 2
+    for r in range(send.shape[0]):
+        send[r] = message[:, r % 2 * half : (r % 2 + 1) * half]
+    for c in cuts:
+        c.wait()
+    outs = fetch(
+        [(cut.at[pl.ds(2 * d, 2)], c) for d, c in enumerate((c0, c1, c2, c3))], sems.at[pl.ds(first + MEMBERS, XS)]
+    )
+    for out in outs:
+        out.wait()
+
+
+def remain_kernel(momentum, gradient, indices, table, new_momentum, mom, grad, ind, tab, sems):
+    for load in fetch([(momentum, mom), (gradient, grad), (indices, ind), (table, tab)], sems):
+        load.wait()
+    rows = mom.shape[1]
+    blended, _, picked = choose(mom[0], grad[0], ind, tab[...])
+    kept = [sum(picked[side * TOPK + 1 : (side + 1) * TOPK], picked[side * TOPK]) for side in range(2)]
+    field = contract(jnp.concatenate(kept, axis=0), tab[...], 0, 0)
+    for p in range(blended.shape[1] // PAIR):
         at = slice(p * PAIR, (p + 1) * PAIR)
         new_momentum[0, :, at] = blended[:, at] - field[p * rows : (p + 1) * rows]
-    message = jnp.concatenate(values + [index[...].astype(F32)], axis=0).astype(BF16)
-    for r in range(send.shape[0]):
-        half = r % 2
-        send[r] = message[:, half * lanes // 2 : (half + 1) * lanes // 2]
 
 
 def renew_kernel(received, weight, table, renewed):
@@ -93,14 +156,14 @@
                 renewed[y * XS + x, :, p * PAIR : (p + 1) * PAIR] = new
 
 
-def product_kernel(t0, t1, t2, t3, window, mine, other):
-    count = mine.shape[1]
+def product_kernel(t0, t1, t2, t3, came, window, mine, other):
+    core = lax.axis_index("replica") % 2
+    count = came.shape[1]
     for d, tokens in enumerate((t0, t1, t2, t3)):
-        out = lax.dot_general(
-            tokens[...], window[...], (((1,), (1,)), ((), ())), preferred_element_type=F32
-        )
-        mine[d] = out[:count]
-        other[d] = out[count:].astype(BF16)
+        block = jnp.concatenate([came[d], tokens[core]], axis=0)
+        product = lax.dot_general(block, window[...], (((1,), (1,)), ((), ())), preferred_element_type=F32)
+        other[d] = product[:count].astype(BF16)
+        mine[d] = product[count:]
 
 
 def order_kernel(mine, arrived, out):
@@ -124,7 +187,7 @@
         out_shape=out,
         in_specs=[pl.BlockSpec(memory_space=pltpu.VMEM)] * len(args),
         out_specs=jax.tree.map(lambda _: pl.BlockSpec(memory_space=pltpu.VMEM), out),
-        compiler_params=pltpu.CompilerParams(vmem_limit_bytes=40 * 1024 * 1024),
+        compiler_params=pltpu.CompilerParams(vmem_limit_bytes=20 * 1024 * 1024),
         cost_estimate=pl.CostEstimate(flops=flops, bytes_accessed=moved, transcendentals=0),
     )(*args)
 
@@ -134,51 +197,58 @@
     rows = weight.shape[0]
     half, piece = width // 2, width // 2 // XS
     table = jnp.asarray(pair_table())
-    core = lax.axis_index("replica") % 2
-    x = lax.axis_index("shard") % XS
     replicas = lax.axis_size("replica")
     shards = lax.axis_size("shard")
 
-    with jax.named_scope("tokens_core"):
-        away = lax.dynamic_slice(tokens, (0, (1 - core) * half), (count, half))
-        here = lax.dynamic_slice(tokens, (0, core * half), (count, half))
-        came = lax.ppermute(away, "replica", [(i, i ^ 1) for i in range(replicas)])
-
-    with jax.named_scope("local_step"):
-        lanes = width // PAIR * rows
-        index = indices[0].reshape(rows, width // PAIR, 2, TOPK).transpose(2, 3, 1, 0).reshape(2 * TOPK, lanes)
-        new_momentum, send = call(
-            step_kernel,
-            (
-                jax.ShapeDtypeStruct(momentum.shape, F32),
-                jax.ShapeDtypeStruct((replicas, 4 * TOPK, lanes // 2), BF16),
-            ),
-            momentum,
-            gradient,
-            index,
-            table,
-            flops=10**8,
-        )
-
-    with jax.named_scope("tokens_x"):
-        blocks = []
-        for d in range(XS):
-            start = (x + d) % XS * piece
-            block = jnp.concatenate(
-                [lax.dynamic_slice(a, (0, start), (count, piece)) for a in (here, came)], axis=0
-            )
-            if d > 0:
-                block = lax.ppermute(
-                    block, "shard", [(s, s // XS * XS + (s + d) % XS) for s in range(shards)]
-                )
-            blocks.append(block)
+    lanes = width // PAIR * rows
+    ordered_indices = indices[0].transpose(0, 2, 1)
+    local_scratch = [
+        pltpu.VMEM(momentum.shape, F32),
+        pltpu.VMEM(gradient.shape, BF16),
+        pltpu.VMEM(ordered_indices.shape, jnp.int32),
+        pltpu.VMEM(table.shape, F32),
+    ]
+    hbm, vmem = pl.BlockSpec(memory_space=pltpu.HBM), pl.BlockSpec(memory_space=pltpu.VMEM)
+    params = pltpu.CompilerParams(vmem_limit_bytes=VMEM_BYTES)
+    with jax.named_scope("coefficients"):
+        send, *cut = pl.pallas_call(
+            send_kernel,
+            out_shape=[jax.ShapeDtypeStruct((replicas, 4 * TOPK, lanes // 2), BF16)]
+            + [jax.ShapeDtypeStruct((2, count, piece), BF16)] * XS,
+            in_specs=[hbm] * 5,
+            out_specs=[vmem] + [hbm] * XS,
+            scratch_shapes=[pltpu.VMEM((MEMBERS, count, piece), BF16)]
+            + local_scratch
+            + [pltpu.SemaphoreType.DMA((4 + MEMBERS + XS,))],
+            compiler_params=params,
+            cost_estimate=pl.CostEstimate(flops=10**8, bytes_accessed=4 * 10**6, transcendentals=0),
+        )(tokens, momentum, gradient, ordered_indices, table)
 
     with jax.named_scope("exchange"):
         received = lax.all_to_all(send, "replica", 0, 0)
     with jax.named_scope("renew"):
         renewed = call(
-            renew_kernel, jax.ShapeDtypeStruct((shards, rows, piece), BF16), received, weight, table, flops=10**8
+            renew_kernel, jax.ShapeDtypeStruct((shards, rows, piece), BF16), received, weight, table, flops=10**10
         )
+    with jax.named_scope("momentum"):
+        momentum, renewed = lax.optimization_barrier((momentum, renewed))
+        new_momentum = pl.pallas_call(
+            remain_kernel,
+            out_shape=jax.ShapeDtypeStruct(momentum.shape, F32),
+            in_specs=[hbm] * 4,
+            out_specs=vmem,
+            scratch_shapes=local_scratch + [pltpu.SemaphoreType.DMA((4,))],
+            compiler_params=params,
+            cost_estimate=pl.CostEstimate(flops=5 * 10**10, bytes_accessed=10**6, transcendentals=0),
+        )(momentum, gradient, ordered_indices, table)
+    with jax.named_scope("tokens_x"):
+        blocks = [cut[0]] + [
+            lax.ppermute(cut[d], "shard", [(s, s // XS * XS + (s + d) % XS) for s in range(shards)])
+            for d in range(1, XS)
+        ]
+    with jax.named_scope("tokens_core"):
+        away = call(swap_kernel, jax.ShapeDtypeStruct((XS, count, piece), BF16), *blocks, flops=5 * 10**10)
+        came = lax.ppermute(away, "replica", [(i, i ^ 1) for i in range(replicas)])
     with jax.named_scope("window"):
         window = lax.all_to_all(renewed, "shard", 0, 0).reshape(shards * rows, piece)
     with jax.named_scope("product"):
@@ -187,6 +257,7 @@
             product_kernel,
             (jax.ShapeDtypeStruct(shape, F32), jax.ShapeDtypeStruct(shape, BF16)),
             *blocks,
+            came,
             window,
             flops=2 * 1024 * 768 * 512,
         )

time: 90.7 us -> 82.5 us (0.910)
  blocking collectives: 12.2 us -> 0 us
  local copies, waits for them, and re-layouts: 6.44 us -> 0.01 us
  Pallas kernels: 6.53 us -> 12.5 us
  starting transfers between devices: 36.9 us -> 42.2 us
    ppermute x3, waiting for transfers between devices: 19.3 us -> 1.81 us  [local(): lax.ppermute(cut[d], 'shard', [(s, s // XS * XS + (s + d) % XS) for s in...]
    all_to_all x1, waiting for transfers between devices: 0.01 us -> 15.5 us  [local(): lax.all_to_all(renewed, 'shard', 0, 0).reshape(shards * rows, piece)]
    all_to_all x1 -> x0, blocking collectives: 12.2 us -> none  [local(): parts = lax.all_to_all(ordered, 'shard', 0, 0, axis_index_groups=groups)]
    pallas_call x0 -> x2, Pallas kernels: none -> 7.2 us  [the longest x1 4.07 us: local(): pl.pallas_call(send_kernel, out_shape=[jax.ShapeDtypeStruct((replicas, 4...]
    all_to_all x1, waiting for transfers between devices: 6.09 us -> 0.01 us  [local(): received = lax.all_to_all(send, 'replica', 0, 0)]
    all_to_all x0 -> x1, waiting for transfers between devices: none -> 5.77 us  [local(): parts = lax.all_to_all(ordered, 'shard', 0, 0, axis_index_groups=groups)]
    all_to_all x0 -> x1, starting transfers between devices: none -> 4.22 us  [local(): parts = lax.all_to_all(ordered, 'shard', 0, 0, axis_index_groups=groups)]
    unnamed x13 -> x6, local copies, waits for them, and re-layouts: 3.63 us -> 0.01 us
  transfers between devices with their start and end apart: 7 -> 8, of which waited for: 4 -> 6; matrix products, arithmetic and copies ran while one was open for 3% -> 0% of each run, Pallas kernels for 3% -> 7%
where the time goes in v2:
time: 82.5 us; the launch traced here: 82 us
  starting transfers between devices  42.2 us (51%)
  waiting for transfers between devices  26.5 us (32%)
  Pallas kernels  12.5 us (15%)
    all_to_all x1, waiting for transfers between devices, local(): lax.all_to_all(renewed, 'shard', 0, 0).reshape(shards * rows, piece)  15.5 us
    all_to_all x1, starting transfers between devices, local(): received = lax.all_to_all(send, 'replica', 0, 0)  11.8 us
    ppermute x3, starting transfers between devices, local(): lax.ppermute(cut[d], 'shard', [(s, s // XS * XS + (s + d) % XS) for s in...  10.6 us
    all_to_all x1, starting transfers between devices, local(): lax.all_to_all(renewed, 'shard', 0, 0).reshape(shards * rows, piece)  9.53 us
    all_to_all x1, waiting for transfers between devices, local(): parts = lax.all_to_all(ordered, 'shard', 0, 0, axis_index_groups=groups)  5.77 us
    pallas_call x5, Pallas kernels, call(): pl.pallas_call(kernel, out_shape=out, in_specs=[pl.BlockSpec(memory_space...  5.32 us
    all_to_all x1, starting transfers between devices, local(): parts = lax.all_to_all(ordered, 'shard', 0, 0, axis_index_groups=groups)  4.22 us
    pallas_call x1, Pallas kernels, local(): pl.pallas_call(send_kernel, out_shape=[jax.ShapeDtypeStruct((replicas, 4...  4.07 us
  transfers between devices with their start and end apart: 8, of which 6 were waited for; matrix products, arithmetic and copies ran while one was open for 0% of the time, Pallas kernels for 7%

profile of v2, /device:TPU:1, one launch (start us, length us, event | category | flops | bytes accessed | tf_op | source)
XLA Modules:
  0.0 82.0 jit_solution(16397297761592700027)
XLA Ops:
  0.6 0.0 copy-start.1
  0.7 4.1 %coefficients.1 = (bf16[16,16,384]{2,1,0:T(8,128)(2,1)}, bf16[2,128,768]{2,1,0:T(8,128)(2,1)}, bf16[2,128,768]{2,1,0:T(8,128)(2,1)}, bf16[2,128,768]{2,1,0:T(8,128)(2,1)}, bf16[2,128,768]{2,1,0:T(8,128)(2,1)}) custom-call(bf16[128,6144]{1,0:T(8,128)(2,1)} %tokens.1, f32[1,16,6144]{2,1,0:T(8,128)} %momentum.4, bf16[1,16,6144]{2,1,0:T(8,128)(2,1)} %gradient.3, ...), custom_call_target="tpu_custom_call" | custom-call | flops 100000000 | bytes 4000000 | tf_op jit(solution)/shard_map/coefficients/pallas_call | solution.py:214
  4.7 11.8 %all-to-all-start = ((bf16[16,16,384]{2,1,0:T(8,128)(2,1)}), bf16[16,16,384]{2,1,0:T(8,128)(2,1)S(1)}, u32[]{:S(2)}, u32[]{:S(2)}) async-start(bf16[16,16,384]{2,1,0:T(8,128)(2,1)} %get-tuple-element.15), calls=%async_computation | async-start | bytes 393216 | tf_op jit(solution)/shard_map/exchange/all_to_all | solution.py:228
  16.6 3.1 %collective-permute-start = (bf16[2,128,768]{2,1,0:T(8,128)(2,1)}, bf16[2,128,768]{2,1,0:T(8,128)(2,1)S(1)}, u32[]{:S(2)}, u32[]{:S(2)}) collective-permute-start(bf16[2,128,768]{2,1,0:T(8,128)(2,1)} %get-tuple-element.12), channel_id=1, source_target_pairs={{0,16},{16,32},{32,48},{48,0},{64,80},{80,96},{96,112},{112,64},{1... | collective-permute-start | bytes 1179656 | tf_op jit(solution)/shard_map/tokens_x/ppermute | solution.py:246
  19.7 4.4 %collective-permute-start.1 = (bf16[2,128,768]{2,1,0:T(8,128)(2,1)}, bf16[2,128,768]{2,1,0:T(8,128)(2,1)S(1)}, u32[]{:S(2)}, u32[]{:S(2)}) collective-permute-start(bf16[2,128,768]{2,1,0:T(8,128)(2,1)} %get-tuple-element.13), channel_id=1, source_target_pairs={{0,32},{16,48},{32,0},{48,16},{64,96},{80,112},{96,64},{112,80},{1... | collective-permute-start | bytes 1179656 | tf_op jit(solution)/shard_map/tokens_x/ppermute | solution.py:246
  24.1 3.1 %collective-permute-start.2 = (bf16[2,128,768]{2,1,0:T(8,128)(2,1)}, bf16[2,128,768]{2,1,0:T(8,128)(2,1)S(1)}, u32[]{:S(2)}, u32[]{:S(2)}) collective-permute-start(bf16[2,128,768]{2,1,0:T(8,128)(2,1)} %get-tuple-element.14), channel_id=1, source_target_pairs={{0,48},{16,0},{32,16},{48,32},{64,112},{80,64},{96,80},{112,96},{1... | collective-permute-start | bytes 1179656 | tf_op jit(solution)/shard_map/tokens_x/ppermute | solution.py:246
  27.2 0.0 all-to-all-done.received
  27.2 2.7 %renew.1 = bf16[32,16,768]{2,1,0:T(8,128)(2,1)} custom-call(bf16[16,16,384]{2,1,0:T(8,128)(2,1)S(1)} %all-to-all-done.received, bf16[16,6144]{1,0:T(8,128)(2,1)S(1)} %copy-done.2, f32[128,128]{1,0:T(8,128)S(1)} %copy-done.1), custom_call_target="tpu_custom_call" | custom-call | flops 10000000000 | bytes 1245184 | tf_op jit(solution)/shard_map/renew/pallas_call | solution.py:185
  29.9 9.5 %all-to-all-start.1 = ((bf16[32,16,768]{2,1,0:T(8,128)(2,1)}), bf16[32,16,768]{2,1,0:T(8,128)(2,1)S(1)}, u32[]{:S(2)}, u32[]{:S(2)}) async-start(bf16[32,16,768]{2,1,0:T(8,128)(2,1)} %renew.1), calls=%async_computation.1 | async-start | bytes 1572864 | tf_op jit(solution)/shard_map/window/all_to_all | solution.py:253
  39.4 0.0 collective-permute-done.t1
  39.4 0.6 collective-permute-done.1.t2
  40.0 1.2 %collective-permute-done.2.t3 = bf16[2,128,768]{2,1,0:T(8,128)(2,1)S(1)} collective-permute-done((bf16[2,128,768]{2,1,0:T(8,128)(2,1)}, bf16[2,128,768]{2,1,0:T(8,128)(2,1)S(1)}, u32[]{:S(2)}, u32[]{:S(2)}) %collective-permute-start.2) | collective-permute-done | bytes 393248 | tf_op jit(solution)/shard_map/tokens_x/ppermute | solution.py:246
  41.2 0.1 tokens_core.1
  41.3 3.1 %collective-permute-start.3 = (bf16[4,128,768]{2,1,0:T(8,128)(2,1)S(1)}, bf16[4,128,768]{2,1,0:T(8,128)(2,1)S(1)}, u32[]{:S(2)}, u32[]{:S(2)}) collective-permute-start(bf16[4,128,768]{2,1,0:T(8,128)(2,1)S(1)} %tokens_core.1), channel_id=1, source_target_pairs={{0,1},{1,0},{2,3},{3,2},{4,5},{5,4},{6,7},{7,6},{8,9},{9,8},{10,11... | collective-permute-start | bytes 2359304 | tf_op jit(solution)/shard_map/tokens_core/ppermute | solution.py:251
  44.4 1.9 %collective-permute-done.3.came = bf16[4,128,768]{2,1,0:T(8,128)(2,1)S(1)} collective-permute-done((bf16[4,128,768]{2,1,0:T(8,128)(2,1)S(1)}, bf16[4,128,768]{2,1,0:T(8,128)(2,1)S(1)}, u32[]{:S(2)}, u32[]{:S(2)}) %collective-permute-start.3) | collective-permute-done | bytes 786464 | tf_op jit(solution)/shard_map/tokens_core/ppermute | solution.py:251
  46.3 15.5 %all-to-all-done.1 = bf16[32,16,768]{2,1,0:T(8,128)(2,1)S(1)} async-done(((bf16[32,16,768]{2,1,0:T(8,128)(2,1)}), bf16[32,16,768]{2,1,0:T(8,128)(2,1)S(1)}, u32[]{:S(2)}, u32[]{:S(2)}) %all-to-all-start.1) | async-done | bytes 786464 | tf_op jit(solution)/shard_map/window/all_to_all | solution.py:253
  61.8 1.0 %product.1 = (f32[4,128,512]{2,1,0:T(8,128)S(1)}, bf16[4,128,512]{2,1,0:T(8,128)(2,1)S(1)}) custom-call(bf16[2,128,768]{2,1,0:T(8,128)(2,1)S(1)} %copy-done, bf16[2,128,768]{2,1,0:T(8,128)(2,1)S(1)} %collective-permute-done.t1, bf16[2,128,768]{2,1,0:T(8,128)(2,1)S(1)} %collective-permute-done.1.t2, bf16[2,128,768]{2,1,0:T(8,128)(2,1)S(1)} %collective-permute-done.2.t3, ...), custom_call_target="tpu_custom_call" | custom-call | flops 805306368 | bytes 4718592 | tf_op jit(solution)/shard_map/product/pallas_call | solution.py:185
  62.8 3.0 %collective-permute-start.4 = (bf16[4,128,512]{2,1,0:T(8,128)(2,1)S(1)}, bf16[4,128,512]{2,1,0:T(8,128)(2,1)S(1)}, u32[]{:S(2)}, u32[]{:S(2)}) collective-permute-start(bf16[4,128,512]{2,1,0:T(8,128)(2,1)S(1)} %get-tuple-element.18), channel_id=1, source_target_pairs={{0,1},{1,0},{2,3},{3,2},{4,5},{5,4},{6,7},{7,6},{8,9},{9,8},{10,11... | collective-permute-start | bytes 1572872 | tf_op jit(solution)/shard_map/sum_core/ppermute | solution.py:265
  65.8 1.5 %collective-permute-done.4.arrived = bf16[4,128,512]{2,1,0:T(8,128)(2,1)S(1)} collective-permute-done((bf16[4,128,512]{2,1,0:T(8,128)(2,1)S(1)}, bf16[4,128,512]{2,1,0:T(8,128)(2,1)S(1)}, u32[]{:S(2)}, u32[]{:S(2)}) %collective-permute-start.4) | collective-permute-done | bytes 524320 | tf_op jit(solution)/shard_map/sum_core/ppermute | solution.py:265
  67.3 0.9 %sum_core.1 = bf16[4,128,512]{2,1,0:T(8,128)(2,1)} custom-call(f32[4,128,512]{2,1,0:T(8,128)S(1)} %get-tuple-element.17.mine, bf16[4,128,512]{2,1,0:T(8,128)(2,1)S(1)} %collective-permute-done.4.arrived), custom_call_target="tpu_custom_call" | custom-call | bytes 2097152 | tf_op jit(solution)/shard_map/sum_core/pallas_call | solution.py:185
  68.2 4.2 %all-to-all-start.2 = ((bf16[4,128,512]{2,1,0:T(8,128)(2,1)}), bf16[4,128,512]{2,1,0:T(8,128)(2,1)S(1)}, u32[]{:S(2)}, u32[]{:S(2)}) async-start(bf16[4,128,512]{2,1,0:T(8,128)(2,1)} %sum_core.1), calls=%async_computation.2 | async-start | bytes 1048576 | tf_op jit(solution)/shard_map/sum_x/all_to_all | solution.py:269
  72.4 3.1 %momentum.3 = f32[1,16,6144]{2,1,0:T(8,128)} custom-call(f32[1,16,6144]{2,1,0:T(8,128)} %momentum.4, bf16[1,16,6144]{2,1,0:T(8,128)(2,1)} %gradient.3, s32[16,4,96]{2,1,0:T(4,128)} %bitcast.6, f32[128,128]{1,0:T(8,128)} %constant.2.clone.table), custom_call_target="tpu_custom_call" | custom-call | flops 49999998976 | bytes 1000000 | tf_op jit(solution)/shard_map/momentum/pallas_call | solution.py:235
  75.5 5.8 %all-to-all-done.2.parts = bf16[4,128,512]{2,1,0:T(8,128)(2,1)S(1)} async-done(((bf16[4,128,512]{2,1,0:T(8,128)(2,1)}), bf16[4,128,512]{2,1,0:T(8,128)(2,1)S(1)}, u32[]{:S(2)}, u32[]{:S(2)}) %all-to-all-start.2) | async-done | bytes 524320 | tf_op jit(solution)/shard_map/sum_x/all_to_all | solution.py:269
  81.3 0.7 sum_x.1
  (5 shorter events, 0.0 us)
Async XLA Ops:
  0.6 26.5 %copy-start.1 = (f32[128,128]{1,0:T(8,128)S(1)}, f32[128,128]{1,0:T(8,128)}, u32[]{:S(2)}) copy-start(f32[128,128]{1,0:T(8,128)} %constant.2.clone.table) | copy-start | bytes 196612
  0.6 26.5 %copy-start.2 = (bf16[16,6144]{1,0:T(8,128)(2,1)S(1)}, bf16[16,6144]{1,0:T(8,128)(2,1)}, u32[]{:S(2)}) copy-start(bf16[16,6144]{1,0:T(8,128)(2,1)} %weight.1) | copy-start | bytes 589828
  4.7 22.4 %all-to-all-start = ((bf16[16,16,384]{2,1,0:T(8,128)(2,1)}), bf16[16,16,384]{2,1,0:T(8,128)(2,1)S(1)}, u32[]{:S(2)}, u32[]{:S(2)}) async-start(bf16[16,16,384]{2,1,0:T(8,128)(2,1)} %get-tuple-element.15), calls=%async_computation | async-start | bytes 393216 | tf_op jit(solution)/shard_map/exchange/all_to_all | solution.py:228
  16.6 22.8 %collective-permute-start = (bf16[2,128,768]{2,1,0:T(8,128)(2,1)}, bf16[2,128,768]{2,1,0:T(8,128)(2,1)S(1)}, u32[]{:S(2)}, u32[]{:S(2)}) collective-permute-start(bf16[2,128,768]{2,1,0:T(8,128)(2,1)} %get-tuple-element.12), channel_id=1, source_target_pairs={{0,16},{16,32},{32,48},{48,0},{64,80},{80,96},{96,112},{112,64},{1... | collective-permute-start | bytes 1179656 | tf_op jit(solution)/shard_map/tokens_x/ppermute | solution.py:246
  19.7 20.3 %collective-permute-start.1 = (bf16[2,128,768]{2,1,0:T(8,128)(2,1)}, bf16[2,128,768]{2,1,0:T(8,128)(2,1)S(1)}, u32[]{:S(2)}, u32[]{:S(2)}) collective-permute-start(bf16[2,128,768]{2,1,0:T(8,128)(2,1)} %get-tuple-element.13), channel_id=1, source_target_pairs={{0,32},{16,48},{32,0},{48,16},{64,96},{80,112},{96,64},{112,80},{1... | collective-permute-start | bytes 1179656 | tf_op jit(solution)/shard_map/tokens_x/ppermute | solution.py:246
  24.1 17.1 %collective-permute-start.2 = (bf16[2,128,768]{2,1,0:T(8,128)(2,1)}, bf16[2,128,768]{2,1,0:T(8,128)(2,1)S(1)}, u32[]{:S(2)}, u32[]{:S(2)}) collective-permute-start(bf16[2,128,768]{2,1,0:T(8,128)(2,1)} %get-tuple-element.14), channel_id=1, source_target_pairs={{0,48},{16,0},{32,16},{48,32},{64,112},{80,64},{96,80},{112,96},{1... | collective-permute-start | bytes 1179656 | tf_op jit(solution)/shard_map/tokens_x/ppermute | solution.py:246
  29.9 11.4 %copy-start = (bf16[2,128,768]{2,1,0:T(8,128)(2,1)S(1)}, bf16[2,128,768]{2,1,0:T(8,128)(2,1)}, u32[]{:S(2)}) copy-start(bf16[2,128,768]{2,1,0:T(8,128)(2,1)} %get-tuple-element.11.t0) | copy-start | bytes 1179652
  29.9 31.9 %all-to-all-start.1 = ((bf16[32,16,768]{2,1,0:T(8,128)(2,1)}), bf16[32,16,768]{2,1,0:T(8,128)(2,1)S(1)}, u32[]{:S(2)}, u32[]{:S(2)}) async-start(bf16[32,16,768]{2,1,0:T(8,128)(2,1)} %renew.1), calls=%async_computation.1 | async-start | bytes 1572864 | tf_op jit(solution)/shard_map/window/all_to_all | solution.py:253
  41.3 5.0 %collective-permute-start.3 = (bf16[4,128,768]{2,1,0:T(8,128)(2,1)S(1)}, bf16[4,128,768]{2,1,0:T(8,128)(2,1)S(1)}, u32[]{:S(2)}, u32[]{:S(2)}) collective-permute-start(bf16[4,128,768]{2,1,0:T(8,128)(2,1)S(1)} %tokens_core.1), channel_id=1, source_target_pairs={{0,1},{1,0},{2,3},{3,2},{4,5},{5,4},{6,7},{7,6},{8,9},{9,8},{10,11... | collective-permute-start | bytes 2359304 | tf_op jit(solution)/shard_map/tokens_core/ppermute | solution.py:251
  62.8 4.5 %collective-permute-start.4 = (bf16[4,128,512]{2,1,0:T(8,128)(2,1)S(1)}, bf16[4,128,512]{2,1,0:T(8,128)(2,1)S(1)}, u32[]{:S(2)}, u32[]{:S(2)}) collective-permute-start(bf16[4,128,512]{2,1,0:T(8,128)(2,1)S(1)} %get-tuple-element.18), channel_id=1, source_target_pairs={{0,1},{1,0},{2,3},{3,2},{4,5},{5,4},{6,7},{7,6},{8,9},{9,8},{10,11... | collective-permute-start | bytes 1572872 | tf_op jit(solution)/shard_map/sum_core/ppermute | solution.py:265
  68.2 13.1 %all-to-all-start.2 = ((bf16[4,128,512]{2,1,0:T(8,128)(2,1)}), bf16[4,128,512]{2,1,0:T(8,128)(2,1)S(1)}, u32[]{:S(2)}, u32[]{:S(2)}) async-start(bf16[4,128,512]{2,1,0:T(8,128)(2,1)} %sum_core.1), calls=%async_computation.2 | async-start | bytes 1048576 | tf_op jit(solution)/shard_map/sum_x/all_to_all | solution.py:269

commit v3 on v2

--- a/solution.py
+++ b/solution.py
@@ -36,10 +36,9 @@
     return lax.dot_general(a, b, (((da,), (db,)), ((), ())), precision=HIGH, preferred_element_type=F32)
 
 
-def swap_kernel(t0, t1, t2, t3, away):
-    core = lax.axis_index("replica") % 2
-    for d, tokens in enumerate((t0, t1, t2, t3)):
-        away[d] = tokens[1 - core]
+def forward_kernel(ahead, behind, far0, far1):
+    far0[0] = ahead[2]
+    far1[0] = behind[2]
 
 
 def lay_out(indices, lanes):
@@ -85,17 +84,22 @@
 
 
 def send_kernel(
-    tokens, momentum, gradient, indices, table, send, c0, c1, c2, c3, cut, mom, grad, ind, tab, sems
+    tokens, momentum, gradient, indices, table, send, own, ahead, behind, cut, mom, grad, ind, tab, sems
 ):
     x = lax.axis_index("shard") % XS
     piece = cut.shape[2]
     loads = fetch([(momentum, mom), (gradient, grad), (indices, ind), (table, tab)], sems)
     pieces, first = [], len(loads)
-    for d in range(XS):
-        for h in range(2):
-            at = pl.multiple_of((h * XS + (x + d) % XS) * piece, 128)
-            pieces.append((tokens.at[:, pl.ds(at, piece)], cut.at[2 * d + h]))
+    for i, (d, h) in enumerate([(0, 0), (0, 1), (1, 0), (1, 1), (2, 0), (3, 0), (3, 1), (2, 1)]):
+        at = pl.multiple_of((h * XS + (x + d) % XS) * piece, 128)
+        pieces.append((tokens.at[:, pl.ds(at, piece)], cut.at[i]))
     cuts = fetch(pieces, sems.at[pl.ds(first, MEMBERS)])
+    for c in cuts:
+        c.wait()
+    outs = fetch(
+        [(cut.at[pl.ds(0, 2)], own), (cut.at[pl.ds(2, 3)], ahead), (cut.at[pl.ds(5, 3)], behind)],
+        sems.at[pl.ds(first + MEMBERS, 3)],
+    )
     for load in loads:
         load.wait()
     _, index, picked = choose(mom[0], grad[0], ind, tab[...])
@@ -104,11 +108,6 @@
     half = message.shape[1] // 2
     for r in range(send.shape[0]):
         send[r] = message[:, r % 2 * half : (r % 2 + 1) * half]
-    for c in cuts:
-        c.wait()
-    outs = fetch(
-        [(cut.at[pl.ds(2 * d, 2)], c) for d, c in enumerate((c0, c1, c2, c3))], sems.at[pl.ds(first + MEMBERS, XS)]
-    )
     for out in outs:
         out.wait()
 
@@ -138,11 +137,10 @@
         for r in range(replicas):
             message = received[r, :, at].astype(F32)
             for side in range(2):
-                for j in range(TOPK):
-                    row = side * TOPK + j
-                    sums[side] = sums[side] + jnp.where(
-                        freq == message[8 + row][None, :], message[row][None, :], 0.0
-                    )
+                dense = jnp.zeros((GROUP, 128), F32)
+                for row in range(side * TOPK, (side + 1) * TOPK):
+                    dense = jnp.where(freq == message[2 * TOPK + row][None, :], message[row][None, :], dense)
+                sums[side] = sums[side] + dense
         columns.append(jnp.concatenate(sums, axis=0))
     field = contract(jnp.concatenate(columns, axis=1), table[...], 0, 0)
     old = weight[:, pl.ds(pl.multiple_of(core * half, 128), half)].astype(F32)
@@ -156,20 +154,26 @@
                 renewed[y * XS + x, :, p * PAIR : (p + 1) * PAIR] = new
 
 
-def product_kernel(t0, t1, t2, t3, came, window, mine, other):
-    core = lax.axis_index("replica") % 2
-    count = came.shape[1]
-    for d, tokens in enumerate((t0, t1, t2, t3)):
-        block = jnp.concatenate([came[d], tokens[core]], axis=0)
-        product = lax.dot_general(block, window[...], (((1,), (1,)), ((), ())), preferred_element_type=F32)
-        other[d] = product[:count].astype(BF16)
-        mine[d] = product[count:]
-
-
-def order_kernel(mine, arrived, out):
+def stack(own, ahead, far0, far1, behind, h):
+    return jnp.concatenate([own[h], ahead[h], jnp.where(h == 0, far0[0], far1[0]), behind[h]], axis=0)
+
+
+def product(tokens, window):
+    return lax.dot_general(tokens, window[...], (((1,), (1,)), ((), ())), preferred_element_type=F32)
+
+
+def first_kernel(*refs):
+    *blocks, window, out = refs
+    out[...] = product(stack(*blocks, lax.axis_index("replica") % 2), window)
+
+
+def second_kernel(*refs):
+    *blocks, window, first, out = refs
     x = lax.axis_index("shard") % XS
+    count = out.shape[1]
+    total = first[...] + product(stack(*blocks, 1 - lax.axis_index("replica") % 2), window)
     for d in range(XS):
-        out[(x + XS - d) % XS] = (mine[d] + arrived[d].astype(F32)).astype(BF16)
+        out[(x + XS - d) % XS] = total[d * count : (d + 1) * count].astype(BF16)
 
 
 def finish_kernel(parts, out):
@@ -211,15 +215,15 @@
     hbm, vmem = pl.BlockSpec(memory_space=pltpu.HBM), pl.BlockSpec(memory_space=pltpu.VMEM)
     params = pltpu.CompilerParams(vmem_limit_bytes=VMEM_BYTES)
     with jax.named_scope("coefficients"):
-        send, *cut = pl.pallas_call(
+        send, own, ahead, behind = pl.pallas_call(
             send_kernel,
             out_shape=[jax.ShapeDtypeStruct((replicas, 4 * TOPK, lanes // 2), BF16)]
-            + [jax.ShapeDtypeStruct((2, count, piece), BF16)] * XS,
+            + [jax.ShapeDtypeStruct((n, count, piece), BF16) for n in (2, 3, 3)],
             in_specs=[hbm] * 5,
-            out_specs=[vmem] + [hbm] * XS,
+            out_specs=[vmem] + [hbm] * 3,
             scratch_shapes=[pltpu.VMEM((MEMBERS, count, piece), BF16)]
             + local_scratch
-            + [pltpu.SemaphoreType.DMA((4 + MEMBERS + XS,))],
+            + [pltpu.SemaphoreType.DMA((4 + MEMBERS + 3,))],
             compiler_params=params,
             cost_estimate=pl.CostEstimate(flops=10**8, bytes_accessed=4 * 10**6, transcendentals=0),
         )(tokens, momentum, gradient, ordered_indices, table)
@@ -230,6 +234,17 @@
         renewed = call(
             renew_kernel, jax.ShapeDtypeStruct((shards, rows, piece), BF16), received, weight, table, flops=10**10
         )
+    with jax.named_scope("tokens_x"):
+        on, back = (
+            [(s, s // XS * XS + (s + step) % XS) for s in range(shards)] for step in (1, XS - 1)
+        )
+        ahead = lax.ppermute(ahead, "shard", on)
+        behind = lax.ppermute(behind, "shard", back)
+        one = jax.ShapeDtypeStruct((1, count, piece), BF16)
+        far0, far1 = call(forward_kernel, [one, one], ahead, behind, flops=5 * 10**10)
+        far0 = lax.ppermute(far0, "shard", on)
+        far1 = lax.ppermute(far1, "shard", back)
+        blocks = (own, ahead, far0, far1, behind)
     with jax.named_scope("momentum"):
         momentum, renewed = lax.optimization_barrier((momentum, renewed))
         new_momentum = pl.pallas_call(
@@ -241,29 +256,17 @@
             compiler_params=params,
             cost_estimate=pl.CostEstimate(flops=5 * 10**10, bytes_accessed=10**6, transcendentals=0),
         )(momentum, gradient, ordered_indices, table)
-    with jax.named_scope("tokens_x"):
-        blocks = [cut[0]] + [
-            lax.ppermute(cut[d], "shard", [(s, s // XS * XS + (s + d) % XS) for s in range(shards)])
-            for d in range(1, XS)
-        ]
-    with jax.named_scope("tokens_core"):
-        away = call(swap_kernel, jax.ShapeDtypeStruct((XS, count, piece), BF16), *blocks, flops=5 * 10**10)
-        came = lax.ppermute(away, "replica", [(i, i ^ 1) for i in range(replicas)])
     with jax.named_scope("window"):
         window = lax.all_to_all(renewed, "shard", 0, 0).reshape(shards * rows, piece)
+    with jax.named_scope("window_core"):
+        window, *blocks = lax.optimization_barrier((window, *blocks))
+        other = lax.ppermute(window, "replica", [(i, i ^ 1) for i in range(replicas)])
     with jax.named_scope("product"):
-        shape = (XS, count, shards * rows)
-        mine, other = call(
-            product_kernel,
-            (jax.ShapeDtypeStruct(shape, F32), jax.ShapeDtypeStruct(shape, BF16)),
-            *blocks,
-            came,
-            window,
-            flops=2 * 1024 * 768 * 512,
-        )
-    with jax.named_scope("sum_core"):
-        arrived = lax.ppermute(other, "replica", [(i, i ^ 1) for i in range(replicas)])
-        ordered = call(order_kernel, jax.ShapeDtypeStruct(shape, BF16), mine, arrived)
+        size = shards * rows
+        work = 2 * XS * count * size * piece
+        first = call(first_kernel, jax.ShapeDtypeStruct((XS * count, size), F32), *blocks, window, flops=work)
+        shape = (XS, count, size)
+        ordered = call(second_kernel, jax.ShapeDtypeStruct(shape, BF16), *blocks, other, first, flops=work)
     with jax.named_scope("sum_x"):
         groups = [[y * XS + i for i in range(XS)] for y in range(YS)]
         parts = lax.all_to_all(ordered, "shard", 0, 0, axis_index_groups=groups)

time: 82.5 us -> 81.6 us (0.989)
    all_to_all x1, waiting for transfers between devices: 15.5 us -> 8.44 us  [local(): lax.all_to_all(renewed, 'shard', 0, 0).reshape(shards * rows, piece)]
    all_to_all x1, waiting for transfers between devices: 0.01 us -> 3.8 us  [local(): received = lax.all_to_all(send, 'replica', 0, 0)]
    ppermute x5, waiting for transfers between devices: 5.22 us -> 8.54 us  [the longest x1 7.01 us: local(): far0 = lax.ppermute(far0, 'shard', on)]
  transfers between devices with their start and end apart: 8 -> 8, of which waited for: 6 -> 6; matrix products, arithmetic and copies ran while one was open for 0% -> 0% of each run, Pallas kernels for 7% -> 8%
where the time goes in v3:
time: 81.6 us; the launch traced here: 81.1 us
  starting transfers between devices  41.8 us (51%)
  waiting for transfers between devices  26.5 us (32%)
  Pallas kernels  11.9 us (15%)
    all_to_all x1, starting transfers between devices, local(): received = lax.all_to_all(send, 'replica', 0, 0)  11.8 us
    all_to_all x1, starting transfers between devices, local(): lax.all_to_all(renewed, 'shard', 0, 0).reshape(shards * rows, piece)  9.67 us
    all_to_all x1, waiting for transfers between devices, local(): lax.all_to_all(renewed, 'shard', 0, 0).reshape(shards * rows, piece)  8.44 us
    ppermute x1, waiting for transfers between devices, local(): far0 = lax.ppermute(far0, 'shard', on)  7.01 us
    all_to_all x1, waiting for transfers between devices, local(): parts = lax.all_to_all(ordered, 'shard', 0, 0, axis_index_groups=groups)  5.78 us
    pallas_call x5, Pallas kernels, call(): pl.pallas_call(kernel, out_shape=out, in_specs=[pl.BlockSpec(memory_space...  5.12 us
    all_to_all x1, starting transfers between devices, local(): parts = lax.all_to_all(ordered, 'shard', 0, 0, axis_index_groups=groups)  4.22 us
    all_to_all x1, waiting for transfers between devices, local(): received = lax.all_to_all(send, 'replica', 0, 0)  3.8 us
  transfers between devices with their start and end apart: 8, of which 6 were waited for; matrix products, arithmetic and copies ran while one was open for 0% of the time, Pallas kernels for 8%

profile of v3, /device:TPU:1, one launch (start us, length us, event | category | flops | bytes accessed | tf_op | source)
XLA Modules:
  0.0 81.1 jit_solution(6754785463178699419)
XLA Ops:
  0.6 0.0 copy-start.1
  0.7 3.7 %coefficients.1 = (bf16[16,16,384]{2,1,0:T(8,128)(2,1)}, bf16[2,128,768]{2,1,0:T(8,128)(2,1)}, bf16[3,128,768]{2,1,0:T(8,128)(2,1)}, bf16[3,128,768]{2,1,0:T(8,128)(2,1)}) custom-call(bf16[128,6144]{1,0:T(8,128)(2,1)} %tokens.1, f32[1,16,6144]{2,1,0:T(8,128)} %momentum.4, bf16[1,16,6144]{2,1,0:T(8,128)(2,1)} %gradient.3, s32[16,4,96]{2,1,0:T(4,128)} %bitcast.6, ...), custom_call_target="tpu_custom_call" | custom-call | flops 100000000 | bytes 4000000 | tf_op jit(solution)/shard_map/coefficients/pallas_call | solution.py:218
  4.3 11.8 %all-to-all-start = ((bf16[16,16,384]{2,1,0:T(8,128)(2,1)}), bf16[16,16,384]{2,1,0:T(8,128)(2,1)S(1)}, u32[]{:S(2)}, u32[]{:S(2)}) async-start(bf16[16,16,384]{2,1,0:T(8,128)(2,1)} %get-tuple-element.16), calls=%async_computation | async-start | bytes 393216 | tf_op jit(solution)/shard_map/exchange/all_to_all | solution.py:232
  16.2 3.1 %collective-permute-start = (bf16[3,128,768]{2,1,0:T(8,128)(2,1)}, bf16[3,128,768]{2,1,0:T(8,128)(2,1)S(1)}, u32[]{:S(2)}, u32[]{:S(2)}) collective-permute-start(bf16[3,128,768]{2,1,0:T(8,128)(2,1)} %get-tuple-element.19), channel_id=1, source_target_pairs={{0,16},{16,32},{32,48},{48,0},{64,80},{80,96},{96,112},{112,64},{1... | collective-permute-start | bytes 1769480 | tf_op jit(solution)/shard_map/tokens_x/ppermute | solution.py:241
  19.3 3.4 %collective-permute-start.1 = (bf16[3,128,768]{2,1,0:T(8,128)(2,1)}, bf16[3,128,768]{2,1,0:T(8,128)(2,1)S(1)}, u32[]{:S(2)}, u32[]{:S(2)}) collective-permute-start(bf16[3,128,768]{2,1,0:T(8,128)(2,1)} %get-tuple-element.20), channel_id=1, source_target_pairs={{0,48},{16,0},{32,16},{48,32},{64,112},{80,64},{96,80},{112,96},{1... | collective-permute-start | bytes 1769480 | tf_op jit(solution)/shard_map/tokens_x/ppermute | solution.py:242
  22.7 3.8 %all-to-all-done.received = bf16[16,16,384]{2,1,0:T(8,128)(2,1)S(1)} async-done(((bf16[16,16,384]{2,1,0:T(8,128)(2,1)}), bf16[16,16,384]{2,1,0:T(8,128)(2,1)S(1)}, u32[]{:S(2)}, u32[]{:S(2)}) %all-to-all-start) | async-done | bytes 196640 | tf_op jit(solution)/shard_map/exchange/all_to_all | solution.py:232
  26.5 2.4 %renew.1 = bf16[32,16,768]{2,1,0:T(8,128)(2,1)} custom-call(bf16[16,16,384]{2,1,0:T(8,128)(2,1)S(1)} %all-to-all-done.received, bf16[16,6144]{1,0:T(8,128)(2,1)S(1)} %copy-done.2, f32[128,128]{1,0:T(8,128)S(1)} %copy-done.1), custom_call_target="tpu_custom_call" | custom-call | flops 10000000000 | bytes 1245184 | tf_op jit(solution)/shard_map/renew/pallas_call | solution.py:189
  28.9 9.7 %all-to-all-start.1 = ((bf16[32,16,768]{2,1,0:T(8,128)(2,1)}), bf16[32,16,768]{2,1,0:T(8,128)(2,1)S(1)}, u32[]{:S(2)}, u32[]{:S(2)}) async-start(bf16[32,16,768]{2,1,0:T(8,128)(2,1)} %renew.1), calls=%async_computation.1 | async-start | bytes 1572864 | tf_op jit(solution)/shard_map/window/all_to_all | solution.py:260
  38.5 0.0 copy-start
  38.6 0.0 collective-permute-done.ahead.refs_1_
  38.6 0.0 collective-permute-done.1.behind.refs_4_
  38.6 3.3 %collective-permute-start.2 = (bf16[1,128,768]{2,1,0:T(8,128)(2,1)S(1)}, bf16[1,128,768]{2,1,0:T(8,128)(2,1)S(1)}, u32[]{:S(2)}, u32[]{:S(2)}) collective-permute-start(bf16[1,128,768]{2,1,0:T(8,128)(2,1)S(1)} %get-tuple-element.21), channel_id=1, source_target_pairs={{0,16},{16,32},{32,48},{48,0},{64,80},{80,96},{96,112},{112,64},{1... | collective-permute-start | bytes 589832 | tf_op jit(solution)/shard_map/tokens_x/ppermute | solution.py:245
  41.9 3.4 %collective-permute-start.3 = (bf16[1,128,768]{2,1,0:T(8,128)(2,1)S(1)}, bf16[1,128,768]{2,1,0:T(8,128)(2,1)S(1)}, u32[]{:S(2)}, u32[]{:S(2)}) collective-permute-start(bf16[1,128,768]{2,1,0:T(8,128)(2,1)S(1)} %get-tuple-element.22), channel_id=1, source_target_pairs={{0,48},{16,0},{32,16},{48,32},{64,112},{80,64},{96,80},{112,96},{1... | collective-permute-start | bytes 589832 | tf_op jit(solution)/shard_map/tokens_x/ppermute | solution.py:246
  45.3 7.0 %collective-permute-done.2.refs_2_ = bf16[1,128,768]{2,1,0:T(8,128)(2,1)S(1)} collective-permute-done((bf16[1,128,768]{2,1,0:T(8,128)(2,1)S(1)}, bf16[1,128,768]{2,1,0:T(8,128)(2,1)S(1)}, u32[]{:S(2)}, u32[]{:S(2)}) %collective-permute-start.2) | collective-permute-done | bytes 196640 | tf_op jit(solution)/shard_map/tokens_x/ppermute | solution.py:245
  52.3 0.2 collective-permute-done.3.refs_3_
  52.5 8.4 %all-to-all-done.1 = bf16[32,16,768]{2,1,0:T(8,128)(2,1)S(1)} async-done(((bf16[32,16,768]{2,1,0:T(8,128)(2,1)}), bf16[32,16,768]{2,1,0:T(8,128)(2,1)S(1)}, u32[]{:S(2)}, u32[]{:S(2)}) %all-to-all-start.1) | async-done | bytes 786464 | tf_op jit(solution)/shard_map/window/all_to_all | solution.py:260
  60.9 3.0 %collective-permute-start.4 = (bf16[512,768]{1,0:T(8,128)(2,1)S(1)}, bf16[512,768]{1,0:T(8,128)(2,1)S(1)}, u32[]{:S(2)}, u32[]{:S(2)}) collective-permute-start(bf16[512,768]{1,0:T(8,128)(2,1)S(1)} %bitcast.4), channel_id=1, source_target_pairs={{0,1},{1,0},{2,3},{3,2},{4,5},{5,4},{6,7},{7,6},{8,9},{9,8},{10,11... | collective-permute-start | bytes 2359304 | tf_op jit(solution)/shard_map/window_core/ppermute | solution.py:263
  63.9 0.6 product.2.refs_6_
  64.5 1.3 %collective-permute-done.4.refs_5_ = bf16[512,768]{1,0:T(8,128)(2,1)S(1)} collective-permute-done((bf16[512,768]{1,0:T(8,128)(2,1)S(1)}, bf16[512,768]{1,0:T(8,128)(2,1)S(1)}, u32[]{:S(2)}, u32[]{:S(2)}) %collective-permute-start.4) | collective-permute-done | bytes 786464 | tf_op jit(solution)/shard_map/window_core/ppermute | solution.py:263
  65.8 1.4 %product.3 = bf16[4,128,512]{2,1,0:T(8,128)(2,1)} custom-call(bf16[2,128,768]{2,1,0:T(8,128)(2,1)S(1)} %copy-done, bf16[3,128,768]{2,1,0:T(8,128)(2,1)S(1)} %collective-permute-done.ahead.refs_1_, bf16[1,128,768]{2,1,0:T(8,128)(2,1)S(1)} %collective-permute-done.2.refs_2_, bf16[1,128,768]{2,1,0:T(8,128)(2,1)S(1)} %collective-permute-done.3.refs_3_, ...), custom_call_target="tpu_custom_call" | custom-call | flops 402653184 | bytes 4325376 | tf_op jit(solution)/shard_map/product/pallas_call | solution.py:189
  67.2 4.2 %all-to-all-start.2 = ((bf16[4,128,512]{2,1,0:T(8,128)(2,1)}), bf16[4,128,512]{2,1,0:T(8,128)(2,1)S(1)}, u32[]{:S(2)}, u32[]{:S(2)}) async-start(bf16[4,128,512]{2,1,0:T(8,128)(2,1)} %product.3), calls=%async_computation.2 | async-start | bytes 1048576 | tf_op jit(solution)/shard_map/sum_x/all_to_all | solution.py:272
  71.4 3.1 %momentum.3 = f32[1,16,6144]{2,1,0:T(8,128)} custom-call(f32[1,16,6144]{2,1,0:T(8,128)} %momentum.4, bf16[1,16,6144]{2,1,0:T(8,128)(2,1)} %gradient.3, s32[16,4,96]{2,1,0:T(4,128)} %bitcast.7, f32[128,128]{1,0:T(8,128)} %constant.2.clone.table), custom_call_target="tpu_custom_call" | custom-call | flops 49999998976 | bytes 1000000 | tf_op jit(solution)/shard_map/momentum/pallas_call | solution.py:250
  74.6 5.8 %all-to-all-done.2.parts = bf16[4,128,512]{2,1,0:T(8,128)(2,1)S(1)} async-done(((bf16[4,128,512]{2,1,0:T(8,128)(2,1)}), bf16[4,128,512]{2,1,0:T(8,128)(2,1)S(1)}, u32[]{:S(2)}, u32[]{:S(2)}) %all-to-all-start.2) | async-done | bytes 524320 | tf_op jit(solution)/shard_map/sum_x/all_to_all | solution.py:272
  80.3 0.7 sum_x.1
  (5 shorter events, 0.0 us)
Async XLA Ops:
  0.6 25.9 %copy-start.1 = (f32[128,128]{1,0:T(8,128)S(1)}, f32[128,128]{1,0:T(8,128)}, u32[]{:S(2)}) copy-start(f32[128,128]{1,0:T(8,128)} %constant.2.clone.table) | copy-start | bytes 196612
  0.6 25.8 %copy-start.2 = (bf16[16,6144]{1,0:T(8,128)(2,1)S(1)}, bf16[16,6144]{1,0:T(8,128)(2,1)}, u32[]{:S(2)}) copy-start(bf16[16,6144]{1,0:T(8,128)(2,1)} %weight.1) | copy-start | bytes 589828
  4.3 22.2 %all-to-all-start = ((bf16[16,16,384]{2,1,0:T(8,128)(2,1)}), bf16[16,16,384]{2,1,0:T(8,128)(2,1)S(1)}, u32[]{:S(2)}, u32[]{:S(2)}) async-start(bf16[16,16,384]{2,1,0:T(8,128)(2,1)} %get-tuple-element.16), calls=%async_computation | async-start | bytes 393216 | tf_op jit(solution)/shard_map/exchange/all_to_all | solution.py:232
  16.2 22.4 %collective-permute-start = (bf16[3,128,768]{2,1,0:T(8,128)(2,1)}, bf16[3,128,768]{2,1,0:T(8,128)(2,1)S(1)}, u32[]{:S(2)}, u32[]{:S(2)}) collective-permute-start(bf16[3,128,768]{2,1,0:T(8,128)(2,1)} %get-tuple-element.19), channel_id=1, source_target_pairs={{0,16},{16,32},{32,48},{48,0},{64,80},{80,96},{96,112},{112,64},{1... | collective-permute-start | bytes 1769480 | tf_op jit(solution)/shard_map/tokens_x/ppermute | solution.py:241
  19.3 19.3 %collective-permute-start.1 = (bf16[3,128,768]{2,1,0:T(8,128)(2,1)}, bf16[3,128,768]{2,1,0:T(8,128)(2,1)S(1)}, u32[]{:S(2)}, u32[]{:S(2)}) collective-permute-start(bf16[3,128,768]{2,1,0:T(8,128)(2,1)} %get-tuple-element.20), channel_id=1, source_target_pairs={{0,48},{16,0},{32,16},{48,32},{64,112},{80,64},{96,80},{112,96},{1... | collective-permute-start | bytes 1769480 | tf_op jit(solution)/shard_map/tokens_x/ppermute | solution.py:242
  28.9 32.1 %all-to-all-start.1 = ((bf16[32,16,768]{2,1,0:T(8,128)(2,1)}), bf16[32,16,768]{2,1,0:T(8,128)(2,1)S(1)}, u32[]{:S(2)}, u32[]{:S(2)}) async-start(bf16[32,16,768]{2,1,0:T(8,128)(2,1)} %renew.1), calls=%async_computation.1 | async-start | bytes 1572864 | tf_op jit(solution)/shard_map/window/all_to_all | solution.py:260
  38.5 25.4 %copy-start = (bf16[2,128,768]{2,1,0:T(8,128)(2,1)S(1)}, bf16[2,128,768]{2,1,0:T(8,128)(2,1)}, u32[]{:S(2)}) copy-start(bf16[2,128,768]{2,1,0:T(8,128)(2,1)} %get-tuple-element.23.refs_0_) | copy-start | bytes 1179652
  38.6 13.7 %collective-permute-start.2 = (bf16[1,128,768]{2,1,0:T(8,128)(2,1)S(1)}, bf16[1,128,768]{2,1,0:T(8,128)(2,1)S(1)}, u32[]{:S(2)}, u32[]{:S(2)}) collective-permute-start(bf16[1,128,768]{2,1,0:T(8,128)(2,1)S(1)} %get-tuple-element.21), channel_id=1, source_target_pairs={{0,16},{16,32},{32,48},{48,0},{64,80},{80,96},{96,112},{112,64},{1... | collective-permute-start | bytes 589832 | tf_op jit(solution)/shard_map/tokens_x/ppermute | solution.py:245
  41.9 10.6 %collective-permute-start.3 = (bf16[1,128,768]{2,1,0:T(8,128)(2,1)S(1)}, bf16[1,128,768]{2,1,0:T(8,128)(2,1)S(1)}, u32[]{:S(2)}, u32[]{:S(2)}) collective-permute-start(bf16[1,128,768]{2,1,0:T(8,128)(2,1)S(1)} %get-tuple-element.22), channel_id=1, source_target_pairs={{0,48},{16,0},{32,16},{48,32},{64,112},{80,64},{96,80},{112,96},{1... | collective-permute-start | bytes 589832 | tf_op jit(solution)/shard_map/tokens_x/ppermute | solution.py:246
  60.9 4.9 %collective-permute-start.4 = (bf16[512,768]{1,0:T(8,128)(2,1)S(1)}, bf16[512,768]{1,0:T(8,128)(2,1)S(1)}, u32[]{:S(2)}, u32[]{:S(2)}) collective-permute-start(bf16[512,768]{1,0:T(8,128)(2,1)S(1)} %bitcast.4), channel_id=1, source_target_pairs={{0,1},{1,0},{2,3},{3,2},{4,5},{5,4},{6,7},{7,6},{8,9},{9,8},{10,11... | collective-permute-start | bytes 2359304 | tf_op jit(solution)/shard_map/window_core/ppermute | solution.py:263
  67.2 13.1 %all-to-all-start.2 = ((bf16[4,128,512]{2,1,0:T(8,128)(2,1)}), bf16[4,128,512]{2,1,0:T(8,128)(2,1)S(1)}, u32[]{:S(2)}, u32[]{:S(2)}) async-start(bf16[4,128,512]{2,1,0:T(8,128)(2,1)} %product.3), calls=%async_computation.2 | async-start | bytes 1048576 | tf_op jit(solution)/shard_map/sum_x/all_to_all | solution.py:272

commit v4 on v3

--- a/solution.py
+++ b/solution.py
@@ -83,24 +83,8 @@
     return copies
 
 
-def send_kernel(
-    tokens, momentum, gradient, indices, table, send, own, ahead, behind, cut, mom, grad, ind, tab, sems
-):
-    x = lax.axis_index("shard") % XS
-    piece = cut.shape[2]
-    loads = fetch([(momentum, mom), (gradient, grad), (indices, ind), (table, tab)], sems)
-    pieces, first = [], len(loads)
-    for i, (d, h) in enumerate([(0, 0), (0, 1), (1, 0), (1, 1), (2, 0), (3, 0), (3, 1), (2, 1)]):
-        at = pl.multiple_of((h * XS + (x + d) % XS) * piece, 128)
-        pieces.append((tokens.at[:, pl.ds(at, piece)], cut.at[i]))
-    cuts = fetch(pieces, sems.at[pl.ds(first, MEMBERS)])
-    for c in cuts:
-        c.wait()
-    outs = fetch(
-        [(cut.at[pl.ds(0, 2)], own), (cut.at[pl.ds(2, 3)], ahead), (cut.at[pl.ds(5, 3)], behind)],
-        sems.at[pl.ds(first + MEMBERS, 3)],
-    )
-    for load in loads:
+def send_kernel(momentum, gradient, indices, table, send, mom, grad, ind, tab, sems):
+    for load in fetch([(momentum, mom), (gradient, grad), (indices, ind), (table, tab)], sems):
         load.wait()
     _, index, picked = choose(mom[0], grad[0], ind, tab[...])
     values = [jnp.sum(p, axis=0, keepdims=True) for p in picked]
@@ -108,6 +92,21 @@
     half = message.shape[1] // 2
     for r in range(send.shape[0]):
         send[r] = message[:, r % 2 * half : (r % 2 + 1) * half]
+
+
+def cut_kernel(tokens, own, ahead, behind, cut, sems):
+    x = lax.axis_index("shard") % XS
+    piece = cut.shape[2]
+    pieces = []
+    for i, (d, h) in enumerate([(1, 0), (1, 1), (2, 0), (3, 0), (3, 1), (2, 1), (0, 0), (0, 1)]):
+        at = pl.multiple_of((h * XS + (x + d) % XS) * piece, 128)
+        pieces.append((tokens.at[:, pl.ds(at, piece)], cut.at[i]))
+    cuts = fetch(pieces, sems)
+    outs = []
+    for i, (first, number, out) in enumerate([(0, 3, ahead), (3, 3, behind), (6, 2, own)]):
+        for c in cuts[first : first + number]:
+            c.wait()
+        outs += fetch([(cut.at[pl.ds(first, number)], out)], sems.at[pl.ds(MEMBERS + i, 1)])
     for out in outs:
         out.wait()
 
@@ -163,15 +162,16 @@
 
 
 def first_kernel(*refs):
-    *blocks, window, out = refs
-    out[...] = product(stack(*blocks, lax.axis_index("replica") % 2), window)
-
-
-def second_kernel(*refs):
-    *blocks, window, first, out = refs
+    *blocks, window, out, rest = refs
+    core = lax.axis_index("replica") % 2
+    out[...] = product(stack(*blocks, core), window)
+    rest[...] = stack(*blocks, 1 - core)
+
+
+def second_kernel(rest, window, first, out):
     x = lax.axis_index("shard") % XS
     count = out.shape[1]
-    total = first[...] + product(stack(*blocks, 1 - lax.axis_index("replica") % 2), window)
+    total = first[...] + product(rest[...], window)
     for d in range(XS):
         out[(x + XS - d) % XS] = total[d * count : (d + 1) * count].astype(BF16)
 
@@ -215,18 +215,26 @@
     hbm, vmem = pl.BlockSpec(memory_space=pltpu.HBM), pl.BlockSpec(memory_space=pltpu.VMEM)
     params = pltpu.CompilerParams(vmem_limit_bytes=VMEM_BYTES)
     with jax.named_scope("coefficients"):
-        send, own, ahead, behind = pl.pallas_call(
+        send = pl.pallas_call(
             send_kernel,
-            out_shape=[jax.ShapeDtypeStruct((replicas, 4 * TOPK, lanes // 2), BF16)]
-            + [jax.ShapeDtypeStruct((n, count, piece), BF16) for n in (2, 3, 3)],
-            in_specs=[hbm] * 5,
-            out_specs=[vmem] + [hbm] * 3,
-            scratch_shapes=[pltpu.VMEM((MEMBERS, count, piece), BF16)]
-            + local_scratch
-            + [pltpu.SemaphoreType.DMA((4 + MEMBERS + 3,))],
+            out_shape=jax.ShapeDtypeStruct((replicas, 4 * TOPK, lanes // 2), BF16),
+            in_specs=[hbm] * 4,
+            out_specs=vmem,
+            scratch_shapes=local_scratch + [pltpu.SemaphoreType.DMA((4,))],
             compiler_params=params,
-            cost_estimate=pl.CostEstimate(flops=10**8, bytes_accessed=4 * 10**6, transcendentals=0),
-        )(tokens, momentum, gradient, ordered_indices, table)
+            cost_estimate=pl.CostEstimate(flops=10**8, bytes_accessed=10**6, transcendentals=0),
+        )(momentum, gradient, ordered_indices, table)
+    with jax.named_scope("cut"):
+        tokens, send = lax.optimization_barrier((tokens, send))
+        own, ahead, behind = pl.pallas_call(
+            cut_kernel,
+            out_shape=[jax.ShapeDtypeStruct((n, count, piece), BF16) for n in (2, 3, 3)],
+            in_specs=[hbm],
+            out_specs=[hbm] * 3,
+            scratch_shapes=[pltpu.VMEM((MEMBERS, count, piece), BF16), pltpu.SemaphoreType.DMA((MEMBERS + 3,))],
+            compiler_params=params,
+            cost_estimate=pl.CostEstimate(flops=0, bytes_accessed=4 * tokens.size, transcendentals=0),
+        )(tokens)
 
     with jax.named_scope("exchange"):
         received = lax.all_to_all(send, "replica", 0, 0)
@@ -264,9 +272,18 @@
     with jax.named_scope("product"):
         size = shards * rows
         work = 2 * XS * count * size * piece
-        first = call(first_kernel, jax.ShapeDtypeStruct((XS * count, size), F32), *blocks, window, flops=work)
+        first, rest = call(
+            first_kernel,
+            [
+                jax.ShapeDtypeStruct((XS * count, size), F32),
+                jax.ShapeDtypeStruct((XS * count, piece), BF16),
+            ],
+            *blocks,
+            window,
+            flops=work,
+        )
         shape = (XS, count, size)
-        ordered = call(second_kernel, jax.ShapeDtypeStruct(shape, BF16), *blocks, other, first, flops=work)
+        ordered = call(second_kernel, jax.ShapeDtypeStruct(shape, BF16), rest, other, first, flops=work)
     with jax.named_scope("sum_x"):
         groups = [[y * XS + i for i in range(XS)] for y in range(YS)]
         parts = lax.all_to_all(ordered, "shard", 0, 0, axis_index_groups=groups)

time: 81.6 us -> 80.7 us (0.989)
  waiting for transfers between devices: 26.5 us -> 24.2 us
  Pallas kernels: 11.9 us -> 13.4 us
    all_to_all x1, waiting for transfers between devices: 3.8 us -> 1.43 us  [local(): received = lax.all_to_all(send, 'replica', 0, 0)]
    pallas_call x1 -> x2, Pallas kernels: 3.65 us -> 5.13 us  [the longest x1 2.76 us: local(): pl.pallas_call(send_kernel, out_shape=jax.ShapeDtypeStruct((replicas, 4 *...]
    ppermute x1, waiting for transfers between devices: 7.01 us -> 5.99 us  [local(): far0 = lax.ppermute(far0, 'shard', on)]
  transfers between devices with their start and end apart: 8 -> 8, of which waited for: 6 -> 6; matrix products, arithmetic and copies ran while one was open for 0% -> 0% of each run, Pallas kernels for 8% -> 11%
where the time goes in v4:
time: 80.7 us; the launch traced here: 80.2 us
  starting transfers between devices  41.8 us (52%)
  waiting for transfers between devices  24.2 us (30%)
  Pallas kernels  13.4 us (17%)
    all_to_all x1, starting transfers between devices, local(): received = lax.all_to_all(send, 'replica', 0, 0)  11.8 us
    all_to_all x1, starting transfers between devices, local(): lax.all_to_all(renewed, 'shard', 0, 0).reshape(shards * rows, piece)  9.67 us
    all_to_all x1, waiting for transfers between devices, local(): lax.all_to_all(renewed, 'shard', 0, 0).reshape(shards * rows, piece)  8.99 us
    ppermute x1, waiting for transfers between devices, local(): far0 = lax.ppermute(far0, 'shard', on)  5.99 us
    all_to_all x1, waiting for transfers between devices, local(): parts = lax.all_to_all(ordered, 'shard', 0, 0, axis_index_groups=groups)  5.77 us
    pallas_call x5, Pallas kernels, call(): pl.pallas_call(kernel, out_shape=out, in_specs=[pl.BlockSpec(memory_space...  5.13 us
    all_to_all x1, starting transfers between devices, local(): parts = lax.all_to_all(ordered, 'shard', 0, 0, axis_index_groups=groups)  4.22 us
    ppermute x1, starting transfers between devices, local(): behind = lax.ppermute(behind, 'shard', back)  3.37 us
  transfers between devices with their start and end apart: 8, of which 6 were waited for; matrix products, arithmetic and copies ran while one was open for 0% of the time, Pallas kernels for 11%

profile of v4, /device:TPU:1, one launch (start us, length us, event | category | flops | bytes accessed | tf_op | source)
XLA Modules:
  0.0 80.2 jit_solution(9969310542661523864)
XLA Ops:
  0.6 0.0 copy-start.1
  0.7 2.8 %coefficients.1 = bf16[16,16,384]{2,1,0:T(8,128)(2,1)} custom-call(f32[1,16,6144]{2,1,0:T(8,128)} %momentum.4, bf16[1,16,6144]{2,1,0:T(8,128)(2,1)} %gradient.3, s32[16,4,96]{2,1,0:T(4,128)} %bitcast.6, f32[128,128]{1,0:T(8,128)} %constant.2.clone.table), custom_call_target="tpu_custom_call" | custom-call | flops 100000000 | bytes 1000000 | tf_op jit(solution)/shard_map/coefficients/pallas_call | solution.py:218
  3.4 11.8 %all-to-all-start = ((bf16[16,16,384]{2,1,0:T(8,128)(2,1)}), bf16[16,16,384]{2,1,0:T(8,128)(2,1)S(1)}, u32[]{:S(2)}, u32[]{:S(2)}) async-start(bf16[16,16,384]{2,1,0:T(8,128)(2,1)} %coefficients.1), calls=%async_computation | async-start | bytes 393216 | tf_op jit(solution)/shard_map/exchange/all_to_all | solution.py:240
  15.3 2.4 %cut.1 = (bf16[2,128,768]{2,1,0:T(8,128)(2,1)}, bf16[3,128,768]{2,1,0:T(8,128)(2,1)}, bf16[3,128,768]{2,1,0:T(8,128)(2,1)}) custom-call(bf16[128,6144]{1,0:T(8,128)(2,1)} %tokens), custom_call_target="tpu_custom_call" | custom-call | bytes 3145728 | tf_op jit(solution)/shard_map/cut/pallas_call | solution.py:229
  17.6 3.1 %collective-permute-start = (bf16[3,128,768]{2,1,0:T(8,128)(2,1)}, bf16[3,128,768]{2,1,0:T(8,128)(2,1)S(1)}, u32[]{:S(2)}, u32[]{:S(2)}) collective-permute-start(bf16[3,128,768]{2,1,0:T(8,128)(2,1)} %get-tuple-element.23), channel_id=1, source_target_pairs={{0,16},{16,32},{32,48},{48,0},{64,80},{80,96},{96,112},{112,64},{1... | collective-permute-start | bytes 1769480 | tf_op jit(solution)/shard_map/tokens_x/ppermute | solution.py:249
  20.8 3.4 %collective-permute-start.1 = (bf16[3,128,768]{2,1,0:T(8,128)(2,1)}, bf16[3,128,768]{2,1,0:T(8,128)(2,1)S(1)}, u32[]{:S(2)}, u32[]{:S(2)}) collective-permute-start(bf16[3,128,768]{2,1,0:T(8,128)(2,1)} %get-tuple-element.24), channel_id=1, source_target_pairs={{0,48},{16,0},{32,16},{48,32},{64,112},{80,64},{96,80},{112,96},{1... | collective-permute-start | bytes 1769480 | tf_op jit(solution)/shard_map/tokens_x/ppermute | solution.py:250
  24.2 1.4 %all-to-all-done.received = bf16[16,16,384]{2,1,0:T(8,128)(2,1)S(1)} async-done(((bf16[16,16,384]{2,1,0:T(8,128)(2,1)}), bf16[16,16,384]{2,1,0:T(8,128)(2,1)S(1)}, u32[]{:S(2)}, u32[]{:S(2)}) %all-to-all-start) | async-done | bytes 196640 | tf_op jit(solution)/shard_map/exchange/all_to_all | solution.py:240
  25.6 2.4 %renew.1 = bf16[32,16,768]{2,1,0:T(8,128)(2,1)} custom-call(bf16[16,16,384]{2,1,0:T(8,128)(2,1)S(1)} %all-to-all-done.received, bf16[16,6144]{1,0:T(8,128)(2,1)S(1)} %copy-done.2, f32[128,128]{1,0:T(8,128)S(1)} %copy-done.1), custom_call_target="tpu_custom_call" | custom-call | flops 10000000000 | bytes 1245184 | tf_op jit(solution)/shard_map/renew/pallas_call | solution.py:189
  28.0 9.7 %all-to-all-start.1 = ((bf16[32,16,768]{2,1,0:T(8,128)(2,1)}), bf16[32,16,768]{2,1,0:T(8,128)(2,1)S(1)}, u32[]{:S(2)}, u32[]{:S(2)}) async-start(bf16[32,16,768]{2,1,0:T(8,128)(2,1)} %renew.1), calls=%async_computation.1 | async-start | bytes 1572864 | tf_op jit(solution)/shard_map/window/all_to_all | solution.py:268
  37.6 0.0 copy-start
  37.7 0.0 collective-permute-done.ahead.refs_1_
  37.7 3.3 %collective-permute-start.2 = (bf16[1,128,768]{2,1,0:T(8,128)(2,1)S(1)}, bf16[1,128,768]{2,1,0:T(8,128)(2,1)S(1)}, u32[]{:S(2)}, u32[]{:S(2)}) collective-permute-start(bf16[1,128,768]{2,1,0:T(8,128)(2,1)S(1)} %get-tuple-element.25), channel_id=1, source_target_pairs={{0,16},{16,32},{32,48},{48,0},{64,80},{80,96},{96,112},{112,64},{1... | collective-permute-start | bytes 589832 | tf_op jit(solution)/shard_map/tokens_x/ppermute | solution.py:253
  41.0 3.4 %collective-permute-start.3 = (bf16[1,128,768]{2,1,0:T(8,128)(2,1)S(1)}, bf16[1,128,768]{2,1,0:T(8,128)(2,1)S(1)}, u32[]{:S(2)}, u32[]{:S(2)}) collective-permute-start(bf16[1,128,768]{2,1,0:T(8,128)(2,1)S(1)} %get-tuple-element.26), channel_id=1, source_target_pairs={{0,48},{16,0},{32,16},{48,32},{64,112},{80,64},{96,80},{112,96},{1... | collective-permute-start | bytes 589832 | tf_op jit(solution)/shard_map/tokens_x/ppermute | solution.py:254
  44.4 6.0 %collective-permute-done.2.refs_2_ = bf16[1,128,768]{2,1,0:T(8,128)(2,1)S(1)} collective-permute-done((bf16[1,128,768]{2,1,0:T(8,128)(2,1)S(1)}, bf16[1,128,768]{2,1,0:T(8,128)(2,1)S(1)}, u32[]{:S(2)}, u32[]{:S(2)}) %collective-permute-start.2) | collective-permute-done | bytes 196640 | tf_op jit(solution)/shard_map/tokens_x/ppermute | solution.py:253
  50.3 0.7 collective-permute-done.3.refs_3_
  51.1 9.0 %all-to-all-done.1 = bf16[32,16,768]{2,1,0:T(8,128)(2,1)S(1)} async-done(((bf16[32,16,768]{2,1,0:T(8,128)(2,1)}), bf16[32,16,768]{2,1,0:T(8,128)(2,1)S(1)}, u32[]{:S(2)}, u32[]{:S(2)}) %all-to-all-start.1) | async-done | bytes 786464 | tf_op jit(solution)/shard_map/window/all_to_all | solution.py:268
  60.1 3.0 %collective-permute-start.4 = (bf16[512,768]{1,0:T(8,128)(2,1)S(1)}, bf16[512,768]{1,0:T(8,128)(2,1)S(1)}, u32[]{:S(2)}, u32[]{:S(2)}) collective-permute-start(bf16[512,768]{1,0:T(8,128)(2,1)S(1)} %bitcast.4), channel_id=1, source_target_pairs={{0,1},{1,0},{2,3},{3,2},{4,5},{5,4},{6,7},{7,6},{8,9},{9,8},{10,11... | collective-permute-start | bytes 2359304 | tf_op jit(solution)/shard_map/window_core/ppermute | solution.py:271
  63.0 0.6 product.2
  63.6 1.3 %collective-permute-done.4.window = bf16[512,768]{1,0:T(8,128)(2,1)S(1)} collective-permute-done((bf16[512,768]{1,0:T(8,128)(2,1)S(1)}, bf16[512,768]{1,0:T(8,128)(2,1)S(1)}, u32[]{:S(2)}, u32[]{:S(2)}) %collective-permute-start.4) | collective-permute-done | bytes 786464 | tf_op jit(solution)/shard_map/window_core/ppermute | solution.py:271
  64.9 1.4 %product.3 = bf16[4,128,512]{2,1,0:T(8,128)(2,1)} custom-call(bf16[512,768]{1,0:T(8,128)(2,1)S(1)} %get-tuple-element.33.rest, bf16[512,768]{1,0:T(8,128)(2,1)S(1)} %collective-permute-done.4.window, f32[512,512]{1,0:T(8,128)S(1)} %get-tuple-element.34.first), custom_call_target="tpu_custom_call" | custom-call | flops 402653184 | bytes 3145728 | tf_op jit(solution)/shard_map/product/pallas_call | solution.py:189
  66.3 4.2 %all-to-all-start.2 = ((bf16[4,128,512]{2,1,0:T(8,128)(2,1)}), bf16[4,128,512]{2,1,0:T(8,128)(2,1)S(1)}, u32[]{:S(2)}, u32[]{:S(2)}) async-start(bf16[4,128,512]{2,1,0:T(8,128)(2,1)} %product.3), calls=%async_computation.2 | async-start | bytes 1048576 | tf_op jit(solution)/shard_map/sum_x/all_to_all | solution.py:289
  70.5 3.1 %momentum.3 = f32[1,16,6144]{2,1,0:T(8,128)} custom-call(f32[1,16,6144]{2,1,0:T(8,128)} %momentum.4, bf16[1,16,6144]{2,1,0:T(8,128)(2,1)} %gradient.3, s32[16,4,96]{2,1,0:T(4,128)} %bitcast.7, f32[128,128]{1,0:T(8,128)} %constant.2.clone.table), custom_call_target="tpu_custom_call" | custom-call | flops 49999998976 | bytes 1000000 | tf_op jit(solution)/shard_map/momentum/pallas_call | solution.py:258
  73.7 5.8 %all-to-all-done.2.parts = bf16[4,128,512]{2,1,0:T(8,128)(2,1)S(1)} async-done(((bf16[4,128,512]{2,1,0:T(8,128)(2,1)}), bf16[4,128,512]{2,1,0:T(8,128)(2,1)S(1)}, u32[]{:S(2)}, u32[]{:S(2)}) %all-to-all-start.2) | async-done | bytes 524320 | tf_op jit(solution)/shard_map/sum_x/all_to_all | solution.py:289
  79.4 0.7 sum_x.1
  (6 shorter events, 0.0 us)
Async XLA Ops:
  0.6 25.0 %copy-start.1 = (f32[128,128]{1,0:T(8,128)S(1)}, f32[128,128]{1,0:T(8,128)}, u32[]{:S(2)}) copy-start(f32[128,128]{1,0:T(8,128)} %constant.2.clone.table) | copy-start | bytes 196612
  0.6 25.0 %copy-start.2 = (bf16[16,6144]{1,0:T(8,128)(2,1)S(1)}, bf16[16,6144]{1,0:T(8,128)(2,1)}, u32[]{:S(2)}) copy-start(bf16[16,6144]{1,0:T(8,128)(2,1)} %weight.1) | copy-start | bytes 589828
  3.4 22.2 %all-to-all-start = ((bf16[16,16,384]{2,1,0:T(8,128)(2,1)}), bf16[16,16,384]{2,1,0:T(8,128)(2,1)S(1)}, u32[]{:S(2)}, u32[]{:S(2)}) async-start(bf16[16,16,384]{2,1,0:T(8,128)(2,1)} %coefficients.1), calls=%async_computation | async-start | bytes 393216 | tf_op jit(solution)/shard_map/exchange/all_to_all | solution.py:240
  17.6 20.0 %collective-permute-start = (bf16[3,128,768]{2,1,0:T(8,128)(2,1)}, bf16[3,128,768]{2,1,0:T(8,128)(2,1)S(1)}, u32[]{:S(2)}, u32[]{:S(2)}) collective-permute-start(bf16[3,128,768]{2,1,0:T(8,128)(2,1)} %get-tuple-element.23), channel_id=1, source_target_pairs={{0,16},{16,32},{32,48},{48,0},{64,80},{80,96},{96,112},{112,64},{1... | collective-permute-start | bytes 1769480 | tf_op jit(solution)/shard_map/tokens_x/ppermute | solution.py:249
  20.8 16.9 %collective-permute-start.1 = (bf16[3,128,768]{2,1,0:T(8,128)(2,1)}, bf16[3,128,768]{2,1,0:T(8,128)(2,1)S(1)}, u32[]{:S(2)}, u32[]{:S(2)}) collective-permute-start(bf16[3,128,768]{2,1,0:T(8,128)(2,1)} %get-tuple-element.24), channel_id=1, source_target_pairs={{0,48},{16,0},{32,16},{48,32},{64,112},{80,64},{96,80},{112,96},{1... | collective-permute-start | bytes 1769480 | tf_op jit(solution)/shard_map/tokens_x/ppermute | solution.py:250
  28.0 32.1 %all-to-all-start.1 = ((bf16[32,16,768]{2,1,0:T(8,128)(2,1)}), bf16[32,16,768]{2,1,0:T(8,128)(2,1)S(1)}, u32[]{:S(2)}, u32[]{:S(2)}) async-start(bf16[32,16,768]{2,1,0:T(8,128)(2,1)} %renew.1), calls=%async_computation.1 | async-start | bytes 1572864 | tf_op jit(solution)/shard_map/window/all_to_all | solution.py:268
  37.6 25.4 %copy-start = (bf16[2,128,768]{2,1,0:T(8,128)(2,1)S(1)}, bf16[2,128,768]{2,1,0:T(8,128)(2,1)}, u32[]{:S(2)}) copy-start(bf16[2,128,768]{2,1,0:T(8,128)(2,1)} %get-tuple-element.27.refs_0_) | copy-start | bytes 1179652
  37.7 12.6 %collective-permute-start.2 = (bf16[1,128,768]{2,1,0:T(8,128)(2,1)S(1)}, bf16[1,128,768]{2,1,0:T(8,128)(2,1)S(1)}, u32[]{:S(2)}, u32[]{:S(2)}) collective-permute-start(bf16[1,128,768]{2,1,0:T(8,128)(2,1)S(1)} %get-tuple-element.25), channel_id=1, source_target_pairs={{0,16},{16,32},{32,48},{48,0},{64,80},{80,96},{96,112},{112,64},{1... | collective-permute-start | bytes 589832 | tf_op jit(solution)/shard_map/tokens_x/ppermute | solution.py:253
  41.0 10.1 %collective-permute-start.3 = (bf16[1,128,768]{2,1,0:T(8,128)(2,1)S(1)}, bf16[1,128,768]{2,1,0:T(8,128)(2,1)S(1)}, u32[]{:S(2)}, u32[]{:S(2)}) collective-permute-start(bf16[1,128,768]{2,1,0:T(8,128)(2,1)S(1)} %get-tuple-element.26), channel_id=1, source_target_pairs={{0,48},{16,0},{32,16},{48,32},{64,112},{80,64},{96,80},{112,96},{1... | collective-permute-start | bytes 589832 | tf_op jit(solution)/shard_map/tokens_x/ppermute | solution.py:254
  60.1 4.9 %collective-permute-start.4 = (bf16[512,768]{1,0:T(8,128)(2,1)S(1)}, bf16[512,768]{1,0:T(8,128)(2,1)S(1)}, u32[]{:S(2)}, u32[]{:S(2)}) collective-permute-start(bf16[512,768]{1,0:T(8,128)(2,1)S(1)} %bitcast.4), channel_id=1, source_target_pairs={{0,1},{1,0},{2,3},{3,2},{4,5},{5,4},{6,7},{7,6},{8,9},{9,8},{10,11... | collective-permute-start | bytes 2359304 | tf_op jit(solution)/shard_map/window_core/ppermute | solution.py:271
  66.3 13.1 %all-to-all-start.2 = ((bf16[4,128,512]{2,1,0:T(8,128)(2,1)}), bf16[4,128,512]{2,1,0:T(8,128)(2,1)S(1)}, u32[]{:S(2)}, u32[]{:S(2)}) async-start(bf16[4,128,512]{2,1,0:T(8,128)(2,1)} %product.3), calls=%async_computation.2 | async-start | bytes 1048576 | tf_op jit(solution)/shard_map/sum_x/all_to_all | solution.py:289

commit v5 on v4

--- a/solution.py
+++ b/solution.py
@@ -39,6 +39,14 @@
 def forward_kernel(ahead, behind, far0, far1):
     far0[0] = ahead[2]
     far1[0] = behind[2]
+
+
+def own_kernel(tokens, own, sems):
+    x = lax.axis_index("shard") % XS
+    piece = own.shape[2]
+    halves = [pl.multiple_of((h * XS + x) * piece, 128) for h in range(2)]
+    for copy in fetch([(tokens.at[:, pl.ds(at, piece)], own.at[h]) for h, at in enumerate(halves)], sems):
+        copy.wait()
 
 
 def lay_out(indices, lanes):
@@ -94,19 +102,19 @@
         send[r] = message[:, r % 2 * half : (r % 2 + 1) * half]
 
 
-def cut_kernel(tokens, own, ahead, behind, cut, sems):
+def cut_kernel(tokens, ahead, behind, cut, sems):
     x = lax.axis_index("shard") % XS
     piece = cut.shape[2]
     pieces = []
-    for i, (d, h) in enumerate([(1, 0), (1, 1), (2, 0), (3, 0), (3, 1), (2, 1), (0, 0), (0, 1)]):
+    for i, (d, h) in enumerate([(1, 0), (1, 1), (2, 0), (3, 0), (3, 1), (2, 1)]):
         at = pl.multiple_of((h * XS + (x + d) % XS) * piece, 128)
         pieces.append((tokens.at[:, pl.ds(at, piece)], cut.at[i]))
     cuts = fetch(pieces, sems)
     outs = []
-    for i, (first, number, out) in enumerate([(0, 3, ahead), (3, 3, behind), (6, 2, own)]):
+    for i, (first, number, out) in enumerate([(0, 3, ahead), (3, 3, behind)]):
         for c in cuts[first : first + number]:
             c.wait()
-        outs += fetch([(cut.at[pl.ds(first, number)], out)], sems.at[pl.ds(MEMBERS + i, 1)])
+        outs += fetch([(cut.at[pl.ds(first, number)], out)], sems.at[pl.ds(len(pieces) + i, 1)])
     for out in outs:
         out.wait()
 
@@ -128,18 +136,18 @@
     rows = weight.shape[0]
     half = weight.shape[1] // 2
     core = lax.axis_index("replica") % 2
-    freq = lax.broadcasted_iota(jnp.int32, (GROUP, 128), 0).astype(F32)
+    freq = lax.broadcasted_iota(jnp.int32, (GROUP, 128), 0).astype(F32).astype(BF16)
     columns = []
     for c in range(lanes // 128):
         at = slice(c * 128, (c + 1) * 128)
         sums = [jnp.zeros((GROUP, 128), F32) for _ in range(2)]
         for r in range(replicas):
-            message = received[r, :, at].astype(F32)
+            message = received[r, :, at]
             for side in range(2):
-                dense = jnp.zeros((GROUP, 128), F32)
+                dense = jnp.zeros((GROUP, 128), BF16)
                 for row in range(side * TOPK, (side + 1) * TOPK):
                     dense = jnp.where(freq == message[2 * TOPK + row][None, :], message[row][None, :], dense)
-                sums[side] = sums[side] + dense
+                sums[side] = sums[side] + dense.astype(F32)
         columns.append(jnp.concatenate(sums, axis=0))
     field = contract(jnp.concatenate(columns, axis=1), table[...], 0, 0)
     old = weight[:, pl.ds(pl.multiple_of(core * half, 128), half)].astype(F32)
@@ -226,12 +234,12 @@
         )(momentum, gradient, ordered_indices, table)
     with jax.named_scope("cut"):
         tokens, send = lax.optimization_barrier((tokens, send))
-        own, ahead, behind = pl.pallas_call(
+        ahead, behind = pl.pallas_call(
             cut_kernel,
-            out_shape=[jax.ShapeDtypeStruct((n, count, piece), BF16) for n in (2, 3, 3)],
+            out_shape=[jax.ShapeDtypeStruct((n, count, piece), BF16) for n in (3, 3)],
             in_specs=[hbm],
-            out_specs=[hbm] * 3,
-            scratch_shapes=[pltpu.VMEM((MEMBERS, count, piece), BF16), pltpu.SemaphoreType.DMA((MEMBERS + 3,))],
+            out_specs=[hbm] * 2,
+            scratch_shapes=[pltpu.VMEM((6, count, piece), BF16), pltpu.SemaphoreType.DMA((8,))],
             compiler_params=params,
             cost_estimate=pl.CostEstimate(flops=0, bytes_accessed=4 * tokens.size, transcendentals=0),
         )(tokens)
@@ -252,6 +260,16 @@
         far0, far1 = call(forward_kernel, [one, one], ahead, behind, flops=5 * 10**10)
         far0 = lax.ppermute(far0, "shard", on)
         far1 = lax.ppermute(far1, "shard", back)
+        tokens, far0 = lax.optimization_barrier((tokens, far0))
+        own = pl.pallas_call(
+            own_kernel,
+            out_shape=jax.ShapeDtypeStruct((2, count, piece), BF16),
+            in_specs=[hbm],
+            out_specs=vmem,
+            scratch_shapes=[pltpu.SemaphoreType.DMA((2,))],
+            compiler_params=params,
+            cost_estimate=pl.CostEstimate(flops=0, bytes_accessed=4 * count * piece, transcendentals=0),
+        )(tokens)
         blocks = (own, ahead, far0, far1, behind)
     with jax.named_scope("momentum"):
         momentum, renewed = lax.optimization_barrier((momentum, renewed))

time: 80.7 us -> 80.4 us (level)
  waiting for transfers between devices: 24.2 us -> 21.7 us
  Pallas kernels: 13.4 us -> 14.7 us
  local copies, waits for them, and re-layouts: 0.02 us -> 1 us
    ppermute x1, waiting for transfers between devices: 5.99 us -> 3.64 us  [local(): far0 = lax.ppermute(far0, 'shard', on)]
    pallas_call x0 -> x1, Pallas kernels: none -> 1.78 us  [local(): pl.pallas_call(own_kernel, out_shape=jax.ShapeDtypeStruct((2, count, piec...]
    ppermute x1, waiting for transfers between devices: 1.27 us -> 0.28 us  [local(): lax.ppermute(window, 'replica', [(i, i ^ 1) for i in range(replicas)])]
    unnamed x6, local copies, waits for them, and re-layouts: 0.02 us -> 1 us
  transfers between devices with their start and end apart: 8 -> 8, of which waited for: 6 -> 6; matrix products, arithmetic and copies ran while one was open for 0% -> 0% of each run, Pallas kernels for 11% -> 12%
where the time goes in v5:
time: 80.4 us; the launch traced here: 79.8 us
  starting transfers between devices  41.7 us (52%)
  waiting for transfers between devices  21.7 us (27%)
  Pallas kernels  14.7 us (18%)
  local copies, waits for them, and re-layouts  1 us (1%)
    all_to_all x1, starting transfers between devices, local(): received = lax.all_to_all(send, 'replica', 0, 0)  11.8 us
    all_to_all x1, starting transfers between devices, local(): lax.all_to_all(renewed, 'shard', 0, 0).reshape(shards * rows, piece)  9.67 us
    all_to_all x1, waiting for transfers between devices, local(): lax.all_to_all(renewed, 'shard', 0, 0).reshape(shards * rows, piece)  9.03 us
    all_to_all x1, waiting for transfers between devices, local(): parts = lax.all_to_all(ordered, 'shard', 0, 0, axis_index_groups=groups)  5.78 us
    pallas_call x5, Pallas kernels, call(): pl.pallas_call(kernel, out_shape=out, in_specs=[pl.BlockSpec(memory_space...  4.8 us
    all_to_all x1, starting transfers between devices, local(): parts = lax.all_to_all(ordered, 'shard', 0, 0, axis_index_groups=groups)  4.22 us
    ppermute x1, waiting for transfers between devices, local(): far0 = lax.ppermute(far0, 'shard', on)  3.64 us
    ppermute x1, starting transfers between devices, local(): behind = lax.ppermute(behind, 'shard', back)  3.37 us
  transfers between devices with their start and end apart: 8, of which 6 were waited for; matrix products, arithmetic and copies ran while one was open for 0% of the time, Pallas kernels for 12%

profile of v5, /device:TPU:1, one launch (start us, length us, event | category | flops | bytes accessed | tf_op | source)
XLA Modules:
  0.0 79.8 jit_solution(13682815774934416533)
XLA Ops:
  0.6 0.0 copy-start.1
  0.7 2.8 %coefficients.1 = bf16[16,16,384]{2,1,0:T(8,128)(2,1)} custom-call(f32[1,16,6144]{2,1,0:T(8,128)} %momentum.4, bf16[1,16,6144]{2,1,0:T(8,128)(2,1)} %gradient.3, s32[16,4,96]{2,1,0:T(4,128)} %bitcast.6, f32[128,128]{1,0:T(8,128)} %constant.2.clone.table), custom_call_target="tpu_custom_call" | custom-call | flops 100000000 | bytes 1000000 | tf_op jit(solution)/shard_map/coefficients/pallas_call | solution.py:226
  3.4 11.8 %all-to-all-start = ((bf16[16,16,384]{2,1,0:T(8,128)(2,1)}), bf16[16,16,384]{2,1,0:T(8,128)(2,1)S(1)}, u32[]{:S(2)}, u32[]{:S(2)}) async-start(bf16[16,16,384]{2,1,0:T(8,128)(2,1)} %coefficients.1), calls=%async_computation | async-start | bytes 393216 | tf_op jit(solution)/shard_map/exchange/all_to_all | solution.py:248
  15.3 2.2 %cut.1 = (bf16[3,128,768]{2,1,0:T(8,128)(2,1)}, bf16[3,128,768]{2,1,0:T(8,128)(2,1)}) custom-call(bf16[128,6144]{1,0:T(8,128)(2,1)} %tokens.1), custom_call_target="tpu_custom_call" | custom-call | bytes 3145728 | tf_op jit(solution)/shard_map/cut/pallas_call | solution.py:237
  17.5 3.1 %collective-permute-start = (bf16[3,128,768]{2,1,0:T(8,128)(2,1)}, bf16[3,128,768]{2,1,0:T(8,128)(2,1)S(1)}, u32[]{:S(2)}, u32[]{:S(2)}) collective-permute-start(bf16[3,128,768]{2,1,0:T(8,128)(2,1)} %get-tuple-element.23), channel_id=1, source_target_pairs={{0,16},{16,32},{32,48},{48,0},{64,80},{80,96},{96,112},{112,64},{1... | collective-permute-start | bytes 1769480 | tf_op jit(solution)/shard_map/tokens_x/ppermute | solution.py:257
  20.6 3.4 %collective-permute-start.1 = (bf16[3,128,768]{2,1,0:T(8,128)(2,1)}, bf16[3,128,768]{2,1,0:T(8,128)(2,1)S(1)}, u32[]{:S(2)}, u32[]{:S(2)}) collective-permute-start(bf16[3,128,768]{2,1,0:T(8,128)(2,1)} %get-tuple-element.24), channel_id=1, source_target_pairs={{0,48},{16,0},{32,16},{48,32},{64,112},{80,64},{96,80},{112,96},{1... | collective-permute-start | bytes 1769480 | tf_op jit(solution)/shard_map/tokens_x/ppermute | solution.py:258
  24.0 1.6 %all-to-all-done.received = bf16[16,16,384]{2,1,0:T(8,128)(2,1)S(1)} async-done(((bf16[16,16,384]{2,1,0:T(8,128)(2,1)}), bf16[16,16,384]{2,1,0:T(8,128)(2,1)S(1)}, u32[]{:S(2)}, u32[]{:S(2)}) %all-to-all-start) | async-done | bytes 196640 | tf_op jit(solution)/shard_map/exchange/all_to_all | solution.py:248
  25.6 2.1 %renew.1 = bf16[32,16,768]{2,1,0:T(8,128)(2,1)} custom-call(bf16[16,16,384]{2,1,0:T(8,128)(2,1)S(1)} %all-to-all-done.received, bf16[16,6144]{1,0:T(8,128)(2,1)S(1)} %copy-done.2, f32[128,128]{1,0:T(8,128)S(1)} %copy-done.1), custom_call_target="tpu_custom_call" | custom-call | flops 10000000000 | bytes 1245184 | tf_op jit(solution)/shard_map/renew/pallas_call | solution.py:197
  27.6 9.7 %all-to-all-start.1 = ((bf16[32,16,768]{2,1,0:T(8,128)(2,1)}), bf16[32,16,768]{2,1,0:T(8,128)(2,1)S(1)}, u32[]{:S(2)}, u32[]{:S(2)}) async-start(bf16[32,16,768]{2,1,0:T(8,128)(2,1)} %renew.1), calls=%async_computation.1 | async-start | bytes 1572864 | tf_op jit(solution)/shard_map/window/all_to_all | solution.py:286
  37.4 3.1 %collective-permute-start.2 = (bf16[1,128,768]{2,1,0:T(8,128)(2,1)S(1)}, bf16[1,128,768]{2,1,0:T(8,128)(2,1)S(1)}, u32[]{:S(2)}, u32[]{:S(2)}) collective-permute-start(bf16[1,128,768]{2,1,0:T(8,128)(2,1)S(1)} %get-tuple-element.25), channel_id=1, source_target_pairs={{0,16},{16,32},{32,48},{48,0},{64,80},{80,96},{96,112},{112,64},{1... | collective-permute-start | bytes 589832 | tf_op jit(solution)/shard_map/tokens_x/ppermute | solution.py:261
  40.5 3.4 %collective-permute-start.3 = (bf16[1,128,768]{2,1,0:T(8,128)(2,1)S(1)}, bf16[1,128,768]{2,1,0:T(8,128)(2,1)S(1)}, u32[]{:S(2)}, u32[]{:S(2)}) collective-permute-start(bf16[1,128,768]{2,1,0:T(8,128)(2,1)S(1)} %get-tuple-element.28), channel_id=1, source_target_pairs={{0,48},{16,0},{32,16},{48,32},{64,112},{80,64},{96,80},{112,96},{1... | collective-permute-start | bytes 589832 | tf_op jit(solution)/shard_map/tokens_x/ppermute | solution.py:262
  43.9 3.6 %collective-permute-done.2.refs_2_ = bf16[1,128,768]{2,1,0:T(8,128)(2,1)S(1)} collective-permute-done((bf16[1,128,768]{2,1,0:T(8,128)(2,1)S(1)}, bf16[1,128,768]{2,1,0:T(8,128)(2,1)S(1)}, u32[]{:S(2)}, u32[]{:S(2)}) %collective-permute-start.2) | collective-permute-done | bytes 196640 | tf_op jit(solution)/shard_map/tokens_x/ppermute | solution.py:261
  47.5 1.8 %tokens_x.3.refs_0_ = bf16[2,128,768]{2,1,0:T(8,128)(2,1)} custom-call(bf16[128,6144]{1,0:T(8,128)(2,1)} %tokens.1), custom_call_target="tpu_custom_call" | custom-call | bytes 393216 | tf_op jit(solution)/shard_map/tokens_x/pallas_call | solution.py:264
  49.3 1.4 %collective-permute-done.3.refs_3_ = bf16[1,128,768]{2,1,0:T(8,128)(2,1)S(1)} collective-permute-done((bf16[1,128,768]{2,1,0:T(8,128)(2,1)S(1)}, bf16[1,128,768]{2,1,0:T(8,128)(2,1)S(1)}, u32[]{:S(2)}, u32[]{:S(2)}) %collective-permute-start.3) | collective-permute-done | bytes 196640 | tf_op jit(solution)/shard_map/tokens_x/ppermute | solution.py:262
  50.7 9.0 %all-to-all-done.1 = bf16[32,16,768]{2,1,0:T(8,128)(2,1)S(1)} async-done(((bf16[32,16,768]{2,1,0:T(8,128)(2,1)}), bf16[32,16,768]{2,1,0:T(8,128)(2,1)S(1)}, u32[]{:S(2)}, u32[]{:S(2)}) %all-to-all-start.1) | async-done | bytes 786464 | tf_op jit(solution)/shard_map/window/all_to_all | solution.py:286
  59.7 3.0 %collective-permute-start.4 = (bf16[512,768]{1,0:T(8,128)(2,1)S(1)}, bf16[512,768]{1,0:T(8,128)(2,1)S(1)}, u32[]{:S(2)}, u32[]{:S(2)}) collective-permute-start(bf16[512,768]{1,0:T(8,128)(2,1)S(1)} %bitcast.4), channel_id=1, source_target_pairs={{0,1},{1,0},{2,3},{3,2},{4,5},{5,4},{6,7},{7,6},{8,9},{9,8},{10,11... | collective-permute-start | bytes 2359304 | tf_op jit(solution)/shard_map/window_core/ppermute | solution.py:289
  62.7 1.0 %copy-done = bf16[2,128,768]{2,1,0:T(8,128)(2,1)S(1)} copy-done((bf16[2,128,768]{2,1,0:T(8,128)(2,1)S(1)}, bf16[2,128,768]{2,1,0:T(8,128)(2,1)}, u32[]{:S(2)}) %copy-start) | copy-done | bytes 393240
  63.7 0.6 product.2
  64.3 0.3 collective-permute-done.4.window
  64.6 1.4 %product.3 = bf16[4,128,512]{2,1,0:T(8,128)(2,1)} custom-call(bf16[512,768]{1,0:T(8,128)(2,1)S(1)} %get-tuple-element.35.rest, bf16[512,768]{1,0:T(8,128)(2,1)S(1)} %collective-permute-done.4.window, f32[512,512]{1,0:T(8,128)S(1)} %get-tuple-element.36.first), custom_call_target="tpu_custom_call" | custom-call | flops 402653184 | bytes 3145728 | tf_op jit(solution)/shard_map/product/pallas_call | solution.py:197
  66.0 4.2 %all-to-all-start.2 = ((bf16[4,128,512]{2,1,0:T(8,128)(2,1)}), bf16[4,128,512]{2,1,0:T(8,128)(2,1)S(1)}, u32[]{:S(2)}, u32[]{:S(2)}) async-start(bf16[4,128,512]{2,1,0:T(8,128)(2,1)} %product.3), calls=%async_computation.2 | async-start | bytes 1048576 | tf_op jit(solution)/shard_map/sum_x/all_to_all | solution.py:307
  70.2 3.1 %momentum.3 = f32[1,16,6144]{2,1,0:T(8,128)} custom-call(f32[1,16,6144]{2,1,0:T(8,128)} %momentum.4, bf16[1,16,6144]{2,1,0:T(8,128)(2,1)} %gradient.3, s32[16,4,96]{2,1,0:T(4,128)} %bitcast.7, f32[128,128]{1,0:T(8,128)} %constant.2.clone.table), custom_call_target="tpu_custom_call" | custom-call | flops 49999998976 | bytes 1000000 | tf_op jit(solution)/shard_map/momentum/pallas_call | solution.py:276
  73.3 5.8 %all-to-all-done.2.parts = bf16[4,128,512]{2,1,0:T(8,128)(2,1)S(1)} async-done(((bf16[4,128,512]{2,1,0:T(8,128)(2,1)}), bf16[4,128,512]{2,1,0:T(8,128)(2,1)S(1)}, u32[]{:S(2)}, u32[]{:S(2)}) %all-to-all-start.2) | async-done | bytes 524320 | tf_op jit(solution)/shard_map/sum_x/all_to_all | solution.py:307
  79.1 0.7 sum_x.1
  (7 shorter events, 0.0 us)
Async XLA Ops:
  0.6 25.0 %copy-start.1 = (f32[128,128]{1,0:T(8,128)S(1)}, f32[128,128]{1,0:T(8,128)}, u32[]{:S(2)}) copy-start(f32[128,128]{1,0:T(8,128)} %constant.2.clone.table) | copy-start | bytes 196612
  0.6 25.0 %copy-start.2 = (bf16[16,6144]{1,0:T(8,128)(2,1)S(1)}, bf16[16,6144]{1,0:T(8,128)(2,1)}, u32[]{:S(2)}) copy-start(bf16[16,6144]{1,0:T(8,128)(2,1)} %weight.1) | copy-start | bytes 589828
  3.4 22.2 %all-to-all-start = ((bf16[16,16,384]{2,1,0:T(8,128)(2,1)}), bf16[16,16,384]{2,1,0:T(8,128)(2,1)S(1)}, u32[]{:S(2)}, u32[]{:S(2)}) async-start(bf16[16,16,384]{2,1,0:T(8,128)(2,1)} %coefficients.1), calls=%async_computation | async-start | bytes 393216 | tf_op jit(solution)/shard_map/exchange/all_to_all | solution.py:248
  17.5 19.8 %collective-permute-start = (bf16[3,128,768]{2,1,0:T(8,128)(2,1)}, bf16[3,128,768]{2,1,0:T(8,128)(2,1)S(1)}, u32[]{:S(2)}, u32[]{:S(2)}) collective-permute-start(bf16[3,128,768]{2,1,0:T(8,128)(2,1)} %get-tuple-element.23), channel_id=1, source_target_pairs={{0,16},{16,32},{32,48},{48,0},{64,80},{80,96},{96,112},{112,64},{1... | collective-permute-start | bytes 1769480 | tf_op jit(solution)/shard_map/tokens_x/ppermute | solution.py:257
  20.6 16.7 %collective-permute-start.1 = (bf16[3,128,768]{2,1,0:T(8,128)(2,1)}, bf16[3,128,768]{2,1,0:T(8,128)(2,1)S(1)}, u32[]{:S(2)}, u32[]{:S(2)}) collective-permute-start(bf16[3,128,768]{2,1,0:T(8,128)(2,1)} %get-tuple-element.24), channel_id=1, source_target_pairs={{0,48},{16,0},{32,16},{48,32},{64,112},{80,64},{96,80},{112,96},{1... | collective-permute-start | bytes 1769480 | tf_op jit(solution)/shard_map/tokens_x/ppermute | solution.py:258
  27.6 32.1 %all-to-all-start.1 = ((bf16[32,16,768]{2,1,0:T(8,128)(2,1)}), bf16[32,16,768]{2,1,0:T(8,128)(2,1)S(1)}, u32[]{:S(2)}, u32[]{:S(2)}) async-start(bf16[32,16,768]{2,1,0:T(8,128)(2,1)} %renew.1), calls=%async_computation.1 | async-start | bytes 1572864 | tf_op jit(solution)/shard_map/window/all_to_all | solution.py:286
  37.4 10.2 %collective-permute-start.2 = (bf16[1,128,768]{2,1,0:T(8,128)(2,1)S(1)}, bf16[1,128,768]{2,1,0:T(8,128)(2,1)S(1)}, u32[]{:S(2)}, u32[]{:S(2)}) collective-permute-start(bf16[1,128,768]{2,1,0:T(8,128)(2,1)S(1)} %get-tuple-element.25), channel_id=1, source_target_pairs={{0,16},{16,32},{32,48},{48,0},{64,80},{80,96},{96,112},{112,64},{1... | collective-permute-start | bytes 589832 | tf_op jit(solution)/shard_map/tokens_x/ppermute | solution.py:261
  40.5 10.2 %collective-permute-start.3 = (bf16[1,128,768]{2,1,0:T(8,128)(2,1)S(1)}, bf16[1,128,768]{2,1,0:T(8,128)(2,1)S(1)}, u32[]{:S(2)}, u32[]{:S(2)}) collective-permute-start(bf16[1,128,768]{2,1,0:T(8,128)(2,1)S(1)} %get-tuple-element.28), channel_id=1, source_target_pairs={{0,48},{16,0},{32,16},{48,32},{64,112},{80,64},{96,80},{112,96},{1... | collective-permute-start | bytes 589832 | tf_op jit(solution)/shard_map/tokens_x/ppermute | solution.py:262
  59.7 4.9 %collective-permute-start.4 = (bf16[512,768]{1,0:T(8,128)(2,1)S(1)}, bf16[512,768]{1,0:T(8,128)(2,1)S(1)}, u32[]{:S(2)}, u32[]{:S(2)}) collective-permute-start(bf16[512,768]{1,0:T(8,128)(2,1)S(1)} %bitcast.4), channel_id=1, source_target_pairs={{0,1},{1,0},{2,3},{3,2},{4,5},{5,4},{6,7},{7,6},{8,9},{9,8},{10,11... | collective-permute-start | bytes 2359304 | tf_op jit(solution)/shard_map/window_core/ppermute | solution.py:289
  62.7 1.0 %copy-start = (bf16[2,128,768]{2,1,0:T(8,128)(2,1)S(1)}, bf16[2,128,768]{2,1,0:T(8,128)(2,1)}, u32[]{:S(2)}) copy-start(bf16[2,128,768]{2,1,0:T(8,128)(2,1)} %tokens_x.3.refs_0_) | copy-start | bytes 1179652
  66.0 13.1 %all-to-all-start.2 = ((bf16[4,128,512]{2,1,0:T(8,128)(2,1)}), bf16[4,128,512]{2,1,0:T(8,128)(2,1)S(1)}, u32[]{:S(2)}, u32[]{:S(2)}) async-start(bf16[4,128,512]{2,1,0:T(8,128)(2,1)} %product.3), calls=%async_computation.2 | async-start | bytes 1048576 | tf_op jit(solution)/shard_map/sum_x/all_to_all | solution.py:307

commit v6 on v5

--- a/solution.py
+++ b/solution.py
@@ -68,7 +68,7 @@
     ]
 
 
-def choose(momentum, gradient, indices, table):
+def choose(momentum, gradient, index, table):
     rows, width = momentum.shape
     pairs = width // PAIR
     lanes = pairs * rows
@@ -76,12 +76,11 @@
     stacked = jnp.concatenate([blended[:, p * PAIR : (p + 1) * PAIR] for p in range(pairs)], axis=0)
     spectra = contract(table, stacked, 1, 1)
     freq = lax.broadcasted_iota(jnp.int32, (GROUP, lanes), 0).astype(F32)
-    index = lay_out(indices, lanes)
     picked = []
     for side in range(2):
         part = spectra[side * GROUP : (side + 1) * GROUP]
         picked += [jnp.where(freq == index[side * TOPK + j], part, 0.0) for j in range(TOPK)]
-    return blended, index, picked
+    return blended, picked
 
 
 def fetch(pairs, sems):
@@ -92,9 +91,12 @@
 
 
 def send_kernel(momentum, gradient, indices, table, send, mom, grad, ind, tab, sems):
-    for load in fetch([(momentum, mom), (gradient, grad), (indices, ind), (table, tab)], sems):
+    first, *loads = fetch([(indices, ind), (momentum, mom), (gradient, grad), (table, tab)], sems)
+    first.wait()
+    index = lay_out(ind, mom.shape[1] * mom.shape[2] // PAIR)
+    for load in loads:
         load.wait()
-    _, index, picked = choose(mom[0], grad[0], ind, tab[...])
+    _, picked = choose(mom[0], grad[0], index, tab[...])
     values = [jnp.sum(p, axis=0, keepdims=True) for p in picked]
     message = jnp.concatenate(values + index, axis=0).astype(BF16)
     half = message.shape[1] // 2
@@ -123,7 +125,8 @@
     for load in fetch([(momentum, mom), (gradient, grad), (indices, ind), (table, tab)], sems):
         load.wait()
     rows = mom.shape[1]
-    blended, _, picked = choose(mom[0], grad[0], ind, tab[...])
+    index = lay_out(ind, rows * mom.shape[2] // PAIR)
+    blended, picked = choose(mom[0], grad[0], index, tab[...])
     kept = [sum(picked[side * TOPK + 1 : (side + 1) * TOPK], picked[side * TOPK]) for side in range(2)]
     field = contract(jnp.concatenate(kept, axis=0), tab[...], 0, 0)
     for p in range(blended.shape[1] // PAIR):
@@ -176,12 +179,18 @@
     rest[...] = stack(*blocks, 1 - core)
 
 
-def second_kernel(rest, window, first, out):
+def second_kernel(rest, window, first, out, ready, sems):
     x = lax.axis_index("shard") % XS
-    count = out.shape[1]
-    total = first[...] + product(rest[...], window)
-    for d in range(XS):
-        out[(x + XS - d) % XS] = total[d * count : (d + 1) * count].astype(BF16)
+    count = ready.shape[1]
+    copies = []
+    for i in range(0, XS, 2):
+        at = slice(i * count, (i + 2) * count)
+        total = first[at] + product(rest[at], window)
+        for d in range(i, i + 2):
+            ready[d] = total[(d - i) * count : (d - i + 1) * count].astype(BF16)
+            copies += fetch([(ready.at[d], out.at[(x + XS - d) % XS])], sems.at[pl.ds(d, 1)])
+    for copy in copies:
+        copy.wait()
 
 
 def finish_kernel(parts, out):
@@ -191,14 +200,15 @@
     out[...] = total.astype(BF16)
 
 
-def call(kernel, out, *args, flops=0):
+def call(kernel, out, *args, flops=0, space=pltpu.VMEM, scratch=()):
     out_list = jax.tree.leaves(out)
     moved = sum(a.size * a.dtype.itemsize for a in args) + sum(o.size * o.dtype.itemsize for o in out_list)
     return pl.pallas_call(
         kernel,
         out_shape=out,
         in_specs=[pl.BlockSpec(memory_space=pltpu.VMEM)] * len(args),
-        out_specs=jax.tree.map(lambda _: pl.BlockSpec(memory_space=pltpu.VMEM), out),
+        out_specs=jax.tree.map(lambda _: pl.BlockSpec(memory_space=space), out),
+        scratch_shapes=list(scratch),
         compiler_params=pltpu.CompilerParams(vmem_limit_bytes=20 * 1024 * 1024),
         cost_estimate=pl.CostEstimate(flops=flops, bytes_accessed=moved, transcendentals=0),
     )(*args)
@@ -248,7 +258,12 @@
         received = lax.all_to_all(send, "replica", 0, 0)
     with jax.named_scope("renew"):
         renewed = call(
-            renew_kernel, jax.ShapeDtypeStruct((shards, rows, piece), BF16), received, weight, table, flops=10**10
+            renew_kernel,
+            jax.ShapeDtypeStruct((shards, rows, piece), BF16),
+            received,
+            weight,
+            table,
+            flops=10**10,
         )
     with jax.named_scope("tokens_x"):
         on, back = (
@@ -267,7 +282,7 @@
             in_specs=[hbm],
             out_specs=vmem,
             scratch_shapes=[pltpu.SemaphoreType.DMA((2,))],
-            compiler_params=params,
+            compiler_params=pltpu.CompilerParams(vmem_limit_bytes=20 * 1024 * 1024),
             cost_estimate=pl.CostEstimate(flops=0, bytes_accessed=4 * count * piece, transcendentals=0),
         )(tokens)
         blocks = (own, ahead, far0, far1, behind)
@@ -301,7 +316,16 @@
             flops=work,
         )
         shape = (XS, count, size)
-        ordered = call(second_kernel, jax.ShapeDtypeStruct(shape, BF16), rest, other, first, flops=work)
+        ordered = call(
+            second_kernel,
+            jax.ShapeDtypeStruct(shape, BF16),
+            rest,
+            other,
+            first,
+            flops=work,
+            space=pltpu.HBM,
+            scratch=(pltpu.VMEM(shape, BF16), pltpu.SemaphoreType.DMA((XS,))),
+        )
     with jax.named_scope("sum_x"):
         groups = [[y * XS + i for i in range(XS)] for y in range(YS)]
         parts = lax.all_to_all(ordered, "shard", 0, 0, axis_index_groups=groups)

time: 80.4 us -> 80.2 us (level)
  waiting for transfers between devices: 21.7 us -> 23.9 us
  Pallas kernels: 14.7 us -> 13.1 us
  local copies, waits for them, and re-layouts: 1 us -> 0.02 us
    pallas_call x1, Pallas kernels: 1.78 us -> 0.08 us  [local(): pl.pallas_call(own_kernel, out_shape=jax.ShapeDtypeStruct((2, count, piec...]
    ppermute x1, waiting for transfers between devices: 1.37 us -> 2.68 us  [local(): far1 = lax.ppermute(far1, 'shard', back)]
    ppermute x1, waiting for transfers between devices: 0.28 us -> 1.28 us  [local(): lax.ppermute(window, 'replica', [(i, i ^ 1) for i in range(replicas)])]
    unnamed x6, local copies, waits for them, and re-layouts: 1 us -> 0.02 us
  transfers between devices with their start and end apart: 8 -> 8, of which waited for: 6 -> 6; matrix products, arithmetic and copies ran while one was open for 0% -> 0% of each run, Pallas kernels for 12% -> 11%
where the time goes in v6:
time: 80.2 us; the launch traced here: 79.6 us
  starting transfers between devices  41.8 us (52%)
  waiting for transfers between devices  23.9 us (30%)
  Pallas kernels  13.1 us (16%)
    all_to_all x1, starting transfers between devices, local(): received = lax.all_to_all(send, 'replica', 0, 0)  11.8 us
    all_to_all x1, starting transfers between devices, local(): lax.all_to_all(renewed, 'shard', 0, 0).reshape(shards * rows, piece)  9.67 us
    all_to_all x1, waiting for transfers between devices, local(): lax.all_to_all(renewed, 'shard', 0, 0).reshape(shards * rows, piece)  9.03 us
    all_to_all x1, waiting for transfers between devices, local(): parts = lax.all_to_all(ordered, 'shard', 0, 0, axis_index_groups=groups)  5.49 us
    pallas_call x5, Pallas kernels, call(): pl.pallas_call(kernel, out_shape=out, in_specs=[pl.BlockSpec(memory_space...  4.72 us
    all_to_all x1, starting transfers between devices, local(): parts = lax.all_to_all(ordered, 'shard', 0, 0, axis_index_groups=groups)  4.22 us
    ppermute x1, waiting for transfers between devices, local(): far0 = lax.ppermute(far0, 'shard', on)  3.9 us
    pallas_call x1, Pallas kernels, local(): pl.pallas_call(remain_kernel, out_shape=jax.ShapeDtypeStruct(momentum.sha...  3.41 us
  transfers between devices with their start and end apart: 8, of which 6 were waited for; matrix products, arithmetic and copies ran while one was open for 0% of the time, Pallas kernels for 11%

profile of v6, /device:TPU:1, one launch (start us, length us, event | category | flops | bytes accessed | tf_op | source)
XLA Modules:
  0.0 79.6 jit_solution(2941918745826855440)
XLA Ops:
  0.6 0.0 copy-start.1
  0.7 2.6 %coefficients.1 = bf16[16,16,384]{2,1,0:T(8,128)(2,1)} custom-call(f32[1,16,6144]{2,1,0:T(8,128)} %momentum.4, bf16[1,16,6144]{2,1,0:T(8,128)(2,1)} %gradient.3, s32[16,4,96]{2,1,0:T(4,128)} %bitcast.6, f32[128,128]{1,0:T(8,128)} %constant.2.clone.table), custom_call_target="tpu_custom_call" | custom-call | flops 100000000 | bytes 1000000 | tf_op jit(solution)/shard_map/coefficients/pallas_call | solution.py:236
  3.3 11.8 %all-to-all-start = ((bf16[16,16,384]{2,1,0:T(8,128)(2,1)}), bf16[16,16,384]{2,1,0:T(8,128)(2,1)S(1)}, u32[]{:S(2)}, u32[]{:S(2)}) async-start(bf16[16,16,384]{2,1,0:T(8,128)(2,1)} %coefficients.1), calls=%async_computation | async-start | bytes 393216 | tf_op jit(solution)/shard_map/exchange/all_to_all | solution.py:258
  15.1 2.2 %cut.1 = (bf16[3,128,768]{2,1,0:T(8,128)(2,1)}, bf16[3,128,768]{2,1,0:T(8,128)(2,1)}) custom-call(bf16[128,6144]{1,0:T(8,128)(2,1)} %tokens.1), custom_call_target="tpu_custom_call" | custom-call | bytes 3145728 | tf_op jit(solution)/shard_map/cut/pallas_call | solution.py:247
  17.4 3.1 %collective-permute-start = (bf16[3,128,768]{2,1,0:T(8,128)(2,1)}, bf16[3,128,768]{2,1,0:T(8,128)(2,1)S(1)}, u32[]{:S(2)}, u32[]{:S(2)}) collective-permute-start(bf16[3,128,768]{2,1,0:T(8,128)(2,1)} %get-tuple-element.23), channel_id=1, source_target_pairs={{0,16},{16,32},{32,48},{48,0},{64,80},{80,96},{96,112},{112,64},{1... | collective-permute-start | bytes 1769480 | tf_op jit(solution)/shard_map/tokens_x/ppermute | solution.py:272
  20.5 3.4 %collective-permute-start.1 = (bf16[3,128,768]{2,1,0:T(8,128)(2,1)}, bf16[3,128,768]{2,1,0:T(8,128)(2,1)S(1)}, u32[]{:S(2)}, u32[]{:S(2)}) collective-permute-start(bf16[3,128,768]{2,1,0:T(8,128)(2,1)} %get-tuple-element.24), channel_id=1, source_target_pairs={{0,48},{16,0},{32,16},{48,32},{64,112},{80,64},{96,80},{112,96},{1... | collective-permute-start | bytes 1769480 | tf_op jit(solution)/shard_map/tokens_x/ppermute | solution.py:273
  23.9 1.6 %all-to-all-done.received = bf16[16,16,384]{2,1,0:T(8,128)(2,1)S(1)} async-done(((bf16[16,16,384]{2,1,0:T(8,128)(2,1)}), bf16[16,16,384]{2,1,0:T(8,128)(2,1)S(1)}, u32[]{:S(2)}, u32[]{:S(2)}) %all-to-all-start) | async-done | bytes 196640 | tf_op jit(solution)/shard_map/exchange/all_to_all | solution.py:258
  25.5 2.1 %renew.1 = bf16[32,16,768]{2,1,0:T(8,128)(2,1)} custom-call(bf16[16,16,384]{2,1,0:T(8,128)(2,1)S(1)} %all-to-all-done.received, bf16[16,6144]{1,0:T(8,128)(2,1)S(1)} %copy-done.2, f32[128,128]{1,0:T(8,128)S(1)} %copy-done.1), custom_call_target="tpu_custom_call" | custom-call | flops 10000000000 | bytes 1245184 | tf_op jit(solution)/shard_map/renew/pallas_call | solution.py:206
  27.5 9.7 %all-to-all-start.1 = ((bf16[32,16,768]{2,1,0:T(8,128)(2,1)}), bf16[32,16,768]{2,1,0:T(8,128)(2,1)S(1)}, u32[]{:S(2)}, u32[]{:S(2)}) async-start(bf16[32,16,768]{2,1,0:T(8,128)(2,1)} %renew.1), calls=%async_computation.1 | async-start | bytes 1572864 | tf_op jit(solution)/shard_map/window/all_to_all | solution.py:301
  37.2 0.0 copy-start
  37.3 3.3 %collective-permute-start.2 = (bf16[1,128,768]{2,1,0:T(8,128)(2,1)S(1)}, bf16[1,128,768]{2,1,0:T(8,128)(2,1)S(1)}, u32[]{:S(2)}, u32[]{:S(2)}) collective-permute-start(bf16[1,128,768]{2,1,0:T(8,128)(2,1)S(1)} %get-tuple-element.25), channel_id=1, source_target_pairs={{0,16},{16,32},{32,48},{48,0},{64,80},{80,96},{96,112},{112,64},{1... | collective-permute-start | bytes 589832 | tf_op jit(solution)/shard_map/tokens_x/ppermute | solution.py:276
  40.6 3.4 %collective-permute-start.3 = (bf16[1,128,768]{2,1,0:T(8,128)(2,1)S(1)}, bf16[1,128,768]{2,1,0:T(8,128)(2,1)S(1)}, u32[]{:S(2)}, u32[]{:S(2)}) collective-permute-start(bf16[1,128,768]{2,1,0:T(8,128)(2,1)S(1)} %get-tuple-element.28), channel_id=1, source_target_pairs={{0,48},{16,0},{32,16},{48,32},{64,112},{80,64},{96,80},{112,96},{1... | collective-permute-start | bytes 589832 | tf_op jit(solution)/shard_map/tokens_x/ppermute | solution.py:277
  43.9 3.9 %collective-permute-done.2.refs_2_ = bf16[1,128,768]{2,1,0:T(8,128)(2,1)S(1)} collective-permute-done((bf16[1,128,768]{2,1,0:T(8,128)(2,1)S(1)}, bf16[1,128,768]{2,1,0:T(8,128)(2,1)S(1)}, u32[]{:S(2)}, u32[]{:S(2)}) %collective-permute-start.2) | collective-permute-done | bytes 196640 | tf_op jit(solution)/shard_map/tokens_x/ppermute | solution.py:276
  47.8 0.1 tokens_x.3.refs_0_
  47.9 2.7 %collective-permute-done.3.refs_3_ = bf16[1,128,768]{2,1,0:T(8,128)(2,1)S(1)} collective-permute-done((bf16[1,128,768]{2,1,0:T(8,128)(2,1)S(1)}, bf16[1,128,768]{2,1,0:T(8,128)(2,1)S(1)}, u32[]{:S(2)}, u32[]{:S(2)}) %collective-permute-start.3) | collective-permute-done | bytes 196640 | tf_op jit(solution)/shard_map/tokens_x/ppermute | solution.py:277
  50.6 9.0 %all-to-all-done.1 = bf16[32,16,768]{2,1,0:T(8,128)(2,1)S(1)} async-done(((bf16[32,16,768]{2,1,0:T(8,128)(2,1)}), bf16[32,16,768]{2,1,0:T(8,128)(2,1)S(1)}, u32[]{:S(2)}, u32[]{:S(2)}) %all-to-all-start.1) | async-done | bytes 786464 | tf_op jit(solution)/shard_map/window/all_to_all | solution.py:301
  59.6 3.0 %collective-permute-start.4 = (bf16[512,768]{1,0:T(8,128)(2,1)S(1)}, bf16[512,768]{1,0:T(8,128)(2,1)S(1)}, u32[]{:S(2)}, u32[]{:S(2)}) collective-permute-start(bf16[512,768]{1,0:T(8,128)(2,1)S(1)} %bitcast.4), channel_id=1, source_target_pairs={{0,1},{1,0},{2,3},{3,2},{4,5},{5,4},{6,7},{7,6},{8,9},{9,8},{10,11... | collective-permute-start | bytes 2359304 | tf_op jit(solution)/shard_map/window_core/ppermute | solution.py:304
  62.6 0.6 product.2
  63.2 1.3 %collective-permute-done.4.window = bf16[512,768]{1,0:T(8,128)(2,1)S(1)} collective-permute-done((bf16[512,768]{1,0:T(8,128)(2,1)S(1)}, bf16[512,768]{1,0:T(8,128)(2,1)S(1)}, u32[]{:S(2)}, u32[]{:S(2)}) %collective-permute-start.4) | collective-permute-done | bytes 786464 | tf_op jit(solution)/shard_map/window_core/ppermute | solution.py:304
  64.5 1.3 %product.3 = bf16[4,128,512]{2,1,0:T(8,128)(2,1)} custom-call(bf16[512,768]{1,0:T(8,128)(2,1)S(1)} %get-tuple-element.35.rest, bf16[512,768]{1,0:T(8,128)(2,1)S(1)} %collective-permute-done.4.window, f32[512,512]{1,0:T(8,128)S(1)} %get-tuple-element.36.first), custom_call_target="tpu_custom_call" | custom-call | flops 402653184 | bytes 3145728 | tf_op jit(solution)/shard_map/product/pallas_call | solution.py:206
  65.8 4.2 %all-to-all-start.2 = ((bf16[4,128,512]{2,1,0:T(8,128)(2,1)}), bf16[4,128,512]{2,1,0:T(8,128)(2,1)S(1)}, u32[]{:S(2)}, u32[]{:S(2)}) async-start(bf16[4,128,512]{2,1,0:T(8,128)(2,1)} %product.3), calls=%async_computation.2 | async-start | bytes 1048576 | tf_op jit(solution)/shard_map/sum_x/all_to_all | solution.py:331
  70.0 3.4 %momentum.3 = f32[1,16,6144]{2,1,0:T(8,128)} custom-call(f32[1,16,6144]{2,1,0:T(8,128)} %momentum.4, bf16[1,16,6144]{2,1,0:T(8,128)(2,1)} %gradient.3, s32[16,4,96]{2,1,0:T(4,128)} %bitcast.7, f32[128,128]{1,0:T(8,128)} %constant.2.clone.table), custom_call_target="tpu_custom_call" | custom-call | flops 49999998976 | bytes 1000000 | tf_op jit(solution)/shard_map/momentum/pallas_call | solution.py:291
  73.4 5.5 %all-to-all-done.2.parts = bf16[4,128,512]{2,1,0:T(8,128)(2,1)S(1)} async-done(((bf16[4,128,512]{2,1,0:T(8,128)(2,1)}), bf16[4,128,512]{2,1,0:T(8,128)(2,1)S(1)}, u32[]{:S(2)}, u32[]{:S(2)}) %all-to-all-start.2) | async-done | bytes 524320 | tf_op jit(solution)/shard_map/sum_x/all_to_all | solution.py:331
  78.9 0.7 sum_x.1
  (7 shorter events, 0.0 us)
Async XLA Ops:
  0.6 24.8 %copy-start.1 = (f32[128,128]{1,0:T(8,128)S(1)}, f32[128,128]{1,0:T(8,128)}, u32[]{:S(2)}) copy-start(f32[128,128]{1,0:T(8,128)} %constant.2.clone.table) | copy-start | bytes 196612
  0.6 24.8 %copy-start.2 = (bf16[16,6144]{1,0:T(8,128)(2,1)S(1)}, bf16[16,6144]{1,0:T(8,128)(2,1)}, u32[]{:S(2)}) copy-start(bf16[16,6144]{1,0:T(8,128)(2,1)} %weight.1) | copy-start | bytes 589828
  3.3 22.2 %all-to-all-start = ((bf16[16,16,384]{2,1,0:T(8,128)(2,1)}), bf16[16,16,384]{2,1,0:T(8,128)(2,1)S(1)}, u32[]{:S(2)}, u32[]{:S(2)}) async-start(bf16[16,16,384]{2,1,0:T(8,128)(2,1)} %coefficients.1), calls=%async_computation | async-start | bytes 393216 | tf_op jit(solution)/shard_map/exchange/all_to_all | solution.py:258
  17.4 19.8 %collective-permute-start = (bf16[3,128,768]{2,1,0:T(8,128)(2,1)}, bf16[3,128,768]{2,1,0:T(8,128)(2,1)S(1)}, u32[]{:S(2)}, u32[]{:S(2)}) collective-permute-start(bf16[3,128,768]{2,1,0:T(8,128)(2,1)} %get-tuple-element.23), channel_id=1, source_target_pairs={{0,16},{16,32},{32,48},{48,0},{64,80},{80,96},{96,112},{112,64},{1... | collective-permute-start | bytes 1769480 | tf_op jit(solution)/shard_map/tokens_x/ppermute | solution.py:272
  20.5 16.7 %collective-permute-start.1 = (bf16[3,128,768]{2,1,0:T(8,128)(2,1)}, bf16[3,128,768]{2,1,0:T(8,128)(2,1)S(1)}, u32[]{:S(2)}, u32[]{:S(2)}) collective-permute-start(bf16[3,128,768]{2,1,0:T(8,128)(2,1)} %get-tuple-element.24), channel_id=1, source_target_pairs={{0,48},{16,0},{32,16},{48,32},{64,112},{80,64},{96,80},{112,96},{1... | collective-permute-start | bytes 1769480 | tf_op jit(solution)/shard_map/tokens_x/ppermute | solution.py:273
  27.5 32.1 %all-to-all-start.1 = ((bf16[32,16,768]{2,1,0:T(8,128)(2,1)}), bf16[32,16,768]{2,1,0:T(8,128)(2,1)S(1)}, u32[]{:S(2)}, u32[]{:S(2)}) async-start(bf16[32,16,768]{2,1,0:T(8,128)(2,1)} %renew.1), calls=%async_computation.1 | async-start | bytes 1572864 | tf_op jit(solution)/shard_map/window/all_to_all | solution.py:301
  37.2 10.6 %copy-start = (bf16[128,6144]{1,0:T(8,128)(2,1)S(1)}, bf16[128,6144]{1,0:T(8,128)(2,1)}, u32[]{:S(2)}) copy-start(bf16[128,6144]{1,0:T(8,128)(2,1)} %tokens.1) | copy-start | bytes 4718596
  37.3 10.5 %collective-permute-start.2 = (bf16[1,128,768]{2,1,0:T(8,128)(2,1)S(1)}, bf16[1,128,768]{2,1,0:T(8,128)(2,1)S(1)}, u32[]{:S(2)}, u32[]{:S(2)}) collective-permute-start(bf16[1,128,768]{2,1,0:T(8,128)(2,1)S(1)} %get-tuple-element.25), channel_id=1, source_target_pairs={{0,16},{16,32},{32,48},{48,0},{64,80},{80,96},{96,112},{112,64},{1... | collective-permute-start | bytes 589832 | tf_op jit(solution)/shard_map/tokens_x/ppermute | solution.py:276
  40.6 10.0 %collective-permute-start.3 = (bf16[1,128,768]{2,1,0:T(8,128)(2,1)S(1)}, bf16[1,128,768]{2,1,0:T(8,128)(2,1)S(1)}, u32[]{:S(2)}, u32[]{:S(2)}) collective-permute-start(bf16[1,128,768]{2,1,0:T(8,128)(2,1)S(1)} %get-tuple-element.28), channel_id=1, source_target_pairs={{0,48},{16,0},{32,16},{48,32},{64,112},{80,64},{96,80},{112,96},{1... | collective-permute-start | bytes 589832 | tf_op jit(solution)/shard_map/tokens_x/ppermute | solution.py:277
  59.6 4.9 %collective-permute-start.4 = (bf16[512,768]{1,0:T(8,128)(2,1)S(1)}, bf16[512,768]{1,0:T(8,128)(2,1)S(1)}, u32[]{:S(2)}, u32[]{:S(2)}) collective-permute-start(bf16[512,768]{1,0:T(8,128)(2,1)S(1)} %bitcast.4), channel_id=1, source_target_pairs={{0,1},{1,0},{2,3},{3,2},{4,5},{5,4},{6,7},{7,6},{8,9},{9,8},{10,11... | collective-permute-start | bytes 2359304 | tf_op jit(solution)/shard_map/window_core/ppermute | solution.py:304
  65.8 13.1 %all-to-all-start.2 = ((bf16[4,128,512]{2,1,0:T(8,128)(2,1)}), bf16[4,128,512]{2,1,0:T(8,128)(2,1)S(1)}, u32[]{:S(2)}, u32[]{:S(2)}) async-start(bf16[4,128,512]{2,1,0:T(8,128)(2,1)} %product.3), calls=%async_computation.2 | async-start | bytes 1048576 | tf_op jit(solution)/shard_map/sum_x/all_to_all | solution.py:331

commit v7 on v6

--- a/solution.py
+++ b/solution.py
@@ -179,18 +179,12 @@
     rest[...] = stack(*blocks, 1 - core)
 
 
-def second_kernel(rest, window, first, out, ready, sems):
+def second_kernel(rest, window, first, out):
     x = lax.axis_index("shard") % XS
-    count = ready.shape[1]
-    copies = []
-    for i in range(0, XS, 2):
-        at = slice(i * count, (i + 2) * count)
-        total = first[at] + product(rest[at], window)
-        for d in range(i, i + 2):
-            ready[d] = total[(d - i) * count : (d - i + 1) * count].astype(BF16)
-            copies += fetch([(ready.at[d], out.at[(x + XS - d) % XS])], sems.at[pl.ds(d, 1)])
-    for copy in copies:
-        copy.wait()
+    count = out.shape[1]
+    total = first[...] + product(rest[...], window)
+    for d in range(XS):
+        out[(x + XS - d) % XS] = total[d * count : (d + 1) * count].astype(BF16)
 
 
 def finish_kernel(parts, out):
@@ -200,15 +194,14 @@
     out[...] = total.astype(BF16)
 
 
-def call(kernel, out, *args, flops=0, space=pltpu.VMEM, scratch=()):
+def call(kernel, out, *args, flops=0):
     out_list = jax.tree.leaves(out)
     moved = sum(a.size * a.dtype.itemsize for a in args) + sum(o.size * o.dtype.itemsize for o in out_list)
     return pl.pallas_call(
         kernel,
         out_shape=out,
         in_specs=[pl.BlockSpec(memory_space=pltpu.VMEM)] * len(args),
-        out_specs=jax.tree.map(lambda _: pl.BlockSpec(memory_space=space), out),
-        scratch_shapes=list(scratch),
+        out_specs=jax.tree.map(lambda _: pl.BlockSpec(memory_space=pltpu.VMEM), out),
         compiler_params=pltpu.CompilerParams(vmem_limit_bytes=20 * 1024 * 1024),
         cost_estimate=pl.CostEstimate(flops=flops, bytes_accessed=moved, transcendentals=0),
     )(*args)
@@ -273,6 +266,7 @@
         behind = lax.ppermute(behind, "shard", back)
         one = jax.ShapeDtypeStruct((1, count, piece), BF16)
         far0, far1 = call(forward_kernel, [one, one], ahead, behind, flops=5 * 10**10)
+        momentum, _ = lax.optimization_barrier((momentum, far0))
         far0 = lax.ppermute(far0, "shard", on)
         far1 = lax.ppermute(far1, "shard", back)
         tokens, far0 = lax.optimization_barrier((tokens, far0))
@@ -287,7 +281,6 @@
         )(tokens)
         blocks = (own, ahead, far0, far1, behind)
     with jax.named_scope("momentum"):
-        momentum, renewed = lax.optimization_barrier((momentum, renewed))
         new_momentum = pl.pallas_call(
             remain_kernel,
             out_shape=jax.ShapeDtypeStruct(momentum.shape, F32),
@@ -295,12 +288,12 @@
             out_specs=vmem,
             scratch_shapes=local_scratch + [pltpu.SemaphoreType.DMA((4,))],
             compiler_params=params,
-            cost_estimate=pl.CostEstimate(flops=5 * 10**10, bytes_accessed=10**6, transcendentals=0),
+            cost_estimate=pl.CostEstimate(flops=10**9, bytes_accessed=10**6, transcendentals=0),
         )(momentum, gradient, ordered_indices, table)
     with jax.named_scope("window"):
         window = lax.all_to_all(renewed, "shard", 0, 0).reshape(shards * rows, piece)
     with jax.named_scope("window_core"):
-        window, *blocks = lax.optimization_barrier((window, *blocks))
+        window, new_momentum, *blocks = lax.optimization_barrier((window, new_momentum, *blocks))
         other = lax.ppermute(window, "replica", [(i, i ^ 1) for i in range(replicas)])
     with jax.named_scope("product"):
         size = shards * rows
@@ -323,8 +316,6 @@
             other,
             first,
             flops=work,
-            space=pltpu.HBM,
-            scratch=(pltpu.VMEM(shape, BF16), pltpu.SemaphoreType.DMA((XS,))),
         )
     with jax.named_scope("sum_x"):
         groups = [[y * XS + i for i in range(XS)] for y in range(YS)]

time: 80.2 us -> 79 us (0.985)
  blocking collectives: 0 us -> 12.6 us
  waiting for transfers between devices: 23.9 us -> 13.4 us
  starting transfers between devices: 41.8 us -> 37.6 us
  Pallas kernels: 13.1 us -> 14 us
    all_to_all x0 -> x1, blocking collectives: none -> 12.6 us  [local(): parts = lax.all_to_all(ordered, 'shard', 0, 0, axis_index_groups=groups)]
    all_to_all x1 -> x0, waiting for transfers between devices: 5.49 us -> none  [local(): parts = lax.all_to_all(ordered, 'shard', 0, 0, axis_index_groups=groups)]
    all_to_all x1 -> x0, starting transfers between devices: 4.22 us -> none  [local(): parts = lax.all_to_all(ordered, 'shard', 0, 0, axis_index_groups=groups)]
    ppermute x1, waiting for transfers between devices: 2.68 us -> 0.16 us  [local(): far1 = lax.ppermute(far1, 'shard', back)]
    ppermute x1, waiting for transfers between devices: 3.9 us -> 2.53 us  [local(): far0 = lax.ppermute(far0, 'shard', on)]
    ppermute x1, waiting for transfers between devices: 1.28 us -> 0.35 us  [local(): lax.ppermute(window, 'replica', [(i, i ^ 1) for i in range(replicas)])]
    pallas_call x5, Pallas kernels: 4.72 us -> 5.64 us  [call(): pl.pallas_call(kernel, out_shape=out, in_specs=[pl.BlockSpec(memory_space...]
  transfers between devices with their start and end apart: 8 -> 7, of which waited for: 6 -> 5; matrix products, arithmetic and copies ran while one was open for 0% -> 0% of each run, Pallas kernels for 11% -> 13%
where the time goes in v7:
time: 79 us; the launch traced here: 78.4 us
  starting transfers between devices  37.6 us (48%)
  Pallas kernels  14 us (18%)
  waiting for transfers between devices  13.4 us (17%)
  blocking collectives  12.6 us (16%)
    all_to_all x1, blocking collectives, local(): parts = lax.all_to_all(ordered, 'shard', 0, 0, axis_index_groups=groups)  12.6 us
    all_to_all x1, starting transfers between devices, local(): received = lax.all_to_all(send, 'replica', 0, 0)  11.8 us
    all_to_all x1, starting transfers between devices, local(): lax.all_to_all(renewed, 'shard', 0, 0).reshape(shards * rows, piece)  9.67 us
    all_to_all x1, waiting for transfers between devices, local(): lax.all_to_all(renewed, 'shard', 0, 0).reshape(shards * rows, piece)  8.83 us
    pallas_call x5, Pallas kernels, call(): pl.pallas_call(kernel, out_shape=out, in_specs=[pl.BlockSpec(memory_space...  5.64 us
    ppermute x1, starting transfers between devices, local(): far1 = lax.ppermute(far1, 'shard', back)  3.49 us
    pallas_call x1, Pallas kernels, local(): pl.pallas_call(remain_kernel, out_shape=jax.ShapeDtypeStruct(momentum.sha...  3.4 us
    ppermute x1, starting transfers between devices, local(): behind = lax.ppermute(behind, 'shard', back)  3.37 us
  transfers between devices with their start and end apart: 7, of which 5 were waited for; matrix products, arithmetic and copies ran while one was open for 0% of the time, Pallas kernels for 13%

profile of v7, /device:TPU:1, one launch (start us, length us, event | category | flops | bytes accessed | tf_op | source)
XLA Modules:
  0.0 78.4 jit_solution(3488806415757032086)
XLA Ops:
  0.6 0.0 copy-start.1
  0.7 2.6 %coefficients.1 = bf16[16,16,384]{2,1,0:T(8,128)(2,1)} custom-call(f32[1,16,6144]{2,1,0:T(8,128)} %momentum.4, bf16[1,16,6144]{2,1,0:T(8,128)(2,1)} %gradient.3, s32[16,4,96]{2,1,0:T(4,128)} %bitcast.6, f32[128,128]{1,0:T(8,128)} %constant.2.clone.table), custom_call_target="tpu_custom_call" | custom-call | flops 100000000 | bytes 1000000 | tf_op jit(solution)/shard_map/coefficients/pallas_call | solution.py:229
  3.3 11.8 %all-to-all-start = ((bf16[16,16,384]{2,1,0:T(8,128)(2,1)}), bf16[16,16,384]{2,1,0:T(8,128)(2,1)S(1)}, u32[]{:S(2)}, u32[]{:S(2)}) async-start(bf16[16,16,384]{2,1,0:T(8,128)(2,1)} %coefficients.1), calls=%async_computation | async-start | bytes 393216 | tf_op jit(solution)/shard_map/exchange/all_to_all | solution.py:251
  15.1 2.3 %cut.1 = (bf16[3,128,768]{2,1,0:T(8,128)(2,1)}, bf16[3,128,768]{2,1,0:T(8,128)(2,1)}) custom-call(bf16[128,6144]{1,0:T(8,128)(2,1)} %tokens.1), custom_call_target="tpu_custom_call" | custom-call | bytes 3145728 | tf_op jit(solution)/shard_map/cut/pallas_call | solution.py:240
  17.4 3.1 %collective-permute-start = (bf16[3,128,768]{2,1,0:T(8,128)(2,1)}, bf16[3,128,768]{2,1,0:T(8,128)(2,1)S(1)}, u32[]{:S(2)}, u32[]{:S(2)}) collective-permute-start(bf16[3,128,768]{2,1,0:T(8,128)(2,1)} %get-tuple-element.22), channel_id=1, source_target_pairs={{0,16},{16,32},{32,48},{48,0},{64,80},{80,96},{96,112},{112,64},{1... | collective-permute-start | bytes 1769480 | tf_op jit(solution)/shard_map/tokens_x/ppermute | solution.py:265
  20.5 3.4 %collective-permute-start.1 = (bf16[3,128,768]{2,1,0:T(8,128)(2,1)}, bf16[3,128,768]{2,1,0:T(8,128)(2,1)S(1)}, u32[]{:S(2)}, u32[]{:S(2)}) collective-permute-start(bf16[3,128,768]{2,1,0:T(8,128)(2,1)} %get-tuple-element.23), channel_id=1, source_target_pairs={{0,48},{16,0},{32,16},{48,32},{64,112},{80,64},{96,80},{112,96},{1... | collective-permute-start | bytes 1769480 | tf_op jit(solution)/shard_map/tokens_x/ppermute | solution.py:266
  23.9 1.5 %all-to-all-done.received = bf16[16,16,384]{2,1,0:T(8,128)(2,1)S(1)} async-done(((bf16[16,16,384]{2,1,0:T(8,128)(2,1)}), bf16[16,16,384]{2,1,0:T(8,128)(2,1)S(1)}, u32[]{:S(2)}, u32[]{:S(2)}) %all-to-all-start) | async-done | bytes 196640 | tf_op jit(solution)/shard_map/exchange/all_to_all | solution.py:251
  25.5 2.1 %renew.1 = bf16[32,16,768]{2,1,0:T(8,128)(2,1)} custom-call(bf16[16,16,384]{2,1,0:T(8,128)(2,1)S(1)} %all-to-all-done.received, bf16[16,6144]{1,0:T(8,128)(2,1)S(1)} %copy-done.2, f32[128,128]{1,0:T(8,128)S(1)} %copy-done.1), custom_call_target="tpu_custom_call" | custom-call | flops 10000000000 | bytes 1245184 | tf_op jit(solution)/shard_map/renew/pallas_call | solution.py:200
  27.5 9.7 %all-to-all-start.1 = ((bf16[32,16,768]{2,1,0:T(8,128)(2,1)}), bf16[32,16,768]{2,1,0:T(8,128)(2,1)S(1)}, u32[]{:S(2)}, u32[]{:S(2)}) async-start(bf16[32,16,768]{2,1,0:T(8,128)(2,1)} %renew.1), calls=%async_computation.1 | async-start | bytes 1572864 | tf_op jit(solution)/shard_map/window/all_to_all | solution.py:294
  37.2 0.7 tokens_x.2
  38.0 3.1 %collective-permute-start.2 = (bf16[1,128,768]{2,1,0:T(8,128)(2,1)S(1)}, bf16[1,128,768]{2,1,0:T(8,128)(2,1)S(1)}, u32[]{:S(2)}, u32[]{:S(2)}) collective-permute-start(bf16[1,128,768]{2,1,0:T(8,128)(2,1)S(1)} %get-tuple-element.24), channel_id=1, source_target_pairs={{0,16},{16,32},{32,48},{48,0},{64,80},{80,96},{96,112},{112,64},{1... | collective-permute-start | bytes 589832 | tf_op jit(solution)/shard_map/tokens_x/ppermute | solution.py:270
  41.1 0.0 copy-start
  41.1 3.5 %collective-permute-start.3 = (bf16[1,128,768]{2,1,0:T(8,128)(2,1)}, bf16[1,128,768]{2,1,0:T(8,128)(2,1)}, u32[]{:S(2)}, u32[]{:S(2)}) collective-permute-start(bf16[1,128,768]{2,1,0:T(8,128)(2,1)} %get-tuple-element.28), channel_id=1, source_target_pairs={{0,48},{16,0},{32,16},{48,32},{64,112},{80,64},{96,80},{112,96},{1... | collective-permute-start | bytes 589832 | tf_op jit(solution)/shard_map/tokens_x/ppermute | solution.py:271
  44.6 3.4 %momentum.3 = f32[1,16,6144]{2,1,0:T(8,128)} custom-call(f32[1,16,6144]{2,1,0:T(8,128)} %momentum.4, bf16[1,16,6144]{2,1,0:T(8,128)(2,1)} %gradient.3, s32[16,4,96]{2,1,0:T(4,128)} %bitcast.7, f32[128,128]{1,0:T(8,128)} %constant.2.clone.table), custom_call_target="tpu_custom_call" | custom-call | flops 1000000000 | bytes 1000000 | tf_op jit(solution)/shard_map/momentum/pallas_call | solution.py:284
  48.0 2.5 %collective-permute-done.2.refs_2_ = bf16[1,128,768]{2,1,0:T(8,128)(2,1)S(1)} collective-permute-done((bf16[1,128,768]{2,1,0:T(8,128)(2,1)S(1)}, bf16[1,128,768]{2,1,0:T(8,128)(2,1)S(1)}, u32[]{:S(2)}, u32[]{:S(2)}) %collective-permute-start.2) | collective-permute-done | bytes 196640 | tf_op jit(solution)/shard_map/tokens_x/ppermute | solution.py:270
  50.5 0.1 tokens_x.3.refs_0_
  50.6 0.2 collective-permute-done.3.refs_3_
  50.8 8.8 %all-to-all-done.1 = bf16[32,16,768]{2,1,0:T(8,128)(2,1)S(1)} async-done(((bf16[32,16,768]{2,1,0:T(8,128)(2,1)}), bf16[32,16,768]{2,1,0:T(8,128)(2,1)S(1)}, u32[]{:S(2)}, u32[]{:S(2)}) %all-to-all-start.1) | async-done | bytes 786464 | tf_op jit(solution)/shard_map/window/all_to_all | solution.py:294
  59.6 3.0 %collective-permute-start.4 = (bf16[512,768]{1,0:T(8,128)(2,1)S(1)}, bf16[512,768]{1,0:T(8,128)(2,1)S(1)}, u32[]{:S(2)}, u32[]{:S(2)}) collective-permute-start(bf16[512,768]{1,0:T(8,128)(2,1)S(1)} %bitcast.4), channel_id=1, source_target_pairs={{0,1},{1,0},{2,3},{3,2},{4,5},{5,4},{6,7},{7,6},{8,9},{9,8},{10,11... | collective-permute-start | bytes 2359304 | tf_op jit(solution)/shard_map/window_core/ppermute | solution.py:297
  62.6 1.5 %product.2 = (f32[512,512]{1,0:T(8,128)S(1)}, bf16[512,768]{1,0:T(8,128)(2,1)S(1)}) custom-call(bf16[2,128,768]{2,1,0:T(8,128)(2,1)S(1)} %tokens_x.3.refs_0_, bf16[3,128,768]{2,1,0:T(8,128)(2,1)S(1)} %collective-permute-done.ahead.refs_1_, bf16[1,128,768]{2,1,0:T(8,128)(2,1)S(1)} %collective-permute-done.2.refs_2_, ...), custom_call_target="tpu_custom_call" | custom-call | flops 402653184 | bytes 4587520 | tf_op jit(solution)/shard_map/product/pallas_call | solution.py:200
  64.1 0.3 collective-permute-done.4.window
  64.5 0.6 product.3
  65.1 12.6 %all_to_all.15.parts = bf16[4,128,512]{2,1,0:T(8,128)(2,1)S(1)} all-to-all(bf16[4,128,512]{2,1,0:T(8,128)(2,1)S(1)} %product.3), channel_id=1, replica_groups={{0,16,32,48},{64,80,96,112},{128,144,160,176},{192,208,224,240},{256,27..., dimensions={0} | all-to-all | bytes 1048576 | tf_op jit(solution)/shard_map/sum_x/all_to_all | solution.py:322
  77.7 0.7 sum_x.1
  (6 shorter events, 0.0 us)
Async XLA Ops:
  0.6 24.8 %copy-start.1 = (f32[128,128]{1,0:T(8,128)S(1)}, f32[128,128]{1,0:T(8,128)}, u32[]{:S(2)}) copy-start(f32[128,128]{1,0:T(8,128)} %constant.2.clone.table) | copy-start | bytes 196612
  0.6 24.8 %copy-start.2 = (bf16[16,6144]{1,0:T(8,128)(2,1)S(1)}, bf16[16,6144]{1,0:T(8,128)(2,1)}, u32[]{:S(2)}) copy-start(bf16[16,6144]{1,0:T(8,128)(2,1)} %weight.1) | copy-start | bytes 589828
  3.3 22.2 %all-to-all-start = ((bf16[16,16,384]{2,1,0:T(8,128)(2,1)}), bf16[16,16,384]{2,1,0:T(8,128)(2,1)S(1)}, u32[]{:S(2)}, u32[]{:S(2)}) async-start(bf16[16,16,384]{2,1,0:T(8,128)(2,1)} %coefficients.1), calls=%async_computation | async-start | bytes 393216 | tf_op jit(solution)/shard_map/exchange/all_to_all | solution.py:251
  17.4 19.8 %collective-permute-start = (bf16[3,128,768]{2,1,0:T(8,128)(2,1)}, bf16[3,128,768]{2,1,0:T(8,128)(2,1)S(1)}, u32[]{:S(2)}, u32[]{:S(2)}) collective-permute-start(bf16[3,128,768]{2,1,0:T(8,128)(2,1)} %get-tuple-element.22), channel_id=1, source_target_pairs={{0,16},{16,32},{32,48},{48,0},{64,80},{80,96},{96,112},{112,64},{1... | collective-permute-start | bytes 1769480 | tf_op jit(solution)/shard_map/tokens_x/ppermute | solution.py:265
  20.5 16.7 %collective-permute-start.1 = (bf16[3,128,768]{2,1,0:T(8,128)(2,1)}, bf16[3,128,768]{2,1,0:T(8,128)(2,1)S(1)}, u32[]{:S(2)}, u32[]{:S(2)}) collective-permute-start(bf16[3,128,768]{2,1,0:T(8,128)(2,1)} %get-tuple-element.23), channel_id=1, source_target_pairs={{0,48},{16,0},{32,16},{48,32},{64,112},{80,64},{96,80},{112,96},{1... | collective-permute-start | bytes 1769480 | tf_op jit(solution)/shard_map/tokens_x/ppermute | solution.py:266
  27.5 32.1 %all-to-all-start.1 = ((bf16[32,16,768]{2,1,0:T(8,128)(2,1)}), bf16[32,16,768]{2,1,0:T(8,128)(2,1)S(1)}, u32[]{:S(2)}, u32[]{:S(2)}) async-start(bf16[32,16,768]{2,1,0:T(8,128)(2,1)} %renew.1), calls=%async_computation.1 | async-start | bytes 1572864 | tf_op jit(solution)/shard_map/window/all_to_all | solution.py:294
  38.0 12.6 %collective-permute-start.2 = (bf16[1,128,768]{2,1,0:T(8,128)(2,1)S(1)}, bf16[1,128,768]{2,1,0:T(8,128)(2,1)S(1)}, u32[]{:S(2)}, u32[]{:S(2)}) collective-permute-start(bf16[1,128,768]{2,1,0:T(8,128)(2,1)S(1)} %get-tuple-element.24), channel_id=1, source_target_pairs={{0,16},{16,32},{32,48},{48,0},{64,80},{80,96},{96,112},{112,64},{1... | collective-permute-start | bytes 589832 | tf_op jit(solution)/shard_map/tokens_x/ppermute | solution.py:270
  41.1 9.5 %copy-start = (bf16[128,6144]{1,0:T(8,128)(2,1)S(1)}, bf16[128,6144]{1,0:T(8,128)(2,1)}, u32[]{:S(2)}) copy-start(bf16[128,6144]{1,0:T(8,128)(2,1)} %tokens.1) | copy-start | bytes 4718596
  41.1 9.7 %collective-permute-start.3 = (bf16[1,128,768]{2,1,0:T(8,128)(2,1)}, bf16[1,128,768]{2,1,0:T(8,128)(2,1)}, u32[]{:S(2)}, u32[]{:S(2)}) collective-permute-start(bf16[1,128,768]{2,1,0:T(8,128)(2,1)} %get-tuple-element.28), channel_id=1, source_target_pairs={{0,48},{16,0},{32,16},{48,32},{64,112},{80,64},{96,80},{112,96},{1... | collective-permute-start | bytes 589832 | tf_op jit(solution)/shard_map/tokens_x/ppermute | solution.py:271
  59.6 4.9 %collective-permute-start.4 = (bf16[512,768]{1,0:T(8,128)(2,1)S(1)}, bf16[512,768]{1,0:T(8,128)(2,1)S(1)}, u32[]{:S(2)}, u32[]{:S(2)}) collective-permute-start(bf16[512,768]{1,0:T(8,128)(2,1)S(1)} %bitcast.4), channel_id=1, source_target_pairs={{0,1},{1,0},{2,3},{3,2},{4,5},{5,4},{6,7},{7,6},{8,9},{9,8},{10,11... | collective-permute-start | bytes 2359304 | tf_op jit(solution)/shard_map/window_core/ppermute | solution.py:297

commit v8 on v7

--- a/solution.py
+++ b/solution.py
@@ -287,7 +287,7 @@
             in_specs=[hbm] * 4,
             out_specs=vmem,
             scratch_shapes=local_scratch + [pltpu.SemaphoreType.DMA((4,))],
-            compiler_params=params,
+            compiler_params=pltpu.CompilerParams(vmem_limit_bytes=40 * 1024 * 1024),
             cost_estimate=pl.CostEstimate(flops=10**9, bytes_accessed=10**6, transcendentals=0),
         )(momentum, gradient, ordered_indices, table)
     with jax.named_scope("window"):

time: 79 us -> 78.9 us (level)
  Pallas kernels: 14 us -> 11.9 us
  waiting for transfers between devices: 13.4 us -> 15.3 us
    ppermute x1, waiting for transfers between devices: 0.16 us -> 2.55 us  [local(): far1 = lax.ppermute(far1, 'shard', back)]
    ppermute x1, waiting for transfers between devices: 2.53 us -> 0.89 us  [local(): far0 = lax.ppermute(far0, 'shard', on)]
    pallas_call x5, Pallas kernels: 5.64 us -> 4.01 us  [call(): pl.pallas_call(kernel, out_shape=out, in_specs=[pl.BlockSpec(memory_space...]
    ppermute x1, waiting for transfers between devices: 0.35 us -> 1.28 us  [local(): lax.ppermute(window, 'replica', [(i, i ^ 1) for i in range(replicas)])]
  transfers between devices with their start and end apart: 7 -> 7, of which waited for: 5 -> 5; matrix products, arithmetic and copies ran while one was open for 0% -> 0% of each run, Pallas kernels for 13% -> 10%
where the time goes in v8:
time: 78.9 us; the launch traced here: 78.4 us
  starting transfers between devices  37.7 us (48%)
  waiting for transfers between devices  15.3 us (19%)
  blocking collectives  12.6 us (16%)
  Pallas kernels  11.9 us (15%)
  between operations  0.82 us (1%)
    all_to_all x1, blocking collectives, local(): parts = lax.all_to_all(ordered, 'shard', 0, 0, axis_index_groups=groups)  12.6 us
    all_to_all x1, starting transfers between devices, local(): received = lax.all_to_all(send, 'replica', 0, 0)  11.8 us
    all_to_all x1, starting transfers between devices, local(): lax.all_to_all(renewed, 'shard', 0, 0).reshape(shards * rows, piece)  9.67 us
    all_to_all x1, waiting for transfers between devices, local(): lax.all_to_all(renewed, 'shard', 0, 0).reshape(shards * rows, piece)  9.05 us
    pallas_call x5, Pallas kernels, call(): pl.pallas_call(kernel, out_shape=out, in_specs=[pl.BlockSpec(memory_space...  4.01 us
    ppermute x1, starting transfers between devices, local(): far1 = lax.ppermute(far1, 'shard', back)  3.49 us
    ppermute x1, starting transfers between devices, local(): behind = lax.ppermute(behind, 'shard', back)  3.37 us
    ppermute x1, starting transfers between devices, local(): far0 = lax.ppermute(far0, 'shard', on)  3.27 us
  transfers between devices with their start and end apart: 7, of which 5 were waited for; matrix products, arithmetic and copies ran while one was open for 0% of the time, Pallas kernels for 10%

profile of v8, /device:TPU:1, one launch (start us, length us, event | category | flops | bytes accessed | tf_op | source)
XLA Modules:
  0.0 78.4 jit_solution(15400431517179044558)
XLA Ops:
  0.6 0.0 copy-start.3
  0.7 2.6 %coefficients.1 = bf16[16,16,384]{2,1,0:T(8,128)(2,1)} custom-call(f32[1,16,6144]{2,1,0:T(8,128)} %momentum.4, bf16[1,16,6144]{2,1,0:T(8,128)(2,1)} %gradient.3, s32[16,4,96]{2,1,0:T(4,128)} %bitcast.6, f32[128,128]{1,0:T(8,128)} %constant.2.clone.table), custom_call_target="tpu_custom_call" | custom-call | flops 100000000 | bytes 1000000 | tf_op jit(solution)/shard_map/coefficients/pallas_call | solution.py:229
  3.3 11.8 %all-to-all-start = ((bf16[16,16,384]{2,1,0:T(8,128)(2,1)}), bf16[16,16,384]{2,1,0:T(8,128)(2,1)S(1)}, u32[]{:S(2)}, u32[]{:S(2)}) async-start(bf16[16,16,384]{2,1,0:T(8,128)(2,1)} %coefficients.1), calls=%async_computation | async-start | bytes 393216 | tf_op jit(solution)/shard_map/exchange/all_to_all | solution.py:251
  15.1 2.2 %cut.1 = (bf16[3,128,768]{2,1,0:T(8,128)(2,1)}, bf16[3,128,768]{2,1,0:T(8,128)(2,1)}) custom-call(bf16[128,6144]{1,0:T(8,128)(2,1)} %tokens.1), custom_call_target="tpu_custom_call" | custom-call | bytes 3145728 | tf_op jit(solution)/shard_map/cut/pallas_call | solution.py:240
  17.4 3.1 %collective-permute-start = (bf16[3,128,768]{2,1,0:T(8,128)(2,1)}, bf16[3,128,768]{2,1,0:T(8,128)(2,1)S(1)}, u32[]{:S(2)}, u32[]{:S(2)}) collective-permute-start(bf16[3,128,768]{2,1,0:T(8,128)(2,1)} %get-tuple-element.22), channel_id=1, source_target_pairs={{0,16},{16,32},{32,48},{48,0},{64,80},{80,96},{96,112},{112,64},{1... | collective-permute-start | bytes 1769480 | tf_op jit(solution)/shard_map/tokens_x/ppermute | solution.py:265
  20.5 3.4 %collective-permute-start.1 = (bf16[3,128,768]{2,1,0:T(8,128)(2,1)}, bf16[3,128,768]{2,1,0:T(8,128)(2,1)S(1)}, u32[]{:S(2)}, u32[]{:S(2)}) collective-permute-start(bf16[3,128,768]{2,1,0:T(8,128)(2,1)} %get-tuple-element.23), channel_id=1, source_target_pairs={{0,48},{16,0},{32,16},{48,32},{64,112},{80,64},{96,80},{112,96},{1... | collective-permute-start | bytes 1769480 | tf_op jit(solution)/shard_map/tokens_x/ppermute | solution.py:266
  23.9 1.6 %all-to-all-done.received = bf16[16,16,384]{2,1,0:T(8,128)(2,1)S(1)} async-done(((bf16[16,16,384]{2,1,0:T(8,128)(2,1)}), bf16[16,16,384]{2,1,0:T(8,128)(2,1)S(1)}, u32[]{:S(2)}, u32[]{:S(2)}) %all-to-all-start) | async-done | bytes 196640 | tf_op jit(solution)/shard_map/exchange/all_to_all | solution.py:251
  25.5 2.0 %renew.1 = bf16[32,16,768]{2,1,0:T(8,128)(2,1)} custom-call(bf16[16,16,384]{2,1,0:T(8,128)(2,1)S(1)} %all-to-all-done.received, bf16[16,6144]{1,0:T(8,128)(2,1)S(1)} %copy-done.5, f32[128,128]{1,0:T(8,128)S(1)} %copy-done.3), custom_call_target="tpu_custom_call" | custom-call | flops 10000000000 | bytes 1245184 | tf_op jit(solution)/shard_map/renew/pallas_call | solution.py:200
  27.5 9.7 %all-to-all-start.1 = ((bf16[32,16,768]{2,1,0:T(8,128)(2,1)}), bf16[32,16,768]{2,1,0:T(8,128)(2,1)S(1)}, u32[]{:S(2)}, u32[]{:S(2)}) async-start(bf16[32,16,768]{2,1,0:T(8,128)(2,1)} %renew.1), calls=%async_computation.1 | async-start | bytes 1572864 | tf_op jit(solution)/shard_map/window/all_to_all | solution.py:294
  37.2 0.0 copy-start.1
  37.2 0.0 copy-start.4
  37.3 3.3 %collective-permute-start.2 = (bf16[1,128,768]{2,1,0:T(8,128)(2,1)S(1)}, bf16[1,128,768]{2,1,0:T(8,128)(2,1)S(1)}, u32[]{:S(2)}, u32[]{:S(2)}) collective-permute-start(bf16[1,128,768]{2,1,0:T(8,128)(2,1)S(1)} %get-tuple-element.24), channel_id=1, source_target_pairs={{0,16},{16,32},{32,48},{48,0},{64,80},{80,96},{96,112},{112,64},{1... | collective-permute-start | bytes 589832 | tf_op jit(solution)/shard_map/tokens_x/ppermute | solution.py:270
  40.6 3.5 %collective-permute-start.3 = (bf16[1,128,768]{2,1,0:T(8,128)(2,1)S(1)}, bf16[1,128,768]{2,1,0:T(8,128)(2,1)S(1)}, u32[]{:S(2)}, u32[]{:S(2)}) collective-permute-start(bf16[1,128,768]{2,1,0:T(8,128)(2,1)S(1)} %get-tuple-element.28), channel_id=1, source_target_pairs={{0,48},{16,0},{32,16},{48,32},{64,112},{80,64},{96,80},{112,96},{1... | collective-permute-start | bytes 589832 | tf_op jit(solution)/shard_map/tokens_x/ppermute | solution.py:271
  44.1 2.9 %momentum.3 = f32[1,16,6144]{2,1,0:T(8,128)} custom-call(f32[1,16,6144]{2,1,0:T(8,128)S(1)} %copy-done.1, bf16[1,16,6144]{2,1,0:T(8,128)(2,1)S(1)} %copy-done.2, s32[16,4,96]{2,1,0:T(4,128)S(1)} %bitcast.7, f32[128,128]{1,0:T(8,128)S(1)} %copy-done.3), custom_call_target="tpu_custom_call" | custom-call | flops 1000000000 | bytes 1000000 | tf_op jit(solution)/shard_map/momentum/pallas_call | solution.py:284
  47.0 0.9 %collective-permute-done.2.refs_2_ = bf16[1,128,768]{2,1,0:T(8,128)(2,1)S(1)} collective-permute-done((bf16[1,128,768]{2,1,0:T(8,128)(2,1)S(1)}, bf16[1,128,768]{2,1,0:T(8,128)(2,1)S(1)}, u32[]{:S(2)}, u32[]{:S(2)}) %collective-permute-start.2) | collective-permute-done | bytes 196640 | tf_op jit(solution)/shard_map/tokens_x/ppermute | solution.py:270
  47.9 0.1 tokens_x.3.refs_0_
  48.0 2.6 %collective-permute-done.3.refs_3_ = bf16[1,128,768]{2,1,0:T(8,128)(2,1)S(1)} collective-permute-done((bf16[1,128,768]{2,1,0:T(8,128)(2,1)S(1)}, bf16[1,128,768]{2,1,0:T(8,128)(2,1)S(1)}, u32[]{:S(2)}, u32[]{:S(2)}) %collective-permute-start.3) | collective-permute-done | bytes 196640 | tf_op jit(solution)/shard_map/tokens_x/ppermute | solution.py:271
  50.6 9.1 %all-to-all-done.1 = bf16[32,16,768]{2,1,0:T(8,128)(2,1)S(1)} async-done(((bf16[32,16,768]{2,1,0:T(8,128)(2,1)}), bf16[32,16,768]{2,1,0:T(8,128)(2,1)S(1)}, u32[]{:S(2)}, u32[]{:S(2)}) %all-to-all-start.1) | async-done | bytes 786464 | tf_op jit(solution)/shard_map/window/all_to_all | solution.py:294
  59.6 3.0 %collective-permute-start.4 = (bf16[512,768]{1,0:T(8,128)(2,1)S(1)}, bf16[512,768]{1,0:T(8,128)(2,1)S(1)}, u32[]{:S(2)}, u32[]{:S(2)}) collective-permute-start(bf16[512,768]{1,0:T(8,128)(2,1)S(1)} %bitcast.4), channel_id=1, source_target_pairs={{0,1},{1,0},{2,3},{3,2},{4,5},{5,4},{6,7},{7,6},{8,9},{9,8},{10,11... | collective-permute-start | bytes 2359304 | tf_op jit(solution)/shard_map/window_core/ppermute | solution.py:297
  62.6 0.6 product.2
  63.2 1.3 %collective-permute-done.4.window = bf16[512,768]{1,0:T(8,128)(2,1)S(1)} collective-permute-done((bf16[512,768]{1,0:T(8,128)(2,1)S(1)}, bf16[512,768]{1,0:T(8,128)(2,1)S(1)}, u32[]{:S(2)}, u32[]{:S(2)}) %collective-permute-start.4) | collective-permute-done | bytes 786464 | tf_op jit(solution)/shard_map/window_core/ppermute | solution.py:297
  64.5 0.6 product.3
  65.1 12.6 %all_to_all.15.parts = bf16[4,128,512]{2,1,0:T(8,128)(2,1)S(1)} all-to-all(bf16[4,128,512]{2,1,0:T(8,128)(2,1)S(1)} %product.3), channel_id=1, replica_groups={{0,16,32,48},{64,80,96,112},{128,144,160,176},{192,208,224,240},{256,27..., dimensions={0} | all-to-all | bytes 1048576 | tf_op jit(solution)/shard_map/sum_x/all_to_all | solution.py:322
  77.7 0.7 sum_x.1
  (12 shorter events, 0.1 us)
Async XLA Ops:
  0.6 24.8 %copy-start.3 = (f32[128,128]{1,0:T(8,128)S(1)}, f32[128,128]{1,0:T(8,128)}, u32[]{:S(2)}) copy-start(f32[128,128]{1,0:T(8,128)} %constant.2.clone.table) | copy-start | bytes 196612
  0.6 24.8 %copy-start.5 = (bf16[16,6144]{1,0:T(8,128)(2,1)S(1)}, bf16[16,6144]{1,0:T(8,128)(2,1)}, u32[]{:S(2)}) copy-start(bf16[16,6144]{1,0:T(8,128)(2,1)} %weight.1) | copy-start | bytes 589828
  3.3 22.2 %all-to-all-start = ((bf16[16,16,384]{2,1,0:T(8,128)(2,1)}), bf16[16,16,384]{2,1,0:T(8,128)(2,1)S(1)}, u32[]{:S(2)}, u32[]{:S(2)}) async-start(bf16[16,16,384]{2,1,0:T(8,128)(2,1)} %coefficients.1), calls=%async_computation | async-start | bytes 393216 | tf_op jit(solution)/shard_map/exchange/all_to_all | solution.py:251
  17.4 19.8 %collective-permute-start = (bf16[3,128,768]{2,1,0:T(8,128)(2,1)}, bf16[3,128,768]{2,1,0:T(8,128)(2,1)S(1)}, u32[]{:S(2)}, u32[]{:S(2)}) collective-permute-start(bf16[3,128,768]{2,1,0:T(8,128)(2,1)} %get-tuple-element.22), channel_id=1, source_target_pairs={{0,16},{16,32},{32,48},{48,0},{64,80},{80,96},{96,112},{112,64},{1... | collective-permute-start | bytes 1769480 | tf_op jit(solution)/shard_map/tokens_x/ppermute | solution.py:265
  20.5 16.7 %collective-permute-start.1 = (bf16[3,128,768]{2,1,0:T(8,128)(2,1)}, bf16[3,128,768]{2,1,0:T(8,128)(2,1)S(1)}, u32[]{:S(2)}, u32[]{:S(2)}) collective-permute-start(bf16[3,128,768]{2,1,0:T(8,128)(2,1)} %get-tuple-element.23), channel_id=1, source_target_pairs={{0,48},{16,0},{32,16},{48,32},{64,112},{80,64},{96,80},{112,96},{1... | collective-permute-start | bytes 1769480 | tf_op jit(solution)/shard_map/tokens_x/ppermute | solution.py:266
  27.5 32.1 %all-to-all-start.1 = ((bf16[32,16,768]{2,1,0:T(8,128)(2,1)}), bf16[32,16,768]{2,1,0:T(8,128)(2,1)S(1)}, u32[]{:S(2)}, u32[]{:S(2)}) async-start(bf16[32,16,768]{2,1,0:T(8,128)(2,1)} %renew.1), calls=%async_computation.1 | async-start | bytes 1572864 | tf_op jit(solution)/shard_map/window/all_to_all | solution.py:294
  37.2 6.9 %copy-start.1 = (f32[1,16,6144]{2,1,0:T(8,128)S(1)}, f32[1,16,6144]{2,1,0:T(8,128)}, u32[]{:S(2)}) copy-start(f32[1,16,6144]{2,1,0:T(8,128)} %momentum.4) | copy-start | bytes 1179652
  37.2 6.9 %copy-start.2 = (bf16[1,16,6144]{2,1,0:T(8,128)(2,1)S(1)}, bf16[1,16,6144]{2,1,0:T(8,128)(2,1)}, u32[]{:S(2)}) copy-start(bf16[1,16,6144]{2,1,0:T(8,128)(2,1)} %gradient.3) | copy-start | bytes 589828
  37.2 6.9 %copy-start.4 = (s32[1,16,96,4]{2,3,1,0:T(4,128)S(1)}, s32[1,16,96,4]{2,3,1,0:T(4,128)}, u32[]{:S(2)}) copy-start(s32[1,16,96,4]{2,3,1,0:T(4,128)} %param.10) | copy-start | bytes 73732
  37.3 10.6 %collective-permute-start.2 = (bf16[1,128,768]{2,1,0:T(8,128)(2,1)S(1)}, bf16[1,128,768]{2,1,0:T(8,128)(2,1)S(1)}, u32[]{:S(2)}, u32[]{:S(2)}) collective-permute-start(bf16[1,128,768]{2,1,0:T(8,128)(2,1)S(1)} %get-tuple-element.24), channel_id=1, source_target_pairs={{0,16},{16,32},{32,48},{48,0},{64,80},{80,96},{96,112},{112,64},{1... | collective-permute-start | bytes 589832 | tf_op jit(solution)/shard_map/tokens_x/ppermute | solution.py:270
  40.6 7.3 %copy-start = (bf16[128,6144]{1,0:T(8,128)(2,1)S(1)}, bf16[128,6144]{1,0:T(8,128)(2,1)}, u32[]{:S(2)}) copy-start(bf16[128,6144]{1,0:T(8,128)(2,1)} %tokens.1) | copy-start | bytes 4718596
  40.6 10.0 %collective-permute-start.3 = (bf16[1,128,768]{2,1,0:T(8,128)(2,1)S(1)}, bf16[1,128,768]{2,1,0:T(8,128)(2,1)S(1)}, u32[]{:S(2)}, u32[]{:S(2)}) collective-permute-start(bf16[1,128,768]{2,1,0:T(8,128)(2,1)S(1)} %get-tuple-element.28), channel_id=1, source_target_pairs={{0,48},{16,0},{32,16},{48,32},{64,112},{80,64},{96,80},{112,96},{1... | collective-permute-start | bytes 589832 | tf_op jit(solution)/shard_map/tokens_x/ppermute | solution.py:271
  59.6 4.9 %collective-permute-start.4 = (bf16[512,768]{1,0:T(8,128)(2,1)S(1)}, bf16[512,768]{1,0:T(8,128)(2,1)S(1)}, u32[]{:S(2)}, u32[]{:S(2)}) collective-permute-start(bf16[512,768]{1,0:T(8,128)(2,1)S(1)} %bitcast.4), channel_id=1, source_target_pairs={{0,1},{1,0},{2,3},{3,2},{4,5},{5,4},{6,7},{7,6},{8,9},{9,8},{10,11... | collective-permute-start | bytes 2359304 | tf_op jit(solution)/shard_map/window_core/ppermute | solution.py:297

commit v9 on v8

--- a/solution.py
+++ b/solution.py
@@ -36,9 +36,8 @@
     return lax.dot_general(a, b, (((da,), (db,)), ((), ())), precision=HIGH, preferred_element_type=F32)
 
 
-def forward_kernel(ahead, behind, far0, far1):
-    far0[0] = ahead[2]
-    far1[0] = behind[2]
+def forward_kernel(arrived, far):
+    far[0] = arrived[2]
 
 
 def own_kernel(tokens, own, sems):
@@ -265,8 +264,8 @@
         ahead = lax.ppermute(ahead, "shard", on)
         behind = lax.ppermute(behind, "shard", back)
         one = jax.ShapeDtypeStruct((1, count, piece), BF16)
-        far0, far1 = call(forward_kernel, [one, one], ahead, behind, flops=5 * 10**10)
-        momentum, _ = lax.optimization_barrier((momentum, far0))
+        far0, far1 = (call(forward_kernel, one, arrived, flops=5 * 10**10) for arrived in (ahead, behind))
+        momentum, _ = lax.optimization_barrier((momentum, far1))
         far0 = lax.ppermute(far0, "shard", on)
         far1 = lax.ppermute(far1, "shard", back)
         tokens, far0 = lax.optimization_barrier((tokens, far0))

time: 78.9 us -> 78.9 us (level)
    ppermute x1, waiting for transfers between devices: 2.55 us -> 0.01 us  [local(): far1 = lax.ppermute(far1, 'shard', back)]
    ppermute x1, waiting for transfers between devices: 0.01 us -> 2.38 us  [local(): ahead = lax.ppermute(ahead, 'shard', on)]
    ppermute x1, waiting for transfers between devices: 0.89 us -> 2.97 us  [local(): far0 = lax.ppermute(far0, 'shard', on)]
    all_to_all x1, waiting for transfers between devices: 9.05 us -> 7.14 us  [local(): lax.all_to_all(renewed, 'shard', 0, 0).reshape(shards * rows, piece)]
    ppermute x1, starting transfers between devices: 3.27 us -> 2.05 us  [local(): far0 = lax.ppermute(far0, 'shard', on)]
    ppermute x1, starting transfers between devices: 3.49 us -> 4.7 us  [local(): far1 = lax.ppermute(far1, 'shard', back)]
    ppermute x1, starting transfers between devices: 3.13 us -> 1.92 us  [local(): ahead = lax.ppermute(ahead, 'shard', on)]
    ppermute x1, starting transfers between devices: 3.37 us -> 4.39 us  [local(): behind = lax.ppermute(behind, 'shard', back)]
where the time goes in v9:
time: 78.9 us; the launch traced here: 78.4 us
  starting transfers between devices  37.5 us (48%)
  waiting for transfers between devices  15.5 us (20%)
  blocking collectives  12.6 us (16%)
  Pallas kernels  11.9 us (15%)
  between operations  0.83 us (1%)
    all_to_all x1, blocking collectives, local(): parts = lax.all_to_all(ordered, 'shard', 0, 0, axis_index_groups=groups)  12.6 us
    all_to_all x1, starting transfers between devices, local(): received = lax.all_to_all(send, 'replica', 0, 0)  11.8 us
    all_to_all x1, starting transfers between devices, local(): lax.all_to_all(renewed, 'shard', 0, 0).reshape(shards * rows, piece)  9.67 us
    all_to_all x1, waiting for transfers between devices, local(): lax.all_to_all(renewed, 'shard', 0, 0).reshape(shards * rows, piece)  7.14 us
    ppermute x1, starting transfers between devices, local(): far1 = lax.ppermute(far1, 'shard', back)  4.7 us
    ppermute x1, starting transfers between devices, local(): behind = lax.ppermute(behind, 'shard', back)  4.39 us
    pallas_call x6, Pallas kernels, call(): pl.pallas_call(kernel, out_shape=out, in_specs=[pl.BlockSpec(memory_space...  4.01 us
    ppermute x1, waiting for transfers between devices, local(): far0 = lax.ppermute(far0, 'shard', on)  2.97 us
  transfers between devices with their start and end apart: 7, of which 5 were waited for; matrix products, arithmetic and copies ran while one was open for 0% of the time, Pallas kernels for 10%

profile of v9, /device:TPU:1, one launch (start us, length us, event | category | flops | bytes accessed | tf_op | source)
XLA Modules:
  0.0 78.4 jit_solution(5297685102900797520)
XLA Ops:
  0.6 0.0 copy-start.3
  0.7 2.6 %coefficients.1 = bf16[16,16,384]{2,1,0:T(8,128)(2,1)} custom-call(f32[1,16,6144]{2,1,0:T(8,128)} %momentum.4, bf16[1,16,6144]{2,1,0:T(8,128)(2,1)} %gradient.3, s32[16,4,96]{2,1,0:T(4,128)} %bitcast.6, f32[128,128]{1,0:T(8,128)} %constant.2.clone.table), custom_call_target="tpu_custom_call" | custom-call | flops 100000000 | bytes 1000000 | tf_op jit(solution)/shard_map/coefficients/pallas_call | solution.py:228
  3.3 11.8 %all-to-all-start = ((bf16[16,16,384]{2,1,0:T(8,128)(2,1)}), bf16[16,16,384]{2,1,0:T(8,128)(2,1)S(1)}, u32[]{:S(2)}, u32[]{:S(2)}) async-start(bf16[16,16,384]{2,1,0:T(8,128)(2,1)} %coefficients.1), calls=%async_computation | async-start | bytes 393216 | tf_op jit(solution)/shard_map/exchange/all_to_all | solution.py:250
  15.1 2.2 %cut.1 = (bf16[3,128,768]{2,1,0:T(8,128)(2,1)}, bf16[3,128,768]{2,1,0:T(8,128)(2,1)}) custom-call(bf16[128,6144]{1,0:T(8,128)(2,1)} %tokens.1), custom_call_target="tpu_custom_call" | custom-call | bytes 3145728 | tf_op jit(solution)/shard_map/cut/pallas_call | solution.py:239
  17.4 4.4 %collective-permute-start = (bf16[3,128,768]{2,1,0:T(8,128)(2,1)}, bf16[3,128,768]{2,1,0:T(8,128)(2,1)S(1)}, u32[]{:S(2)}, u32[]{:S(2)}) collective-permute-start(bf16[3,128,768]{2,1,0:T(8,128)(2,1)} %get-tuple-element.20), channel_id=1, source_target_pairs={{0,48},{16,0},{32,16},{48,32},{64,112},{80,64},{96,80},{112,96},{1... | collective-permute-start | bytes 1769480 | tf_op jit(solution)/shard_map/tokens_x/ppermute | solution.py:265
  21.8 1.9 %collective-permute-start.1 = (bf16[3,128,768]{2,1,0:T(8,128)(2,1)}, bf16[3,128,768]{2,1,0:T(8,128)(2,1)S(1)}, u32[]{:S(2)}, u32[]{:S(2)}) collective-permute-start(bf16[3,128,768]{2,1,0:T(8,128)(2,1)} %get-tuple-element.22), channel_id=1, source_target_pairs={{0,16},{16,32},{32,48},{48,0},{64,80},{80,96},{96,112},{112,64},{1... | collective-permute-start | bytes 1769480 | tf_op jit(solution)/shard_map/tokens_x/ppermute | solution.py:264
  23.7 1.7 %all-to-all-done.received = bf16[16,16,384]{2,1,0:T(8,128)(2,1)S(1)} async-done(((bf16[16,16,384]{2,1,0:T(8,128)(2,1)}), bf16[16,16,384]{2,1,0:T(8,128)(2,1)S(1)}, u32[]{:S(2)}, u32[]{:S(2)}) %all-to-all-start) | async-done | bytes 196640 | tf_op jit(solution)/shard_map/exchange/all_to_all | solution.py:250
  25.5 2.1 %renew.1 = bf16[32,16,768]{2,1,0:T(8,128)(2,1)} custom-call(bf16[16,16,384]{2,1,0:T(8,128)(2,1)S(1)} %all-to-all-done.received, bf16[16,6144]{1,0:T(8,128)(2,1)S(1)} %copy-done.5, f32[128,128]{1,0:T(8,128)S(1)} %copy-done.3), custom_call_target="tpu_custom_call" | custom-call | flops 10000000000 | bytes 1245184 | tf_op jit(solution)/shard_map/renew/pallas_call | solution.py:199
  27.5 9.7 %all-to-all-start.1 = ((bf16[32,16,768]{2,1,0:T(8,128)(2,1)}), bf16[32,16,768]{2,1,0:T(8,128)(2,1)S(1)}, u32[]{:S(2)}, u32[]{:S(2)}) async-start(bf16[32,16,768]{2,1,0:T(8,128)(2,1)} %renew.1), calls=%async_computation.1 | async-start | bytes 1572864 | tf_op jit(solution)/shard_map/window/all_to_all | solution.py:293
  37.2 2.4 %collective-permute-done.1.arrived.refs_1_ = bf16[3,128,768]{2,1,0:T(8,128)(2,1)S(1)} collective-permute-done((bf16[3,128,768]{2,1,0:T(8,128)(2,1)}, bf16[3,128,768]{2,1,0:T(8,128)(2,1)S(1)}, u32[]{:S(2)}, u32[]{:S(2)}) %collective-permute-start.1) | collective-permute-done | bytes 589856 | tf_op jit(solution)/shard_map/tokens_x/ppermute | solution.py:264
  39.6 0.0 copy-start.2
  39.6 0.0 copy-start.4
  39.6 2.1 %collective-permute-start.2 = (bf16[1,128,768]{2,1,0:T(8,128)(2,1)S(1)}, bf16[1,128,768]{2,1,0:T(8,128)(2,1)S(1)}, u32[]{:S(2)}, u32[]{:S(2)}) collective-permute-start(bf16[1,128,768]{2,1,0:T(8,128)(2,1)S(1)} %tokens_x.4), channel_id=1, source_target_pairs={{0,16},{16,32},{32,48},{48,0},{64,80},{80,96},{96,112},{112,64},{1... | collective-permute-start | bytes 589832 | tf_op jit(solution)/shard_map/tokens_x/ppermute | solution.py:269
  41.7 4.7 %collective-permute-start.3 = (bf16[1,128,768]{2,1,0:T(8,128)(2,1)S(1)}, bf16[1,128,768]{2,1,0:T(8,128)(2,1)S(1)}, u32[]{:S(2)}, u32[]{:S(2)}) collective-permute-start(bf16[1,128,768]{2,1,0:T(8,128)(2,1)S(1)} %tokens_x.3), channel_id=1, source_target_pairs={{0,48},{16,0},{32,16},{48,32},{64,112},{80,64},{96,80},{112,96},{1... | collective-permute-start | bytes 589832 | tf_op jit(solution)/shard_map/tokens_x/ppermute | solution.py:270
  46.5 2.9 %momentum.3 = f32[1,16,6144]{2,1,0:T(8,128)} custom-call(f32[1,16,6144]{2,1,0:T(8,128)S(1)} %copy-done.1, bf16[1,16,6144]{2,1,0:T(8,128)(2,1)S(1)} %copy-done.2, s32[16,4,96]{2,1,0:T(4,128)S(1)} %bitcast.7, f32[128,128]{1,0:T(8,128)S(1)} %copy-done.3), custom_call_target="tpu_custom_call" | custom-call | flops 1000000000 | bytes 1000000 | tf_op jit(solution)/shard_map/momentum/pallas_call | solution.py:283
  49.4 3.0 %collective-permute-done.2.refs_2_ = bf16[1,128,768]{2,1,0:T(8,128)(2,1)S(1)} collective-permute-done((bf16[1,128,768]{2,1,0:T(8,128)(2,1)S(1)}, bf16[1,128,768]{2,1,0:T(8,128)(2,1)S(1)}, u32[]{:S(2)}, u32[]{:S(2)}) %collective-permute-start.2) | collective-permute-done | bytes 196640 | tf_op jit(solution)/shard_map/tokens_x/ppermute | solution.py:269
  52.4 0.1 tokens_x.5.refs_0_
  52.5 7.1 %all-to-all-done.1 = bf16[32,16,768]{2,1,0:T(8,128)(2,1)S(1)} async-done(((bf16[32,16,768]{2,1,0:T(8,128)(2,1)}), bf16[32,16,768]{2,1,0:T(8,128)(2,1)S(1)}, u32[]{:S(2)}, u32[]{:S(2)}) %all-to-all-start.1) | async-done | bytes 786464 | tf_op jit(solution)/shard_map/window/all_to_all | solution.py:293
  59.6 3.0 %collective-permute-start.4 = (bf16[512,768]{1,0:T(8,128)(2,1)S(1)}, bf16[512,768]{1,0:T(8,128)(2,1)S(1)}, u32[]{:S(2)}, u32[]{:S(2)}) collective-permute-start(bf16[512,768]{1,0:T(8,128)(2,1)S(1)} %bitcast.4), channel_id=1, source_target_pairs={{0,1},{1,0},{2,3},{3,2},{4,5},{5,4},{6,7},{7,6},{8,9},{9,8},{10,11... | collective-permute-start | bytes 2359304 | tf_op jit(solution)/shard_map/window_core/ppermute | solution.py:296
  62.6 0.6 product.2
  63.2 1.3 %collective-permute-done.4.window = bf16[512,768]{1,0:T(8,128)(2,1)S(1)} collective-permute-done((bf16[512,768]{1,0:T(8,128)(2,1)S(1)}, bf16[512,768]{1,0:T(8,128)(2,1)S(1)}, u32[]{:S(2)}, u32[]{:S(2)}) %collective-permute-start.4) | collective-permute-done | bytes 786464 | tf_op jit(solution)/shard_map/window_core/ppermute | solution.py:296
  64.5 0.6 product.3
  65.1 12.6 %all_to_all.15.parts = bf16[4,128,512]{2,1,0:T(8,128)(2,1)S(1)} all-to-all(bf16[4,128,512]{2,1,0:T(8,128)(2,1)S(1)} %product.3), channel_id=1, replica_groups={{0,16,32,48},{64,80,96,112},{128,144,160,176},{192,208,224,240},{256,27..., dimensions={0} | all-to-all | bytes 1048576 | tf_op jit(solution)/shard_map/sum_x/all_to_all | solution.py:321
  77.7 0.7 sum_x.1
  (13 shorter events, 0.1 us)
Async XLA Ops:
  0.6 24.8 %copy-start.3 = (f32[128,128]{1,0:T(8,128)S(1)}, f32[128,128]{1,0:T(8,128)}, u32[]{:S(2)}) copy-start(f32[128,128]{1,0:T(8,128)} %constant.2.clone.table) | copy-start | bytes 196612
  0.6 24.8 %copy-start.5 = (bf16[16,6144]{1,0:T(8,128)(2,1)S(1)}, bf16[16,6144]{1,0:T(8,128)(2,1)}, u32[]{:S(2)}) copy-start(bf16[16,6144]{1,0:T(8,128)(2,1)} %weight.1) | copy-start | bytes 589828
  3.3 22.2 %all-to-all-start = ((bf16[16,16,384]{2,1,0:T(8,128)(2,1)}), bf16[16,16,384]{2,1,0:T(8,128)(2,1)S(1)}, u32[]{:S(2)}, u32[]{:S(2)}) async-start(bf16[16,16,384]{2,1,0:T(8,128)(2,1)} %coefficients.1), calls=%async_computation | async-start | bytes 393216 | tf_op jit(solution)/shard_map/exchange/all_to_all | solution.py:250
  17.4 24.3 %collective-permute-start = (bf16[3,128,768]{2,1,0:T(8,128)(2,1)}, bf16[3,128,768]{2,1,0:T(8,128)(2,1)S(1)}, u32[]{:S(2)}, u32[]{:S(2)}) collective-permute-start(bf16[3,128,768]{2,1,0:T(8,128)(2,1)} %get-tuple-element.20), channel_id=1, source_target_pairs={{0,48},{16,0},{32,16},{48,32},{64,112},{80,64},{96,80},{112,96},{1... | collective-permute-start | bytes 1769480 | tf_op jit(solution)/shard_map/tokens_x/ppermute | solution.py:265
  21.8 17.8 %collective-permute-start.1 = (bf16[3,128,768]{2,1,0:T(8,128)(2,1)}, bf16[3,128,768]{2,1,0:T(8,128)(2,1)S(1)}, u32[]{:S(2)}, u32[]{:S(2)}) collective-permute-start(bf16[3,128,768]{2,1,0:T(8,128)(2,1)} %get-tuple-element.22), channel_id=1, source_target_pairs={{0,16},{16,32},{32,48},{48,0},{64,80},{80,96},{96,112},{112,64},{1... | collective-permute-start | bytes 1769480 | tf_op jit(solution)/shard_map/tokens_x/ppermute | solution.py:264
  27.5 32.1 %all-to-all-start.1 = ((bf16[32,16,768]{2,1,0:T(8,128)(2,1)}), bf16[32,16,768]{2,1,0:T(8,128)(2,1)S(1)}, u32[]{:S(2)}, u32[]{:S(2)}) async-start(bf16[32,16,768]{2,1,0:T(8,128)(2,1)} %renew.1), calls=%async_computation.1 | async-start | bytes 1572864 | tf_op jit(solution)/shard_map/window/all_to_all | solution.py:293
  39.6 6.9 %copy-start.1 = (f32[1,16,6144]{2,1,0:T(8,128)S(1)}, f32[1,16,6144]{2,1,0:T(8,128)}, u32[]{:S(2)}) copy-start(f32[1,16,6144]{2,1,0:T(8,128)} %momentum.4) | copy-start | bytes 1179652
  39.6 6.9 %copy-start.2 = (bf16[1,16,6144]{2,1,0:T(8,128)(2,1)S(1)}, bf16[1,16,6144]{2,1,0:T(8,128)(2,1)}, u32[]{:S(2)}) copy-start(bf16[1,16,6144]{2,1,0:T(8,128)(2,1)} %gradient.3) | copy-start | bytes 589828
  39.6 6.9 %copy-start.4 = (s32[1,16,96,4]{2,3,1,0:T(4,128)S(1)}, s32[1,16,96,4]{2,3,1,0:T(4,128)}, u32[]{:S(2)}) copy-start(s32[1,16,96,4]{2,3,1,0:T(4,128)} %param.10) | copy-start | bytes 73732
  39.6 12.7 %collective-permute-start.2 = (bf16[1,128,768]{2,1,0:T(8,128)(2,1)S(1)}, bf16[1,128,768]{2,1,0:T(8,128)(2,1)S(1)}, u32[]{:S(2)}, u32[]{:S(2)}) collective-permute-start(bf16[1,128,768]{2,1,0:T(8,128)(2,1)S(1)} %tokens_x.4), channel_id=1, source_target_pairs={{0,16},{16,32},{32,48},{48,0},{64,80},{80,96},{96,112},{112,64},{1... | collective-permute-start | bytes 589832 | tf_op jit(solution)/shard_map/tokens_x/ppermute | solution.py:269
  41.7 10.6 %copy-start = (bf16[128,6144]{1,0:T(8,128)(2,1)S(1)}, bf16[128,6144]{1,0:T(8,128)(2,1)}, u32[]{:S(2)}) copy-start(bf16[128,6144]{1,0:T(8,128)(2,1)} %tokens.1) | copy-start | bytes 4718596
  41.7 10.7 %collective-permute-start.3 = (bf16[1,128,768]{2,1,0:T(8,128)(2,1)S(1)}, bf16[1,128,768]{2,1,0:T(8,128)(2,1)S(1)}, u32[]{:S(2)}, u32[]{:S(2)}) collective-permute-start(bf16[1,128,768]{2,1,0:T(8,128)(2,1)S(1)} %tokens_x.3), channel_id=1, source_target_pairs={{0,48},{16,0},{32,16},{48,32},{64,112},{80,64},{96,80},{112,96},{1... | collective-permute-start | bytes 589832 | tf_op jit(solution)/shard_map/tokens_x/ppermute | solution.py:270
  59.6 4.9 %collective-permute-start.4 = (bf16[512,768]{1,0:T(8,128)(2,1)S(1)}, bf16[512,768]{1,0:T(8,128)(2,1)S(1)}, u32[]{:S(2)}, u32[]{:S(2)}) collective-permute-start(bf16[512,768]{1,0:T(8,128)(2,1)S(1)} %bitcast.4), channel_id=1, source_target_pairs={{0,1},{1,0},{2,3},{3,2},{4,5},{5,4},{6,7},{7,6},{8,9},{9,8},{10,11... | collective-permute-start | bytes 2359304 | tf_op jit(solution)/shard_map/window_core/ppermute | solution.py:296
